TPU v7x, 32 devices: a whole 2x2x4 slice. The times are simulated.
32 devices in a mesh: parts: 1, row: 16 (over z, y, core), col: 2 (over x).
Axes of the slice: x: 2, y: 2, z: 4, core: 2. Of those that a mesh axis runs over, the one named last changes fastest.
Arguments:
- pair_act: bfloat16 [256, 256, 128], P(('parts', 'row'), 'col'), may hold values from -6 to 6
- in_weights: bfloat16 [2, 128, 640], replicated, may hold values from -0.5 to 0.5
- out_weights: bfloat16 [2, 128, 128], replicated, may hold values from -0.5 to 0.5
- chain_lengths: int32 [8], P('parts'), may hold values from 1 to 64, 256 in all
Outputs:
- pair_out: bfloat16 [256, 256, 128], P(('parts', 'row'), 'col')
Inputs may be any that keep to these rules, and one draw needn't show every extreme that they name: `chain_lengths`: the first 7 entries are chain lengths, the last counts padding residues at the end of the complex; all entries sum to 256, and the largest entry equals 64.
All inputs are finite; a program needn't handle non-finite values.
Results may differ from a plain program's by a relative error of at most 0.0095.
Values may be sent and summed in bfloat16 or wider, within the bound.
No kernel may reach another device: no remote copies, remote signals or barrier semaphores. Data moves between devices by JAX's collectives and lax.ppermute only.
A program may use at most 64 MiB of HBM per device.

v0:
```python
import jax
import jax.numpy as jnp
from jax import lax
from jax.sharding import PartitionSpec as P

epsilon = 1e-05


def layer_norm(values, along_axis):
    mean_vals = jnp.mean(values, axis=along_axis, keepdims=True)
    centred = values - mean_vals
    variance = jnp.mean(centred * centred, axis=along_axis, keepdims=True)
    return centred * lax.rsqrt(variance + epsilon)


def project(pair_act, weights, pair_mask):
    width = pair_act.shape[2]
    normed = layer_norm(pair_act.astype(jnp.float32), 2).astype(jnp.bfloat16)
    projected = jnp.einsum(
        "rjd,de->erj", normed, weights[:, 0 : 4 * width], preferred_element_type=jnp.float32
    )
    left_vals = (
        jax.nn.sigmoid(projected[0:width]) * projected[width : 2 * width] * pair_mask
    ).astype(jnp.bfloat16)
    right_vals = (
        jax.nn.sigmoid(projected[2 * width : 3 * width])
        * projected[3 * width : 4 * width]
        * pair_mask
    ).astype(jnp.bfloat16)
    gate_vals = jax.nn.sigmoid(
        jnp.einsum(
            "rjd,de->rje",
            normed,
            weights[:, 4 * width : 5 * width],
            preferred_element_type=jnp.float32,
        )
    ).astype(jnp.bfloat16)
    return (left_vals, right_vals, gate_vals)


def to_channels(left_vals, right_vals):
    return (
        lax.all_to_all(left_vals, "row", split_axis=0, concat_axis=1, tiled=True),
        lax.all_to_all(right_vals, "row", split_axis=0, concat_axis=1, tiled=True),
    )


def finish(pair_act, triangle, gate_vals, weights_out):
    tri_normed = layer_norm(triangle.astype(jnp.float32), 0).astype(jnp.bfloat16)
    delta_vals = jnp.einsum(
        "crj,cd->rjd", tri_normed, weights_out, preferred_element_type=jnp.float32
    )
    delta_vals = delta_vals * gate_vals.astype(jnp.float32)
    return (pair_act.astype(jnp.float32) + delta_vals).astype(jnp.bfloat16)


def per_device(pair_act, in_weights, out_weights, chain_lengths):
    row_tile = pair_act.shape[0]
    col_tile = pair_act.shape[1]
    total_rows = row_tile * lax.axis_size("row")
    count_valid = total_rows - chain_lengths[chain_lengths.shape[0] - 1]
    row_first = lax.axis_index("row") * row_tile
    col_first = lax.axis_index("col") * col_tile
    row_valid = (row_first + jnp.arange(row_tile, dtype=jnp.int32) < count_valid).astype(
        jnp.float32
    )
    col_valid = (col_first + jnp.arange(col_tile, dtype=jnp.int32) < count_valid).astype(
        jnp.float32
    )
    pair_mask = row_valid[:, None] * col_valid[None, :]
    left_vals, right_vals, gate_vals = project(pair_act, in_weights[0], pair_mask)
    left_chan, right_chan = to_channels(left_vals, right_vals)
    left_rows = lax.all_to_all(left_chan, "col", split_axis=1, concat_axis=2, tiled=True)
    summed = jnp.einsum(
        "cik,cjk->cij",
        left_rows,
        lax.all_gather(right_chan, "col", axis=2, tiled=True),
        preferred_element_type=jnp.float32,
    )
    triangle = lax.all_to_all(
        lax.all_to_all(summed.astype(jnp.bfloat16), "col", split_axis=2, concat_axis=1, tiled=True),
        "row",
        split_axis=1,
        concat_axis=0,
        tiled=True,
    )
    first_pass = finish(pair_act, triangle, gate_vals, out_weights[0])
    left_vals, right_vals, gate_vals = project(first_pass, in_weights[1], pair_mask)
    left_chan, right_chan = to_channels(left_vals, right_vals)
    summed_in = jnp.einsum(
        "cki,ckj->cij",
        lax.all_gather(left_chan, "col", axis=2, tiled=True),
        right_chan,
        preferred_element_type=jnp.float32,
    ).astype(jnp.bfloat16)
    triangle_in = lax.all_to_all(summed_in, "row", split_axis=1, concat_axis=0, tiled=True)
    return finish(first_pass, triangle_in, gate_vals, out_weights[1])


def solution(mesh):
    in_specs = (P(("parts", "row"), "col", None), P(), P(), P("parts"))
    out_specs = P(("parts", "row"), "col", None)
    return jax.shard_map(
        per_device, mesh=mesh, in_specs=in_specs, out_specs=out_specs, check_vma=False
    )
```

profile of v0, /device:TPU:0, one launch (start us, length us, event | category | flops | bytes accessed | tf_op | source)
XLA Modules:
  0.0 178.8 jit_solution(2690783328120721286)
XLA Ops:
  6.5 1.3 copy.96
  8.1 1.0 slice_bitcast_fusion
  9.2 1.2 slice.55
  12.5 1.2 copy.103
  13.7 7.4 %all-to-all-start.2 = ((bf16[128,16,128]{2,1,0:T(8,128)(2,1)}), bf16[128,16,128]{2,1,0:T(8,128)(2,1)S(1)}, u32[]{:S(2)}, u32[]{:S(2)}) async-start(bf16[128,16,128]{2,1,0:T(8,128)(2,1)} %copy.103), calls=%async_computation.2 | async-start | bytes 1048576 | tf_op jit(solution)/shard_map/all_to_all | solution.py:44
  21.1 1.2 copy.98
  22.3 13.3 %all-to-all-done.2 = bf16[128,16,128]{2,1,0:T(8,128)(2,1)S(1)} async-done(((bf16[128,16,128]{2,1,0:T(8,128)(2,1)}), bf16[128,16,128]{2,1,0:T(8,128)(2,1)S(1)}, u32[]{:S(2)}, u32[]{:S(2)}) %all-to-all-start.2) | async-done | bytes 524320 | tf_op jit(solution)/shard_map/all_to_all | solution.py:44
  35.5 4.1 %all-to-all-start = ((bf16[128,16,128]{2,1,0:T(8,128)(2,1)}), bf16[128,16,128]{2,1,0:T(8,128)(2,1)S(1)}, u32[]{:S(2)}, u32[]{:S(2)}) async-start(bf16[128,16,128]{2,1,0:T(8,128)(2,1)} %copy.98), calls=%async_computation | async-start | bytes 1048576 | tf_op jit(solution)/shard_map/all_to_all | solution.py:43
  40.6 13.5 %all-to-all-done = bf16[128,16,128]{2,1,0:T(8,128)(2,1)S(1)} async-done(((bf16[128,16,128]{2,1,0:T(8,128)(2,1)}), bf16[128,16,128]{2,1,0:T(8,128)(2,1)S(1)}, u32[]{:S(2)}, u32[]{:S(2)}) %all-to-all-start) | async-done | bytes 524320 | tf_op jit(solution)/shard_map/all_to_all | solution.py:43
  54.5 15.5 %all_to_all.126 = bf16[8,256,128]{2,0,1:T(8,128)(2,1)S(1)} all-to-all(bf16[8,256,128]{2,0,1:T(8,128)(2,1)S(1)} %copy.100), channel_id=1, replica_groups=mesh['parts'=1,'row'=16,'col'=2] {'col'}, dimensions={1} | all-to-all | bytes 1048576 | tf_op jit(solution)/shard_map/all_to_all | solution.py:73
  71.0 1.7 convolution_convert_fusion.1
  73.0 10.6 %all_to_all.127 = bf16[8,128,256]{1,0,2:T(8,128)(2,1)S(1)} all-to-all(bf16[8,128,256]{1,0,2:T(8,128)(2,1)S(1)} %copy.105), channel_id=1, replica_groups=mesh['parts'=1,'row'=16,'col'=2] {'col'}, dimensions={2} | all-to-all | bytes 1048576 | tf_op jit(solution)/shard_map/all_to_all | solution.py:81
  83.6 1.2 copy.138
  84.8 5.5 %all-to-all-start.4 = ((bf16[8,256,128]{2,0,1:T(8,128)(2,1)}), bf16[8,256,128]{2,0,1:T(8,128)(2,1)S(1)}, u32[]{:S(2)}, u32[]{:S(2)}) async-start(bf16[8,256,128]{2,0,1:T(8,128)(2,1)} %bitcast.17), calls=%async_computation.4 | async-start | bytes 1048576 | tf_op jit(solution)/shard_map/all_to_all | solution.py:80
  90.8 13.9 %all-to-all-done.4 = bf16[8,256,128]{2,0,1:T(8,128)(2,1)S(1)} async-done(((bf16[8,256,128]{2,0,1:T(8,128)(2,1)}), bf16[8,256,128]{2,0,1:T(8,128)(2,1)S(1)}, u32[]{:S(2)}, u32[]{:S(2)}) %all-to-all-start.4) | async-done | bytes 524320 | tf_op jit(solution)/shard_map/all_to_all | solution.py:80
  107.7 18.4 %all_to_all.128 = bf16[128,16,128]{2,1,0:T(8,128)(2,1)S(1)} all-to-all(bf16[128,16,128]{2,1,0:T(8,128)(2,1)S(1)} %copy.116), channel_id=1, replica_groups=mesh['parts'=1,'row'=16,'col'=2] {'row'}, dimensions={0} | all-to-all | bytes 1048576 | tf_op jit(solution)/shard_map/all_to_all | solution.py:43
  126.1 1.0 copy.118
  127.6 18.4 %all_to_all.129 = bf16[128,16,128]{2,1,0:T(8,128)(2,1)S(1)} all-to-all(bf16[128,16,128]{2,1,0:T(8,128)(2,1)S(1)} %copy.119), channel_id=1, replica_groups=mesh['parts'=1,'row'=16,'col'=2] {'row'}, dimensions={0} | all-to-all | bytes 1048576 | tf_op jit(solution)/shard_map/all_to_all | solution.py:44
  146.0 1.1 all-gather.5.cloned.1.call-done
  147.1 1.6 convolution_convert_fusion
  148.7 1.1 copy.121
  149.9 5.6 %all-to-all-start.7 = ((bf16[8,256,128]{2,0,1:T(8,128)(2,1)}), bf16[8,256,128]{2,0,1:T(8,128)(2,1)S(1)}, u32[]{:S(2)}, u32[]{:S(2)}) async-start(bf16[8,256,128]{2,0,1:T(8,128)(2,1)} %copy.121), calls=%async_computation.7 | async-start | bytes 1048576 | tf_op jit(solution)/shard_map/all_to_all | solution.py:96
  156.0 14.0 %all-to-all-done.7 = bf16[8,256,128]{2,0,1:T(8,128)(2,1)S(1)} async-done(((bf16[8,256,128]{2,0,1:T(8,128)(2,1)}), bf16[8,256,128]{2,0,1:T(8,128)(2,1)S(1)}, u32[]{:S(2)}, u32[]{:S(2)}) %all-to-all-start.7) | async-done | bytes 524320 | tf_op jit(solution)/shard_map/all_to_all | solution.py:96
  171.0 1.0 copy.128
  (49 shorter events, 9.5 us)
Async XLA Ops:
  13.7 21.9 %all-to-all-start.2 = ((bf16[128,16,128]{2,1,0:T(8,128)(2,1)}), bf16[128,16,128]{2,1,0:T(8,128)(2,1)S(1)}, u32[]{:S(2)}, u32[]{:S(2)}) async-start(bf16[128,16,128]{2,1,0:T(8,128)(2,1)} %copy.103), calls=%async_computation.2 | async-start | bytes 1048576 | tf_op jit(solution)/shard_map/all_to_all | solution.py:44
  35.5 18.6 %all-to-all-start = ((bf16[128,16,128]{2,1,0:T(8,128)(2,1)}), bf16[128,16,128]{2,1,0:T(8,128)(2,1)S(1)}, u32[]{:S(2)}, u32[]{:S(2)}) async-start(bf16[128,16,128]{2,1,0:T(8,128)(2,1)} %copy.98), calls=%async_computation | async-start | bytes 1048576 | tf_op jit(solution)/shard_map/all_to_all | solution.py:43
  39.6 31.3 %all-gather.3.cloned.1.call-start = ((), (), s32[]{:S(2)}) async-start(), calls=%async_computation.8 | async-start | bytes 1572864 | tf_op jit(solution)/shard_map/all_gather | solution.py:77
  84.8 20.0 %all-to-all-start.4 = ((bf16[8,256,128]{2,0,1:T(8,128)(2,1)}), bf16[8,256,128]{2,0,1:T(8,128)(2,1)S(1)}, u32[]{:S(2)}, u32[]{:S(2)}) async-start(bf16[8,256,128]{2,0,1:T(8,128)(2,1)} %bitcast.17), calls=%async_computation.4 | async-start | bytes 1048576 | tf_op jit(solution)/shard_map/all_to_all | solution.py:80
  90.3 15.1 %copy-start = (bf16[2,128,128]{2,1,0:T(8,128)(2,1)S(1)}, bf16[2,128,128]{2,1,0:T(8,128)(2,1)}, u32[]{:S(2)}) copy-start(bf16[2,128,128]{2,1,0:T(8,128)(2,1)} %param.6) | copy-start | bytes 196612
  90.3 56.8 %all-gather.5.cloned.1.call-start = ((), (), s32[]{:S(2)}) async-start(), calls=%async_computation.9 | async-start | bytes 1572864 | tf_op jit(solution)/shard_map/all_gather | solution.py:92
  149.9 20.1 %all-to-all-start.7 = ((bf16[8,256,128]{2,0,1:T(8,128)(2,1)}), bf16[8,256,128]{2,0,1:T(8,128)(2,1)S(1)}, u32[]{:S(2)}, u32[]{:S(2)}) async-start(bf16[8,256,128]{2,0,1:T(8,128)(2,1)} %copy.121), calls=%async_computation.7 | async-start | bytes 1048576 | tf_op jit(solution)/shard_map/all_to_all | solution.py:96
Sparse Core Ops, SparseCore 0:
  42.0 27.1 all-gather.2
  127.3 19.7 all-gather.4
where the time goes:
time: 180 us; the launch traced here: 179 us
  blocking collectives  62.9 us (35%)
  waiting for transfers between devices  55.8 us (31%)
  starting transfers between devices  22.7 us (13%)
  between operations  14.4 us (8%)
  local copies, waits for them, and re-layouts  13.9 us (8%)
  matrix products  6.5 us (4%)
  other arithmetic  2.65 us (1%)
    all_to_all x1, blocking collectives, to_channels(): lax.all_to_all(left_vals, 'row', split_axis=0, concat_axis=1, tiled=True)  18.4 us
    all_to_all x1, blocking collectives, to_channels(): lax.all_to_all(right_vals, 'row', split_axis=0, concat_axis=1, tiled=True)  18.4 us
    all_to_all x1, blocking collectives, per_device(): lax.all_to_all(left_chan, 'col', split_axis=1, concat_axis=2, tiled=True)  15.5 us
    all_to_all x1, waiting for transfers between devices, per_device(): lax.all_to_all(summed_in, 'row', split_axis=1, concat_axis=0, tiled=True)  14 us
    all_to_all x1, waiting for transfers between devices, per_device(): lax.all_to_all(lax.all_to_all(summed.astype(jnp.bfloat16), 'col', split_a...  13.9 us
    all_to_all x1, waiting for transfers between devices, to_channels(): lax.all_to_all(left_vals, 'row', split_axis=0, concat_axis=1, tiled=True)  13.5 us
    all_to_all x1, waiting for transfers between devices, to_channels(): lax.all_to_all(right_vals, 'row', split_axis=0, concat_axis=1, tiled=True)  13.3 us
    all_to_all x1, blocking collectives, per_device(): lax.all_to_all(summed.astype(jnp.bfloat16), 'col', split_axis=2, concat_a...  10.6 us
  transfers between devices with their start and end apart: 6, of which 5 were waited for; matrix products, arithmetic and copies ran while one was open for 2% of the time, Pallas kernels for 0%

commit v1 on v0

v1 whole, which is shorter than its diff:
```python
import functools

import jax
import jax.numpy as jnp
from jax import lax
from jax.experimental import pallas as pl
from jax.experimental.pallas import tpu as pltpu
from jax.sharding import PartitionSpec as P

epsilon = 1e-05
F32 = jnp.float32
BF16 = jnp.bfloat16
VMEM_LIMIT = 32 * 1024 * 1024


def layer_norm(values, along_axis):
    mean_vals = jnp.mean(values, axis=along_axis, keepdims=True)
    centred = values - mean_vals
    variance = jnp.mean(centred * centred, axis=along_axis, keepdims=True)
    return centred * lax.rsqrt(variance + epsilon)


def sigmoid(values):
    return 0.5 * jnp.tanh(0.5 * values) + 0.5


def dot(lhs, rhs):
    return jnp.dot(lhs, rhs, preferred_element_type=F32)


def mask_of(limits_ref, first, group, cols):
    lane = lax.broadcasted_iota(jnp.int32, (1, cols), 1)
    col_valid = lane < limits_ref[1]
    parts = [
        jnp.where(jnp.logical_and(col_valid, first + g < limits_ref[0]), 1.0, 0.0)
        for g in range(group)
    ]
    return jnp.concatenate(parts, axis=1).astype(F32)


def project_rows(first, group, pair_vals, mask, weights_t, left_scr, right_scr, gate_ref):
    width = pair_vals.shape[0]
    cols = pair_vals.shape[1] // group
    normed = layer_norm(pair_vals, 0).astype(BF16)
    for side, scr in enumerate((left_scr, right_scr)):
        both = dot(weights_t[2 * side * width : (2 * side + 2) * width, :], normed)
        vals = sigmoid(both[0:width]) * both[width : 2 * width] * mask
        for g in range(group):
            scr[(first + g) * width : (first + g + 1) * width, :] = vals[
                :, g * cols : (g + 1) * cols
            ]
    gate = sigmoid(dot(weights_t[4 * width : 5 * width, :], normed)).astype(BF16)
    for g in range(group):
        gate_ref[first + g] = gate[:, g * cols : (g + 1) * cols]


def send_channels(rows, width, left_scr, right_scr, send_ref):
    per = send_ref.shape[2]
    for c in range(width):
        for side, scr in enumerate((left_scr, right_scr)):
            send_ref[c // per, side, c % per] = scr[pl.ds(c, rows, stride=width), :].astype(BF16)


def first_kernel(limits_ref, pair_ref, weights_ref, send_ref, gate_ref, pair_t_ref, left_scr, right_scr, wt_scr):
    rows, cols, width = pair_ref.shape
    group = 2
    wt_scr[...] = weights_ref[0].astype(F32).T.astype(BF16)
    for first in range(0, rows, group):
        blocks = [pair_ref[first + g].astype(F32).T for g in range(group)]
        for g in range(group):
            pair_t_ref[first + g] = blocks[g].astype(BF16)
        project_rows(
            first, group, jnp.concatenate(blocks, axis=1), mask_of(limits_ref, first, group, cols),
            wt_scr, left_scr, right_scr, gate_ref,
        )
    send_channels(rows, width, left_scr, right_scr, send_ref)


def finish_rows(first, group, tri_scr, rows, wo_t, gate_ref, pair_t_ref):
    width = pair_t_ref.shape[1]
    tri = jnp.concatenate(
        [tri_scr[pl.ds(first + g, width, stride=rows), :] for g in range(group)], axis=1
    )
    tri_normed = layer_norm(tri, 0).astype(BF16)
    delta = dot(wo_t, tri_normed)
    gate = jnp.concatenate([gate_ref[first + g] for g in range(group)], axis=1)
    pair = jnp.concatenate([pair_t_ref[first + g] for g in range(group)], axis=1)
    return (pair.astype(F32) + delta * gate.astype(F32)).astype(BF16)


def middle_kernel(
    limits_ref, tri_ref, gate_in_ref, pair_t_in_ref, wo_ref, weights_ref,
    send_ref, gate_ref, pair_t_ref, left_scr, right_scr, wt_scr, tri_scr,
):
    width, rows, cols = tri_ref.shape
    group = 2
    wt_scr[...] = weights_ref[1].astype(F32).T.astype(BF16)
    wo_t = wo_ref[0].astype(F32).T.astype(BF16)
    tri_scr[...] = tri_ref[...].astype(F32).reshape(width * rows, cols)
    for first in range(0, rows, group):
        passed = finish_rows(first, group, tri_scr, rows, wo_t, gate_in_ref, pair_t_in_ref)
        for g in range(group):
            pair_t_ref[first + g] = passed[:, g * cols : (g + 1) * cols]
        project_rows(
            first, group, passed.astype(F32), mask_of(limits_ref, first, group, cols),
            wt_scr, left_scr, right_scr, gate_ref,
        )
    send_channels(rows, width, left_scr, right_scr, send_ref)


def last_kernel(tri_ref, gate_ref, pair_t_ref, wo_ref, out_ref, tri_scr):
    width, rows, cols = tri_ref.shape
    group = 2
    wo_t = wo_ref[1].astype(F32).T.astype(BF16)
    tri_scr[...] = tri_ref[...].astype(F32).reshape(width * rows, cols)
    for first in range(0, rows, group):
        passed = finish_rows(first, group, tri_scr, rows, wo_t, gate_ref, pair_t_ref)
        for g in range(group):
            out_ref[first + g] = passed[:, g * cols : (g + 1) * cols].astype(F32).T.astype(BF16)


def triangle_kernel(incoming, recv_ref, out_ref):
    n_row, n_col, _, per, rows, cols = recv_ref.shape
    for c in range(per):
        left, right = (
            jnp.concatenate(
                [recv_ref[:, x, side, c].reshape(n_row * rows, cols) for x in range(n_col)], axis=1
            )
            for side in (0, 1)
        )
        dims = (((0,), (0,)), ((), ())) if incoming else (((1,), (1,)), ((), ()))
        tri = lax.dot_general(left, right, dims, preferred_element_type=F32).astype(BF16)
        for x in range(n_col):
            out_ref[:, x, c] = tri[:, x * cols : (x + 1) * cols].reshape(n_row, rows, cols)


def call(kernel, name, out_shape, scratch, in_specs, flops, *args):
    return pl.pallas_call(
        kernel,
        name=name,
        out_shape=out_shape,
        in_specs=in_specs,
        out_specs=jax.tree.map(lambda _: pl.BlockSpec(memory_space=pltpu.VMEM), out_shape),
        scratch_shapes=scratch,
        compiler_params=pltpu.CompilerParams(vmem_limit_bytes=VMEM_LIMIT),
        cost_estimate=pl.CostEstimate(flops=flops, bytes_accessed=2 << 20, transcendentals=0),
    )(*args)


VM = pl.BlockSpec(memory_space=pltpu.VMEM)
SM = pl.BlockSpec(memory_space=pltpu.SMEM)


def split_channels(n_row, n_col, pair_act, in_weights, out_weights, chain_lengths):
    rows, cols, width = pair_act.shape
    group = n_row * n_col
    per = width // group
    axes = ("row", "col")
    count_valid = rows * n_row - chain_lengths[chain_lengths.shape[0] - 1]
    limits = jnp.stack(
        [count_valid - lax.axis_index("row") * rows, count_valid - lax.axis_index("col") * cols]
    ).astype(jnp.int32)

    send_shape = jax.ShapeDtypeStruct((group, 2, per, rows, cols), BF16)
    block_shape = jax.ShapeDtypeStruct((rows, width, cols), BF16)
    tri_shape = jax.ShapeDtypeStruct((n_row, n_col, per, rows, cols), BF16)
    scr = pltpu.VMEM((rows * width, cols), F32)
    wt_scr = pltpu.VMEM((5 * width, width), BF16)
    flops_in = 2 * rows * cols * width * 5 * width
    flops_out = 2 * rows * cols * width * width
    flops_tri = 2 * per * (n_row * rows) ** 2 * n_col * cols

    def exchange(array):
        return lax.all_to_all(array, axes, split_axis=0, concat_axis=0, tiled=True)

    def triangle(send, incoming):
        recv = exchange(send).reshape((n_row, n_col) + send.shape[1:])
        tri = call(
            functools.partial(triangle_kernel, incoming), "triangle", tri_shape, [], [VM], flops_tri, recv
        )
        return exchange(tri.reshape((group,) + tri.shape[2:])).reshape(width, rows, cols)

    send, gate, pair_t = call(
        first_kernel, "project", (send_shape, block_shape, block_shape), [scr, scr, wt_scr],
        [SM, VM, VM], flops_in, limits, pair_act, in_weights,
    )
    tri = triangle(send, False)
    send, gate, pair_t = call(
        middle_kernel, "finish_project", (send_shape, block_shape, block_shape), [scr, scr, wt_scr, scr],
        [SM, VM, VM, VM, VM, VM], flops_in + flops_out,
        limits, tri, gate, pair_t, out_weights, in_weights,
    )
    tri = triangle(send, True)
    return call(
        last_kernel, "finish", jax.ShapeDtypeStruct(pair_act.shape, BF16), [scr],
        [VM, VM, VM, VM], flops_out, tri, gate, pair_t, out_weights,
    )


def project(pair_act, weights, pair_mask):
    width = pair_act.shape[2]
    normed = layer_norm(pair_act.astype(F32), 2).astype(BF16)
    projected = jnp.einsum("rjd,de->erj", normed, weights[:, 0 : 4 * width], preferred_element_type=F32)
    left_vals = (jax.nn.sigmoid(projected[0:width]) * projected[width : 2 * width] * pair_mask).astype(BF16)
    right_vals = (
        jax.nn.sigmoid(projected[2 * width : 3 * width]) * projected[3 * width : 4 * width] * pair_mask
    ).astype(BF16)
    gate_vals = jax.nn.sigmoid(
        jnp.einsum("rjd,de->rje", normed, weights[:, 4 * width : 5 * width], preferred_element_type=F32)
    ).astype(BF16)
    return (left_vals, right_vals, gate_vals)


def to_channels(left_vals, right_vals):
    return (
        lax.all_to_all(left_vals, "row", split_axis=0, concat_axis=1, tiled=True),
        lax.all_to_all(right_vals, "row", split_axis=0, concat_axis=1, tiled=True),
    )


def finish(pair_act, triangle, gate_vals, weights_out):
    tri_normed = layer_norm(triangle.astype(F32), 0).astype(BF16)
    delta_vals = jnp.einsum("crj,cd->rjd", tri_normed, weights_out, preferred_element_type=F32)
    delta_vals = delta_vals * gate_vals.astype(F32)
    return (pair_act.astype(F32) + delta_vals).astype(BF16)


def split_rows(pair_act, in_weights, out_weights, chain_lengths):
    row_tile = pair_act.shape[0]
    col_tile = pair_act.shape[1]
    total_rows = row_tile * lax.axis_size("row")
    count_valid = total_rows - chain_lengths[chain_lengths.shape[0] - 1]
    row_first = lax.axis_index("row") * row_tile
    col_first = lax.axis_index("col") * col_tile
    row_valid = (row_first + jnp.arange(row_tile, dtype=jnp.int32) < count_valid).astype(F32)
    col_valid = (col_first + jnp.arange(col_tile, dtype=jnp.int32) < count_valid).astype(F32)
    pair_mask = row_valid[:, None] * col_valid[None, :]
    left_vals, right_vals, gate_vals = project(pair_act, in_weights[0], pair_mask)
    left_chan, right_chan = to_channels(left_vals, right_vals)
    left_rows = lax.all_to_all(left_chan, "col", split_axis=1, concat_axis=2, tiled=True)
    summed = jnp.einsum(
        "cik,cjk->cij",
        left_rows,
        lax.all_gather(right_chan, "col", axis=2, tiled=True),
        preferred_element_type=F32,
    )
    triangle = lax.all_to_all(
        lax.all_to_all(summed.astype(BF16), "col", split_axis=2, concat_axis=1, tiled=True),
        "row",
        split_axis=1,
        concat_axis=0,
        tiled=True,
    )
    first_pass = finish(pair_act, triangle, gate_vals, out_weights[0])
    left_vals, right_vals, gate_vals = project(first_pass, in_weights[1], pair_mask)
    left_chan, right_chan = to_channels(left_vals, right_vals)
    summed_in = jnp.einsum(
        "cki,ckj->cij",
        lax.all_gather(left_chan, "col", axis=2, tiled=True),
        right_chan,
        preferred_element_type=F32,
    ).astype(BF16)
    triangle_in = lax.all_to_all(summed_in, "row", split_axis=1, concat_axis=0, tiled=True)
    return finish(first_pass, triangle_in, gate_vals, out_weights[1])


def solution(mesh):
    n_row, n_col = mesh.shape["row"], mesh.shape["col"]

    def per_device(pair_act, in_weights, out_weights, chain_lengths):
        if pair_act.shape[2] % (n_row * n_col) == 0:
            return split_channels(n_row, n_col, pair_act, in_weights, out_weights, chain_lengths)
        return split_rows(pair_act, in_weights, out_weights, chain_lengths)

    in_specs = (P(("parts", "row"), "col", None), P(), P(), P("parts"))
    out_specs = P(("parts", "row"), "col", None)
    return jax.shard_map(
        per_device, mesh=mesh, in_specs=in_specs, out_specs=out_specs, check_vma=False
    )
```

time: 180 us -> 115 us (0.64)
  waiting for transfers between devices: 55.8 us -> 0 us
  blocking collectives: 62.9 us -> 99.9 us
  starting transfers between devices: 22.7 us -> 0 us
  between operations: 14.4 us -> 0.71 us
  local copies, waits for them, and re-layouts: 13.9 us -> 3.26 us
  Pallas kernels: 0 us -> 10.5 us
  matrix products: 6.5 us -> 0 us
  other arithmetic: 2.65 us -> 0.08 us
    all_to_all x4 -> x0, waiting for transfers between devices: 54.7 us -> none  [the longest x1 14 us: per_device(): lax.all_to_all(summed_in, 'row', split_axis=1, concat_axis=0, tiled=True)]
    all_to_all x4, blocking collectives: 62.9 us -> 99.9 us  [exchange(): return lax.all_to_all(array, axes, split_axis=0, concat_axis=0, tiled=True)]
    all_to_all x4 -> x0, starting transfers between devices: 22.6 us -> none  [the longest x1 7.39 us: to_channels(): lax.all_to_all(right_vals, 'row', split_axis=0, concat_axis=1, tiled=True)]
    pallas_call x0 -> x5, Pallas kernels: none -> 10.5 us  [call(): pl.pallas_call(kernel, name=name, out_shape=out_shape, in_specs=in_specs,...]
    dot_general x8 -> x0, matrix products: 6.5 us -> none  [the longest x1 1.7 us: per_device(): jnp.einsum('cik,cjk->cij', left_rows, lax.all_gather(right_chan, 'col', a...]
    convert_element_type x9 -> x0, local copies, waits for them, and re-layouts: 5.79 us -> none  [the longest x2 1.62 us: project(): left_vals = (jax.nn.sigmoid(projected[0:width]) * projected[width:2 * wid...]
    all_to_all x11 -> x0, local copies, waits for them, and re-layouts: 4.56 us -> none  [the longest x4 1.42 us: to_channels(): lax.all_to_all(left_vals, 'row', split_axis=0, concat_axis=1, tiled=True)]
  transfers between devices with their start and end apart: 6 -> 0, of which waited for: 5 -> 0; matrix products, arithmetic and copies ran while one was open for 2% -> 0% of each run, Pallas kernels for 0% -> 0%
where the time goes in v1:
time: 115 us; the launch traced here: 114 us
  blocking collectives  99.9 us (87%)
  Pallas kernels  10.5 us (9%)
  local copies, waits for them, and re-layouts  3.26 us (3%)
    all_to_all x4, blocking collectives, exchange(): return lax.all_to_all(array, axes, split_axis=0, concat_axis=0, tiled=True)  99.9 us
    pallas_call x5, Pallas kernels, call(): pl.pallas_call(kernel, name=name, out_shape=out_shape, in_specs=in_specs,...  10.5 us
    unnamed x10, local copies, waits for them, and re-layouts  2.68 us

profile of v1, /device:TPU:0, one launch (start us, length us, event | category | flops | bytes accessed | tf_op | source)
XLA Modules:
  0.0 114.4 jit_solution(5877449604514402276)
XLA Ops:
  0.0 0.0 copy-start.4
  0.0 0.7 copy-done.4
  0.7 0.6 slice.3
  1.9 0.1 pad_add_fusion.limits_ref
  2.0 0.0 copy-start
  2.0 1.0 copy-done
  2.9 0.0 copy-start.3
  2.9 1.0 copy-done.3
  4.0 3.5 %project.1 = (bf16[32,2,4,16,128]{4,3,2,1,0:T(8,128)(2,1)S(1)}, bf16[16,128,128]{2,1,0:T(8,128)(2,1)S(1)}, bf16[16,128,128]{2,1,0:T(8,128)(2,1)S(1)}) custom-call(s32[2]{0:T(128)S(1)} %pad_add_fusion.limits_ref, bf16[16,128,128]{2,1,0:T(8,128)(2,1)S(1)} %copy-done.3, bf16[2,128,640]{2,1,0:T(8,128)(2,1)S(1)} %copy-done), custom_call_target="tpu_custom_call" | custom-call | flops 335544320 | bytes 2097152 | tf_op jit(solution)/shard_map/project/pallas_call | solution.py:138
  7.5 33.3 %all_to_all.20 = bf16[32,2,4,16,128]{4,3,2,1,0:T(8,128)(2,1)S(1)} all-to-all(bf16[32,2,4,16,128]{4,3,2,1,0:T(8,128)(2,1)S(1)} %get-tuple-element.11), channel_id=1, replica_groups=mesh['parts'=1,'row'=16,'col'=2] {'row','col'}, dimensions={0} | all-to-all | bytes 2097152 | tf_op jit(solution)/shard_map/all_to_all | solution.py:174
  40.8 0.3 triangle.2
  41.1 0.0 copy-start.1
  41.2 0.0 copy-start.2
  41.2 18.4 %all_to_all.21 = bf16[32,4,16,128]{3,2,1,0:T(8,128)(2,1)S(1)} all-to-all(bf16[32,4,16,128]{3,2,1,0:T(8,128)(2,1)S(1)} %bitcast.12), channel_id=1, replica_groups=mesh['parts'=1,'row'=16,'col'=2] {'row','col'}, dimensions={0} | all-to-all | bytes 1048576 | tf_op jit(solution)/shard_map/all_to_all | solution.py:174
  59.6 0.0 copy-done.1
  59.6 0.0 copy-done.2
  59.6 4.7 %finish_project.1 = (bf16[32,2,4,16,128]{4,3,2,1,0:T(8,128)(2,1)S(1)}, bf16[16,128,128]{2,1,0:T(8,128)(2,1)S(1)}, bf16[16,128,128]{2,1,0:T(8,128)(2,1)S(1)}) custom-call(s32[2]{0:T(128)S(1)} %pad_add_fusion.limits_ref, bf16[128,16,128]{2,1,0:T(8,128)(2,1)S(1)} %bitcast.11, bf16[16,128,128]{2,1,0:T(8,128)(2,1)S(1)} %get-tuple-element.12.gate_in_ref, ...), custom_call_target="tpu_custom_call" | custom-call | flops 402653184 | bytes 2097152 | tf_op jit(solution)/shard_map/finish_project/pallas_call | solution.py:138
  64.3 29.7 %all_to_all.22 = bf16[32,2,4,16,128]{4,3,2,1,0:T(8,128)(2,1)S(1)} all-to-all(bf16[32,2,4,16,128]{4,3,2,1,0:T(8,128)(2,1)S(1)} %get-tuple-element.14), channel_id=1, replica_groups=mesh['parts'=1,'row'=16,'col'=2] {'row','col'}, dimensions={0} | all-to-all | bytes 2097152 | tf_op jit(solution)/shard_map/all_to_all | solution.py:174
  94.0 0.3 triangle.3
  94.3 18.4 %all_to_all.23 = bf16[32,4,16,128]{3,2,1,0:T(8,128)(2,1)S(1)} all-to-all(bf16[32,4,16,128]{3,2,1,0:T(8,128)(2,1)S(1)} %bitcast.13), channel_id=1, replica_groups=mesh['parts'=1,'row'=16,'col'=2] {'row','col'}, dimensions={0} | all-to-all | bytes 1048576 | tf_op jit(solution)/shard_map/all_to_all | solution.py:174
  112.7 1.7 %finish.1 = bf16[16,128,128]{2,1,0:T(8,128)(2,1)} custom-call(bf16[128,16,128]{2,1,0:T(8,128)(2,1)S(1)} %bitcast.14, bf16[16,128,128]{2,1,0:T(8,128)(2,1)S(1)} %get-tuple-element.15.gate_ref, bf16[16,128,128]{2,1,0:T(8,128)(2,1)S(1)} %get-tuple-element.16.pair_t_ref, bf16[2,128,128]{2,1,0:T(8,128)(2,1)S(1)} %copy-done.2), custom_call_target="tpu_custom_call" | custom-call | flops 67108864 | bytes 2097152 | tf_op jit(solution)/shard_map/finish/pallas_call | solution.py:138
Async XLA Ops:
  0.0 0.7 copy-start.4
  2.0 1.0 copy-start
  2.9 1.0 copy-start.3
  41.1 18.5 %copy-start.1 = (bf16[2,128,640]{2,1,0:T(8,128)(2,1)S(1)}, bf16[2,128,640]{2,1,0:T(8,128)(2,1)}, u32[]{:S(2)}) copy-start(bf16[2,128,640]{2,1,0:T(8,128)(2,1)} %weights_ref.3) | copy-start | bytes 983044
  41.2 18.4 %copy-start.2 = (bf16[2,128,128]{2,1,0:T(8,128)(2,1)S(1)}, bf16[2,128,128]{2,1,0:T(8,128)(2,1)}, u32[]{:S(2)}) copy-start(bf16[2,128,128]{2,1,0:T(8,128)(2,1)} %wo_ref.3) | copy-start | bytes 196612

commit v2 on v1

--- a/solution.py
+++ b/solution.py
@@ -28,95 +28,110 @@
     return jnp.dot(lhs, rhs, preferred_element_type=F32)
 
 
-def mask_of(limits_ref, first, group, cols):
+def mask_of(limits, first, group, cols):
     lane = lax.broadcasted_iota(jnp.int32, (1, cols), 1)
-    col_valid = lane < limits_ref[1]
+    col_valid = lane < limits[1]
     parts = [
-        jnp.where(jnp.logical_and(col_valid, first + g < limits_ref[0]), 1.0, 0.0)
-        for g in range(group)
+        jnp.where(jnp.logical_and(col_valid, first + g < limits[0]), 1.0, 0.0) for g in range(group)
     ]
     return jnp.concatenate(parts, axis=1).astype(F32)
 
 
+def limits_of(lengths_ref, rows, cols):
+    valid = rows * lax.axis_size("row") - lengths_ref[lengths_ref.shape[0] - 1]
+    return valid - lax.axis_index("row") * rows, valid - lax.axis_index("col") * cols
+
+
+def store_rows(ref, first, group, vals):
+    cols = vals.shape[1] // group
+    for g in range(group):
+        ref[first + g] = vals[:, g * cols : (g + 1) * cols]
+
+
+def load_rows(ref, first, group):
+    return jnp.concatenate([ref[first + g] for g in range(group)], axis=1)
+
+
 def project_rows(first, group, pair_vals, mask, weights_t, left_scr, right_scr, gate_ref):
     width = pair_vals.shape[0]
-    cols = pair_vals.shape[1] // group
     normed = layer_norm(pair_vals, 0).astype(BF16)
     for side, scr in enumerate((left_scr, right_scr)):
         both = dot(weights_t[2 * side * width : (2 * side + 2) * width, :], normed)
         vals = sigmoid(both[0:width]) * both[width : 2 * width] * mask
-        for g in range(group):
-            scr[(first + g) * width : (first + g + 1) * width, :] = vals[
-                :, g * cols : (g + 1) * cols
-            ]
-    gate = sigmoid(dot(weights_t[4 * width : 5 * width, :], normed)).astype(BF16)
-    for g in range(group):
-        gate_ref[first + g] = gate[:, g * cols : (g + 1) * cols]
-
-
-def send_channels(rows, width, left_scr, right_scr, send_ref):
-    per = send_ref.shape[2]
-    for c in range(width):
-        for side, scr in enumerate((left_scr, right_scr)):
-            send_ref[c // per, side, c % per] = scr[pl.ds(c, rows, stride=width), :].astype(BF16)
-
-
-def first_kernel(limits_ref, pair_ref, weights_ref, send_ref, gate_ref, pair_t_ref, left_scr, right_scr, wt_scr):
-    rows, cols, width = pair_ref.shape
+        store_rows(scr, first, group, vals.astype(BF16))
+    gate = sigmoid(dot(weights_t[4 * width : 5 * width, :], normed))
+    store_rows(gate_ref, first, group, gate.astype(BF16))
+
+
+def send_channels(left_scr, right_scr, send_ref):
+    rows, width, cols = left_scr.shape
+    group, _, per = send_ref.shape[:3]
+    for side, scr in enumerate((left_scr, right_scr)):
+        send_ref[:, side] = jnp.swapaxes(scr[...], 0, 1).reshape(group, per, rows, cols)
+
+
+def first_kernel(
+    lengths_ref, pair_hbm, weights_hbm, send_ref, gate_ref, pair_t_ref,
+    left_scr, right_scr, wt_scr, pair_scr, weights_scr, sems,
+):
+    rows, cols, width = pair_scr.shape
     group = 2
-    wt_scr[...] = weights_ref[0].astype(F32).T.astype(BF16)
+    copies = [
+        pltpu.make_async_copy(weights_hbm.at[0], weights_scr, sems.at[0]),
+        pltpu.make_async_copy(pair_hbm, pair_scr, sems.at[1]),
+    ]
+    for copy in copies:
+        copy.start()
+    limits = limits_of(lengths_ref, rows, cols)
+    copies[0].wait()
+    wt_scr[...] = weights_scr[...].T
+    copies[1].wait()
     for first in range(0, rows, group):
-        blocks = [pair_ref[first + g].astype(F32).T for g in range(group)]
-        for g in range(group):
-            pair_t_ref[first + g] = blocks[g].astype(BF16)
+        blocks = jnp.concatenate([pair_scr[first + g].T for g in range(group)], axis=1)
+        store_rows(pair_t_ref, first, group, blocks)
         project_rows(
-            first, group, jnp.concatenate(blocks, axis=1), mask_of(limits_ref, first, group, cols),
+            first, group, blocks.astype(F32), mask_of(limits, first, group, cols),
             wt_scr, left_scr, right_scr, gate_ref,
         )
-    send_channels(rows, width, left_scr, right_scr, send_ref)
-
-
-def finish_rows(first, group, tri_scr, rows, wo_t, gate_ref, pair_t_ref):
-    width = pair_t_ref.shape[1]
-    tri = jnp.concatenate(
-        [tri_scr[pl.ds(first + g, width, stride=rows), :] for g in range(group)], axis=1
-    )
-    tri_normed = layer_norm(tri, 0).astype(BF16)
-    delta = dot(wo_t, tri_normed)
-    gate = jnp.concatenate([gate_ref[first + g] for g in range(group)], axis=1)
-    pair = jnp.concatenate([pair_t_ref[first + g] for g in range(group)], axis=1)
-    return (pair.astype(F32) + delta * gate.astype(F32)).astype(BF16)
+    send_channels(left_scr, right_scr, send_ref)
+
+
+def finish_rows(first, group, tri_scr, wo_t, gate_ref, pair_t_ref):
+    tri = load_rows(tri_scr, first, group).astype(F32)
+    delta = dot(wo_t, layer_norm(tri, 0).astype(BF16))
+    gate = load_rows(gate_ref, first, group).astype(F32)
+    return (load_rows(pair_t_ref, first, group).astype(F32) + delta * gate).astype(BF16)
 
 
 def middle_kernel(
-    limits_ref, tri_ref, gate_in_ref, pair_t_in_ref, wo_ref, weights_ref,
+    lengths_ref, tri_ref, gate_in_ref, pair_t_in_ref, wo_ref, weights_ref,
     send_ref, gate_ref, pair_t_ref, left_scr, right_scr, wt_scr, tri_scr,
 ):
     width, rows, cols = tri_ref.shape
     group = 2
-    wt_scr[...] = weights_ref[1].astype(F32).T.astype(BF16)
-    wo_t = wo_ref[0].astype(F32).T.astype(BF16)
-    tri_scr[...] = tri_ref[...].astype(F32).reshape(width * rows, cols)
+    limits = limits_of(lengths_ref, rows, cols)
+    wt_scr[...] = weights_ref[1].T
+    wo_t = wo_ref[0].T
+    tri_scr[...] = jnp.swapaxes(tri_ref[...], 0, 1)
     for first in range(0, rows, group):
-        passed = finish_rows(first, group, tri_scr, rows, wo_t, gate_in_ref, pair_t_in_ref)
-        for g in range(group):
-            pair_t_ref[first + g] = passed[:, g * cols : (g + 1) * cols]
+        passed = finish_rows(first, group, tri_scr, wo_t, gate_in_ref, pair_t_in_ref)
+        store_rows(pair_t_ref, first, group, passed)
         project_rows(
-            first, group, passed.astype(F32), mask_of(limits_ref, first, group, cols),
+            first, group, passed.astype(F32), mask_of(limits, first, group, cols),
             wt_scr, left_scr, right_scr, gate_ref,
         )
-    send_channels(rows, width, left_scr, right_scr, send_ref)
+    send_channels(left_scr, right_scr, send_ref)
 
 
 def last_kernel(tri_ref, gate_ref, pair_t_ref, wo_ref, out_ref, tri_scr):
     width, rows, cols = tri_ref.shape
     group = 2
-    wo_t = wo_ref[1].astype(F32).T.astype(BF16)
-    tri_scr[...] = tri_ref[...].astype(F32).reshape(width * rows, cols)
+    wo_t = wo_ref[1].T
+    tri_scr[...] = jnp.swapaxes(tri_ref[...], 0, 1)
     for first in range(0, rows, group):
-        passed = finish_rows(first, group, tri_scr, rows, wo_t, gate_ref, pair_t_ref)
+        passed = finish_rows(first, group, tri_scr, wo_t, gate_ref, pair_t_ref)
         for g in range(group):
-            out_ref[first + g] = passed[:, g * cols : (g + 1) * cols].astype(F32).T.astype(BF16)
+            out_ref[first + g] = passed[:, g * cols : (g + 1) * cols].T
 
 
 def triangle_kernel(incoming, recv_ref, out_ref):
@@ -149,6 +164,7 @@
 
 VM = pl.BlockSpec(memory_space=pltpu.VMEM)
 SM = pl.BlockSpec(memory_space=pltpu.SMEM)
+HBM = pl.BlockSpec(memory_space=pltpu.HBM)
 
 
 def split_channels(n_row, n_col, pair_act, in_weights, out_weights, chain_lengths):
@@ -156,15 +172,10 @@
     group = n_row * n_col
     per = width // group
     axes = ("row", "col")
-    count_valid = rows * n_row - chain_lengths[chain_lengths.shape[0] - 1]
-    limits = jnp.stack(
-        [count_valid - lax.axis_index("row") * rows, count_valid - lax.axis_index("col") * cols]
-    ).astype(jnp.int32)
-
     send_shape = jax.ShapeDtypeStruct((group, 2, per, rows, cols), BF16)
     block_shape = jax.ShapeDtypeStruct((rows, width, cols), BF16)
     tri_shape = jax.ShapeDtypeStruct((n_row, n_col, per, rows, cols), BF16)
-    scr = pltpu.VMEM((rows * width, cols), F32)
+    scr = pltpu.VMEM((rows, width, cols), BF16)
     wt_scr = pltpu.VMEM((5 * width, width), BF16)
     flops_in = 2 * rows * cols * width * 5 * width
     flops_out = 2 * rows * cols * width * width
@@ -181,14 +192,18 @@
         return exchange(tri.reshape((group,) + tri.shape[2:])).reshape(width, rows, cols)
 
     send, gate, pair_t = call(
-        first_kernel, "project", (send_shape, block_shape, block_shape), [scr, scr, wt_scr],
-        [SM, VM, VM], flops_in, limits, pair_act, in_weights,
+        first_kernel, "project", (send_shape, block_shape, block_shape),
+        [
+            scr, scr, wt_scr, pltpu.VMEM(pair_act.shape, BF16),
+            pltpu.VMEM(in_weights.shape[1:], BF16), pltpu.SemaphoreType.DMA((2,)),
+        ],
+        [SM, HBM, HBM], flops_in, chain_lengths, pair_act, in_weights,
     )
     tri = triangle(send, False)
     send, gate, pair_t = call(
         middle_kernel, "finish_project", (send_shape, block_shape, block_shape), [scr, scr, wt_scr, scr],
         [SM, VM, VM, VM, VM, VM], flops_in + flops_out,
-        limits, tri, gate, pair_t, out_weights, in_weights,
+        chain_lengths, tri, gate, pair_t, out_weights, in_weights,
     )
     tri = triangle(send, True)
     return call(

time: 115 us -> 112 us (0.974)
  Pallas kernels: 10.5 us -> 8.34 us
    pallas_call x5, Pallas kernels: 10.5 us -> 8.34 us  [call(): pl.pallas_call(kernel, name=name, out_shape=out_shape, in_specs=in_specs,...]
    unnamed x10 -> x12, local copies, waits for them, and re-layouts: 2.68 us -> 3.33 us
where the time goes in v2:
time: 112 us
  blocking collectives  99.9 us (89%)
  Pallas kernels  8.34 us (7%)
  local copies, waits for them, and re-layouts  3.33 us (3%)
    all_to_all x4, blocking collectives, exchange(): return lax.all_to_all(array, axes, split_axis=0, concat_axis=0, tiled=True)  99.9 us
    pallas_call x5, Pallas kernels, call(): pl.pallas_call(kernel, name=name, out_shape=out_shape, in_specs=in_specs,...  8.34 us
    unnamed x12, local copies, waits for them, and re-layouts  3.33 us

profile of v2, /device:TPU:0, one launch (start us, length us, event | category | flops | bytes accessed | tf_op | source)
XLA Modules:
  0.0 111.6 jit_solution(17537433296205685732)
XLA Ops:
  0.0 0.0 copy-start
  0.0 1.0 copy-done
  1.0 0.0 copy-start.3
  1.0 0.7 copy-done.3
  1.6 0.0 copy-start.5
  1.6 1.0 copy-done.5
  2.7 2.5 %project.1 = (bf16[32,2,4,16,128]{4,3,2,1,0:T(8,128)(2,1)S(1)}, bf16[16,128,128]{2,1,0:T(8,128)(2,1)S(1)}, bf16[16,128,128]{2,1,0:T(8,128)(2,1)S(1)}) custom-call(s32[8]{0:T(128)S(1)} %copy-done.3, bf16[16,128,128]{2,1,0:T(8,128)(2,1)S(1)} %copy-done.5, bf16[2,128,640]{2,1,0:T(8,128)(2,1)S(1)} %copy-done), custom_call_target="tpu_custom_call" | custom-call | flops 335544320 | bytes 2097152 | tf_op jit(solution)/shard_map/project/pallas_call | solution.py:153
  5.2 33.3 %all_to_all.20 = bf16[32,2,4,16,128]{4,3,2,1,0:T(8,128)(2,1)S(1)} all-to-all(bf16[32,2,4,16,128]{4,3,2,1,0:T(8,128)(2,1)S(1)} %get-tuple-element.11), channel_id=1, replica_groups=mesh['parts'=1,'row'=16,'col'=2] {'row','col'}, dimensions={0} | all-to-all | bytes 2097152 | tf_op jit(solution)/shard_map/all_to_all | solution.py:185
  38.5 0.3 triangle.2
  38.9 0.0 copy-start.1
  38.9 0.0 copy-start.2
  38.9 18.4 %all_to_all.21 = bf16[32,4,16,128]{3,2,1,0:T(8,128)(2,1)S(1)} all-to-all(bf16[32,4,16,128]{3,2,1,0:T(8,128)(2,1)S(1)} %bitcast.9), channel_id=1, replica_groups=mesh['parts'=1,'row'=16,'col'=2] {'row','col'}, dimensions={0} | all-to-all | bytes 1048576 | tf_op jit(solution)/shard_map/all_to_all | solution.py:185
  57.3 0.0 copy-start.4
  57.3 0.0 copy-done.1
  57.3 0.0 copy-done.2
  57.3 0.6 copy-done.4
  58.0 3.7 %finish_project.1 = (bf16[32,2,4,16,128]{4,3,2,1,0:T(8,128)(2,1)S(1)}, bf16[16,128,128]{2,1,0:T(8,128)(2,1)S(1)}, bf16[16,128,128]{2,1,0:T(8,128)(2,1)S(1)}) custom-call(s32[8]{0:T(128)S(1)} %copy-done.4, bf16[128,16,128]{2,1,0:T(8,128)(2,1)S(1)} %bitcast.8, bf16[16,128,128]{2,1,0:T(8,128)(2,1)S(1)} %get-tuple-element.12.gate_in_ref, ...), custom_call_target="tpu_custom_call" | custom-call | flops 402653184 | bytes 2097152 | tf_op jit(solution)/shard_map/finish_project/pallas_call | solution.py:153
  61.7 29.7 %all_to_all.22 = bf16[32,2,4,16,128]{4,3,2,1,0:T(8,128)(2,1)S(1)} all-to-all(bf16[32,2,4,16,128]{4,3,2,1,0:T(8,128)(2,1)S(1)} %get-tuple-element.14), channel_id=1, replica_groups=mesh['parts'=1,'row'=16,'col'=2] {'row','col'}, dimensions={0} | all-to-all | bytes 2097152 | tf_op jit(solution)/shard_map/all_to_all | solution.py:185
  91.3 0.3 triangle.3
  91.7 18.4 %all_to_all.23 = bf16[32,4,16,128]{3,2,1,0:T(8,128)(2,1)S(1)} all-to-all(bf16[32,4,16,128]{3,2,1,0:T(8,128)(2,1)S(1)} %bitcast.10), channel_id=1, replica_groups=mesh['parts'=1,'row'=16,'col'=2] {'row','col'}, dimensions={0} | all-to-all | bytes 1048576 | tf_op jit(solution)/shard_map/all_to_all | solution.py:185
  110.1 1.5 %finish.1 = bf16[16,128,128]{2,1,0:T(8,128)(2,1)} custom-call(bf16[128,16,128]{2,1,0:T(8,128)(2,1)S(1)} %bitcast.11, bf16[16,128,128]{2,1,0:T(8,128)(2,1)S(1)} %get-tuple-element.15.gate_ref, bf16[16,128,128]{2,1,0:T(8,128)(2,1)S(1)} %get-tuple-element.16.pair_t_ref, bf16[2,128,128]{2,1,0:T(8,128)(2,1)S(1)} %copy-done.2), custom_call_target="tpu_custom_call" | custom-call | flops 67108864 | bytes 2097152 | tf_op jit(solution)/shard_map/finish/pallas_call | solution.py:153
Async XLA Ops:
  0.0 1.0 copy-start
  1.0 0.7 copy-start.3
  1.6 1.0 copy-start.5
  38.9 18.5 %copy-start.1 = (bf16[2,128,640]{2,1,0:T(8,128)(2,1)S(1)}, bf16[2,128,640]{2,1,0:T(8,128)(2,1)}, u32[]{:S(2)}) copy-start(bf16[2,128,640]{2,1,0:T(8,128)(2,1)} %weights_ref.1) | copy-start | bytes 983044
  38.9 18.4 %copy-start.2 = (bf16[2,128,128]{2,1,0:T(8,128)(2,1)S(1)}, bf16[2,128,128]{2,1,0:T(8,128)(2,1)}, u32[]{:S(2)}) copy-start(bf16[2,128,128]{2,1,0:T(8,128)(2,1)} %wo_ref.3) | copy-start | bytes 196612
  57.3 0.7 copy-start.4

commit v3 on v2

v3 whole, which is shorter than its diff:
```python
import functools

import jax
import jax.numpy as jnp
from jax import lax
from jax.experimental import pallas as pl
from jax.experimental.pallas import tpu as pltpu
from jax.sharding import PartitionSpec as P

epsilon = 1e-05
F32 = jnp.float32
BF16 = jnp.bfloat16
VMEM_LIMIT = 32 * 1024 * 1024


def layer_norm(values, along_axis):
    mean_vals = jnp.mean(values, axis=along_axis, keepdims=True)
    centred = values - mean_vals
    variance = jnp.mean(centred * centred, axis=along_axis, keepdims=True)
    return centred * lax.rsqrt(variance + epsilon)


def sigmoid(values):
    return 0.5 * jnp.tanh(0.5 * values) + 0.5


def dot(lhs, rhs):
    return jnp.dot(lhs, rhs, preferred_element_type=F32)


def store_mask(ref, row_limit, col_limit):
    row = lax.broadcasted_iota(jnp.int32, ref.shape, 0)
    col = lax.broadcasted_iota(jnp.int32, ref.shape, 1)
    ref[...] = jnp.where(jnp.logical_and(row < row_limit, col < col_limit), 1.0, 0.0).astype(F32)


def load_mask(ref, first, group):
    return jnp.concatenate([ref[first + g : first + g + 1, :] for g in range(group)], axis=1)


def store_rows(ref, first, group, vals):
    cols = vals.shape[1] // group
    for g in range(group):
        ref[first + g] = vals[:, g * cols : (g + 1) * cols]


def load_rows(ref, first, group):
    return jnp.concatenate([ref[first + g] for g in range(group)], axis=1)


def project_side(normed, mask, weights_t, side):
    width = normed.shape[0]
    both = dot(weights_t[2 * side * width : (2 * side + 2) * width, :], normed)
    return (sigmoid(both[0:width]) * both[width : 2 * width] * mask).astype(BF16)


def project_rows(first, group, pair_vals, mask, weights_t, left_scr, right_scr, gate_ref):
    width = pair_vals.shape[0]
    normed = layer_norm(pair_vals, 0).astype(BF16)
    for side, scr in enumerate((left_scr, right_scr)):
        store_rows(scr, first, group, project_side(normed, mask, weights_t, side))
    gate = sigmoid(dot(weights_t[4 * width : 5 * width, :], normed))
    store_rows(gate_ref, first, group, gate.astype(BF16))


def send_channels(scr, send_ref, side):
    rows, width, cols = scr.shape
    group, _, per = send_ref.shape[:3]
    send_ref[:, side] = jnp.swapaxes(scr[...], 0, 1).reshape(group, per, rows, cols)


def first_kernel(
    lengths_ref, pair_ref, weights_ref, send_ref, gate_ref, pair_t_ref, mask_ref, other_mask_ref,
    left_scr, right_scr, wt_scr,
):
    rows, cols, width = pair_ref.shape
    group = 2
    halves, in_half = lax.axis_size("half"), lax.axis_size("row")
    half, row = lax.axis_index("half"), lax.axis_index("row")
    valid = rows * halves * in_half - lengths_ref[lengths_ref.shape[0] - 1]
    col_limit = valid - lax.axis_index("col") * cols
    store_mask(mask_ref, valid - (half * in_half + row) * rows, col_limit)
    store_mask(other_mask_ref, valid - ((1 - half) * in_half + row) * rows, col_limit)
    wt_scr[...] = weights_ref[0].T
    for first in range(0, rows, group):
        blocks = jnp.concatenate([pair_ref[first + g].T for g in range(group)], axis=1)
        store_rows(pair_t_ref, first, group, blocks)
        project_rows(
            first, group, blocks.astype(F32), load_mask(mask_ref, first, group),
            wt_scr, left_scr, right_scr, gate_ref,
        )
    send_channels(left_scr, send_ref, 0)
    send_channels(right_scr, send_ref, 1)


def right_kernel(pair_ref, weights_ref, mask_ref, send_ref, right_scr, wt_scr):
    rows, cols, width = pair_ref.shape
    group = 2
    wt_scr[2 * width : 4 * width, :] = weights_ref[0, :, 2 * width : 4 * width].T
    for first in range(0, rows, group):
        blocks = jnp.concatenate([pair_ref[first + g].T for g in range(group)], axis=1)
        normed = layer_norm(blocks.astype(F32), 0).astype(BF16)
        vals = project_side(normed, load_mask(mask_ref, first, group), wt_scr, 1)
        store_rows(right_scr, first, group, vals)
    send_channels(right_scr, send_ref, 0)


def finish_rows(first, group, tri_scr, wo_t, gate_ref, pair_t_ref):
    tri = load_rows(tri_scr, first, group).astype(F32)
    delta = dot(wo_t, layer_norm(tri, 0).astype(BF16))
    gate = load_rows(gate_ref, first, group).astype(F32)
    return (load_rows(pair_t_ref, first, group).astype(F32) + delta * gate).astype(BF16)


def middle_kernel(
    tri_ref, gate_in_ref, pair_t_in_ref, mask_ref, wo_ref, weights_ref,
    send_ref, gate_ref, pair_t_ref, left_scr, right_scr, wt_scr, tri_scr,
):
    width, rows, cols = tri_ref.shape
    group = 2
    wt_scr[...] = weights_ref[1].T
    wo_t = wo_ref[0].T
    tri_scr[...] = jnp.swapaxes(tri_ref[...], 0, 1)
    for first in range(0, rows, group):
        passed = finish_rows(first, group, tri_scr, wo_t, gate_in_ref, pair_t_in_ref)
        store_rows(pair_t_ref, first, group, passed)
        project_rows(
            first, group, passed.astype(F32), load_mask(mask_ref, first, group),
            wt_scr, left_scr, right_scr, gate_ref,
        )
    send_channels(left_scr, send_ref, 0)
    send_channels(right_scr, send_ref, 1)


def last_kernel(tri_ref, gate_ref, pair_t_ref, wo_ref, out_ref, tri_scr):
    width, rows, cols = tri_ref.shape
    group = 2
    wo_t = wo_ref[1].T
    tri_scr[...] = jnp.swapaxes(tri_ref[...], 0, 1)
    for first in range(0, rows, group):
        passed = finish_rows(first, group, tri_scr, wo_t, gate_ref, pair_t_ref)
        for g in range(group):
            out_ref[first + g] = passed[:, g * cols : (g + 1) * cols].T


def channel_of(recv_ref, side, c):
    n_row, n_col, _, _, rows, cols = recv_ref.shape
    return jnp.concatenate(
        [recv_ref[:, x, side, c].reshape(n_row * rows, cols) for x in range(n_col)], axis=1
    )


def store_channel(out_ref, c, tri):
    n_row, n_col, _, rows, cols = out_ref.shape
    for x in range(n_col):
        out_ref[:, x, c] = tri[:, x * cols : (x + 1) * cols].reshape(n_row, rows, cols)


def outgoing_kernel(own_ref, other_ref, out_ref):
    lower = lax.axis_index("half") == 0
    for c in range(own_ref.shape[3]):
        own, other = channel_of(own_ref, 1, c), channel_of(other_ref, 0, c)
        right = jnp.concatenate(
            [jnp.where(lower, own, other), jnp.where(lower, other, own)], axis=0
        )
        tri = lax.dot_general(
            channel_of(own_ref, 0, c), right, (((1,), (1,)), ((), ())), preferred_element_type=F32
        )
        store_channel(out_ref, c, tri.astype(BF16))


def incoming_kernel(recv_ref, out_ref):
    for c in range(recv_ref.shape[3]):
        tri = lax.dot_general(
            channel_of(recv_ref, 0, c), channel_of(recv_ref, 1, c), (((0,), (0,)), ((), ())),
            preferred_element_type=F32,
        )
        store_channel(out_ref, c, tri.astype(BF16))


def call(kernel, name, out_shape, scratch, in_specs, flops, *args):
    return pl.pallas_call(
        kernel,
        name=name,
        out_shape=out_shape,
        in_specs=in_specs,
        out_specs=jax.tree.map(lambda _: pl.BlockSpec(memory_space=pltpu.VMEM), out_shape),
        scratch_shapes=scratch,
        compiler_params=pltpu.CompilerParams(vmem_limit_bytes=VMEM_LIMIT),
        cost_estimate=pl.CostEstimate(flops=flops, bytes_accessed=2 << 20, transcendentals=0),
    )(*args)


VM = pl.BlockSpec(memory_space=pltpu.VMEM)
SM = pl.BlockSpec(memory_space=pltpu.SMEM)


def split_channels(n_half, n_row, n_col, pair_act, in_weights, out_weights, chain_lengths):
    rows, cols, width = pair_act.shape
    in_half, in_all = ("row", "col"), ("half", "row", "col")
    half_group, group = n_row * n_col, n_half * n_row * n_col
    half_per, per = width // half_group, width // group

    def shape_of(*dims, dtype=BF16):
        return jax.ShapeDtypeStruct(dims, dtype)

    def exchange(array, axes):
        return lax.all_to_all(array, axes, split_axis=0, concat_axis=0, tiled=True)

    block_shape = shape_of(rows, width, cols)
    mask_shape = shape_of(rows, cols, dtype=F32)
    scr = pltpu.VMEM((rows, width, cols), BF16)
    wt_scr = pltpu.VMEM((5 * width, width), BF16)
    flops_out = 2 * rows * cols * width * width
    flops_tri = 2 * per * (n_half * n_row * rows) ** 2 * n_col * cols

    other = lax.ppermute(pair_act, "half", [(0, 1), (1, 0)])
    send, gate, pair_t, mask, other_mask = call(
        first_kernel, "project",
        (shape_of(half_group, 2, half_per, rows, cols), block_shape, block_shape, mask_shape, mask_shape),
        [scr, scr, wt_scr], [SM, VM, VM], 5 * flops_out, chain_lengths, pair_act, in_weights,
    )
    own = exchange(send, in_half).reshape(n_row, n_col, 2, half_per, rows, cols)
    send = call(
        right_kernel, "project_right", shape_of(half_group, 1, half_per, rows, cols),
        [scr, wt_scr], [VM, VM, VM], 2 * flops_out, other, in_weights, other_mask,
    )
    other = exchange(send, in_half).reshape(n_row, n_col, 1, half_per, rows, cols)
    tri = call(
        outgoing_kernel, "outgoing", shape_of(n_row, n_col, half_per, rows, cols),
        [], [VM, VM], flops_tri, own, other,
    )
    tri = exchange(tri.reshape(half_group, half_per, rows, cols), in_half).reshape(width, rows, cols)
    send, gate, pair_t = call(
        middle_kernel, "finish_project", (shape_of(group, 2, per, rows, cols), block_shape, block_shape),
        [scr, scr, wt_scr, scr], [VM] * 6, 6 * flops_out,
        tri, gate, pair_t, mask, out_weights, in_weights,
    )
    recv = exchange(send, in_all).reshape(n_half * n_row, n_col, 2, per, rows, cols)
    tri = call(
        incoming_kernel, "incoming", shape_of(n_half * n_row, n_col, per, rows, cols), [], [VM], flops_tri, recv
    )
    tri = exchange(tri.reshape(group, per, rows, cols), in_all).reshape(width, rows, cols)
    return call(
        last_kernel, "finish", shape_of(*pair_act.shape), [scr], [VM] * 4, flops_out,
        tri, gate, pair_t, out_weights,
    )


def project(pair_act, weights, pair_mask):
    width = pair_act.shape[2]
    normed = layer_norm(pair_act.astype(F32), 2).astype(BF16)
    projected = jnp.einsum("rjd,de->erj", normed, weights[:, 0 : 4 * width], preferred_element_type=F32)
    left_vals = (jax.nn.sigmoid(projected[0:width]) * projected[width : 2 * width] * pair_mask).astype(BF16)
    right_vals = (
        jax.nn.sigmoid(projected[2 * width : 3 * width]) * projected[3 * width : 4 * width] * pair_mask
    ).astype(BF16)
    gate_vals = jax.nn.sigmoid(
        jnp.einsum("rjd,de->rje", normed, weights[:, 4 * width : 5 * width], preferred_element_type=F32)
    ).astype(BF16)
    return (left_vals, right_vals, gate_vals)


def to_channels(left_vals, right_vals):
    return (
        lax.all_to_all(left_vals, "row", split_axis=0, concat_axis=1, tiled=True),
        lax.all_to_all(right_vals, "row", split_axis=0, concat_axis=1, tiled=True),
    )


def finish(pair_act, triangle, gate_vals, weights_out):
    tri_normed = layer_norm(triangle.astype(F32), 0).astype(BF16)
    delta_vals = jnp.einsum("crj,cd->rjd", tri_normed, weights_out, preferred_element_type=F32)
    delta_vals = delta_vals * gate_vals.astype(F32)
    return (pair_act.astype(F32) + delta_vals).astype(BF16)


def split_rows(pair_act, in_weights, out_weights, chain_lengths):
    row_tile = pair_act.shape[0]
    col_tile = pair_act.shape[1]
    total_rows = row_tile * lax.axis_size("row")
    count_valid = total_rows - chain_lengths[chain_lengths.shape[0] - 1]
    row_first = lax.axis_index("row") * row_tile
    col_first = lax.axis_index("col") * col_tile
    row_valid = (row_first + jnp.arange(row_tile, dtype=jnp.int32) < count_valid).astype(F32)
    col_valid = (col_first + jnp.arange(col_tile, dtype=jnp.int32) < count_valid).astype(F32)
    pair_mask = row_valid[:, None] * col_valid[None, :]
    left_vals, right_vals, gate_vals = project(pair_act, in_weights[0], pair_mask)
    left_chan, right_chan = to_channels(left_vals, right_vals)
    left_rows = lax.all_to_all(left_chan, "col", split_axis=1, concat_axis=2, tiled=True)
    summed = jnp.einsum(
        "cik,cjk->cij",
        left_rows,
        lax.all_gather(right_chan, "col", axis=2, tiled=True),
        preferred_element_type=F32,
    )
    triangle = lax.all_to_all(
        lax.all_to_all(summed.astype(BF16), "col", split_axis=2, concat_axis=1, tiled=True),
        "row",
        split_axis=1,
        concat_axis=0,
        tiled=True,
    )
    first_pass = finish(pair_act, triangle, gate_vals, out_weights[0])
    left_vals, right_vals, gate_vals = project(first_pass, in_weights[1], pair_mask)
    left_chan, right_chan = to_channels(left_vals, right_vals)
    summed_in = jnp.einsum(
        "cki,ckj->cij",
        lax.all_gather(left_chan, "col", axis=2, tiled=True),
        right_chan,
        preferred_element_type=F32,
    ).astype(BF16)
    triangle_in = lax.all_to_all(summed_in, "row", split_axis=1, concat_axis=0, tiled=True)
    return finish(first_pass, triangle_in, gate_vals, out_weights[1])


def solution(mesh):
    n_parts, n_row, n_col = (mesh.shape[axis] for axis in ("parts", "row", "col"))

    def by_rows(pair_act, in_weights, out_weights, chain_lengths):
        in_specs = (P(("parts", "row"), "col", None), P(), P(), P("parts"))
        return jax.shard_map(
            split_rows, mesh=mesh, in_specs=in_specs, out_specs=in_specs[0], check_vma=False
        )(pair_act, in_weights, out_weights, chain_lengths)

    def by_channels(pair_act, in_weights, out_weights, chain_lengths):
        halves = jax.sharding.Mesh(
            mesh.devices.reshape(n_parts, 2, n_row // 2, n_col), ("parts", "half", "row", "col")
        )
        in_specs = (P(("parts", "half", "row"), "col", None), P(), P(), P("parts"))
        return jax.shard_map(
            functools.partial(split_channels, 2, n_row // 2, n_col),
            mesh=halves, in_specs=in_specs, out_specs=in_specs[0], check_vma=False,
        )(pair_act, in_weights, out_weights, chain_lengths)

    def program(pair_act, in_weights, out_weights, chain_lengths):
        fits = n_row % 2 == 0 and pair_act.shape[2] % (n_row * n_col) == 0
        form = by_channels if fits else by_rows
        return form(pair_act, in_weights, out_weights, chain_lengths)

    return program
```

time: 112 us -> 127 us (1.13)
  waiting for transfers between devices: 0 us -> 18.5 us
  blocking collectives: 99.9 us -> 92 us
  starting transfers between devices: 0 us -> 4.04 us
    ppermute x0 -> x1, waiting for transfers between devices: none -> 18.5 us  [split_channels(): other = lax.ppermute(pair_act, 'half', [(0, 1), (1, 0)])]
    all_to_all x4 -> x5, blocking collectives: 99.9 us -> 92 us  [exchange(): return lax.all_to_all(array, axes, split_axis=0, concat_axis=0, tiled=True)]
    ppermute x0 -> x1, starting transfers between devices: none -> 4.04 us  [split_channels(): other = lax.ppermute(pair_act, 'half', [(0, 1), (1, 0)])]
    unnamed x12 -> x10, local copies, waits for them, and re-layouts: 3.33 us -> 2.68 us
    pallas_call x5 -> x6, Pallas kernels: 8.34 us -> 8.42 us  [call(): pl.pallas_call(kernel, name=name, out_shape=out_shape, in_specs=in_specs,...]
  transfers between devices with their start and end apart: 0 -> 1, of which waited for: 0 -> 1; matrix products, arithmetic and copies ran while one was open for 0% -> 0% of each run, Pallas kernels for 0% -> 2%
where the time goes in v3:
time: 127 us; the launch traced here: 126 us
  blocking collectives  92 us (72%)
  waiting for transfers between devices  18.5 us (15%)
  Pallas kernels  8.42 us (7%)
  starting transfers between devices  4.04 us (3%)
  local copies, waits for them, and re-layouts  2.68 us (2%)
    all_to_all x5, blocking collectives, exchange(): return lax.all_to_all(array, axes, split_axis=0, concat_axis=0, tiled=True)  92 us
    ppermute x1, waiting for transfers between devices, split_channels(): other = lax.ppermute(pair_act, 'half', [(0, 1), (1, 0)])  18.5 us
    pallas_call x6, Pallas kernels, call(): pl.pallas_call(kernel, name=name, out_shape=out_shape, in_specs=in_specs,...  8.42 us
    ppermute x1, starting transfers between devices, split_channels(): other = lax.ppermute(pair_act, 'half', [(0, 1), (1, 0)])  4.04 us
    unnamed x10, local copies, waits for them, and re-layouts  2.68 us
  transfers between devices with their start and end apart: 1, of which 1 were waited for; matrix products, arithmetic and copies ran while one was open for 0% of the time, Pallas kernels for 2%

profile of v3, /device:TPU:0, one launch (start us, length us, event | category | flops | bytes accessed | tf_op | source)
XLA Modules:
  0.0 125.7 jit_solution(3156476706931849225)
XLA Ops:
  0.0 4.0 %collective-permute-start = (bf16[16,128,128]{2,1,0:T(8,128)(2,1)}, bf16[16,128,128]{2,1,0:T(8,128)(2,1)S(1)}, u32[]{:S(2)}, u32[]{:S(2)}) collective-permute-start(bf16[16,128,128]{2,1,0:T(8,128)(2,1)} %pair_ref.1), channel_id=1, source_target_pairs={{0,16},{16,0},{1,17},{17,1},{2,18},{18,2},{3,19},{19,3},{4,20},{20... | collective-permute-start | bytes 1572872 | tf_op jit(solution)/shard_map/ppermute | solution.py:217
  4.0 0.0 copy-start
  4.0 1.0 copy-done
  5.0 0.0 copy-start.3
  5.0 1.0 copy-done.3
  6.1 0.0 copy-start.4
  6.1 0.7 copy-done.4
  6.7 0.0 copy-start.1
  6.7 2.1 %project.1 = (bf16[16,2,8,16,128]{4,3,2,1,0:T(8,128)(2,1)S(1)}, bf16[16,128,128]{2,1,0:T(8,128)(2,1)S(1)}, bf16[16,128,128]{2,1,0:T(8,128)(2,1)S(1)}, f32[16,128]{1,0:T(8,128)S(1)}, f32[16,128]{1,0:T(8,128)S(1)}) custom-call(s32[8]{0:T(128)S(1)} %copy-done.4, bf16[16,128,128]{2,1,0:T(8,128)(2,1)S(1)} %copy-done.3, bf16[2,128,640]{2,1,0:T(8,128)(2,1)S(1)} %copy-done), custom_call_target="tpu_custom_call" | custom-call | flops 335544320 | bytes 2097152 | tf_op jit(solution)/shard_map/project/pallas_call | solution.py:182
  8.9 18.5 %collective-permute-done.pair_ref = bf16[16,128,128]{2,1,0:T(8,128)(2,1)S(1)} collective-permute-done((bf16[16,128,128]{2,1,0:T(8,128)(2,1)}, bf16[16,128,128]{2,1,0:T(8,128)(2,1)S(1)}, u32[]{:S(2)}, u32[]{:S(2)}) %collective-permute-start) | collective-permute-done | bytes 524320 | tf_op jit(solution)/shard_map/ppermute | solution.py:217
  27.4 0.0 copy-done.1
  27.4 0.8 project_right.1
  28.3 13.1 %all_to_all.25 = bf16[16,1,8,16,128]{4,3,2,1,0:T(8,128)(2,1)S(1)} all-to-all(bf16[16,1,8,16,128]{4,3,2,1,0:T(8,128)(2,1)S(1)} %project_right.1), channel_id=1, replica_groups=mesh['parts'=1,'half'=2,'row'=8,'col'=2] {'row','col'}, dimensions={0} | all-to-all | bytes 1048576 | tf_op jit(solution)/shard_map/all_to_all | solution.py:208
  41.3 17.6 %all_to_all.26 = bf16[16,2,8,16,128]{4,3,2,1,0:T(8,128)(2,1)S(1)} all-to-all(bf16[16,2,8,16,128]{4,3,2,1,0:T(8,128)(2,1)S(1)} %get-tuple-element.13), channel_id=1, replica_groups=mesh['parts'=1,'half'=2,'row'=8,'col'=2] {'row','col'}, dimensions={0} | all-to-all | bytes 2097152 | tf_op jit(solution)/shard_map/all_to_all | solution.py:208
  59.0 0.5 outgoing.1
  59.4 0.0 copy-start.2
  59.5 12.1 %all_to_all.27 = bf16[16,8,16,128]{3,2,1,0:T(8,128)(2,1)S(1)} all-to-all(bf16[16,8,16,128]{3,2,1,0:T(8,128)(2,1)S(1)} %bitcast.13), channel_id=1, replica_groups=mesh['parts'=1,'half'=2,'row'=8,'col'=2] {'row','col'}, dimensions={0} | all-to-all | bytes 1048576 | tf_op jit(solution)/shard_map/all_to_all | solution.py:208
  71.6 0.0 copy-done.2
  71.6 3.1 %finish_project.1 = (bf16[32,2,4,16,128]{4,3,2,1,0:T(8,128)(2,1)S(1)}, bf16[16,128,128]{2,1,0:T(8,128)(2,1)S(1)}, bf16[16,128,128]{2,1,0:T(8,128)(2,1)S(1)}) custom-call(bf16[128,16,128]{2,1,0:T(8,128)(2,1)S(1)} %bitcast.10, bf16[16,128,128]{2,1,0:T(8,128)(2,1)S(1)} %get-tuple-element.15.gate_in_ref, ...), custom_call_target="tpu_custom_call" | custom-call | flops 402653184 | bytes 2097152 | tf_op jit(solution)/shard_map/finish_project/pallas_call | solution.py:182
  74.7 30.8 %all_to_all.28 = bf16[32,2,4,16,128]{4,3,2,1,0:T(8,128)(2,1)S(1)} all-to-all(bf16[32,2,4,16,128]{4,3,2,1,0:T(8,128)(2,1)S(1)} %get-tuple-element.18), channel_id=1, replica_groups=mesh['parts'=1,'half'=2,'row'=8,'col'=2] {'half','row','col'}, dimensions={0} | all-to-all | bytes 2097152 | tf_op jit(solution)/shard_map/all_to_all | solution.py:208
  105.5 0.3 incoming.1
  105.8 18.4 %all_to_all.29 = bf16[32,4,16,128]{3,2,1,0:T(8,128)(2,1)S(1)} all-to-all(bf16[32,4,16,128]{3,2,1,0:T(8,128)(2,1)S(1)} %bitcast.9), channel_id=1, replica_groups=mesh['parts'=1,'half'=2,'row'=8,'col'=2] {'half','row','col'}, dimensions={0} | all-to-all | bytes 1048576 | tf_op jit(solution)/shard_map/all_to_all | solution.py:208
  124.2 1.5 %finish.1 = bf16[16,128,128]{2,1,0:T(8,128)(2,1)} custom-call(bf16[128,16,128]{2,1,0:T(8,128)(2,1)S(1)} %bitcast.11, bf16[16,128,128]{2,1,0:T(8,128)(2,1)S(1)} %get-tuple-element.19.gate_ref, bf16[16,128,128]{2,1,0:T(8,128)(2,1)S(1)} %get-tuple-element.20.pair_t_ref, bf16[2,128,128]{2,1,0:T(8,128)(2,1)S(1)} %copy-done.2), custom_call_target="tpu_custom_call" | custom-call | flops 67108864 | bytes 2097152 | tf_op jit(solution)/shard_map/finish/pallas_call | solution.py:182
Async XLA Ops:
  0.0 27.4 %collective-permute-start = (bf16[16,128,128]{2,1,0:T(8,128)(2,1)}, bf16[16,128,128]{2,1,0:T(8,128)(2,1)S(1)}, u32[]{:S(2)}, u32[]{:S(2)}) collective-permute-start(bf16[16,128,128]{2,1,0:T(8,128)(2,1)} %pair_ref.1), channel_id=1, source_target_pairs={{0,16},{16,0},{1,17},{17,1},{2,18},{18,2},{3,19},{19,3},{4,20},{20... | collective-permute-start | bytes 1572872 | tf_op jit(solution)/shard_map/ppermute | solution.py:217
  4.0 1.0 copy-start
  5.0 1.0 copy-start.3
  6.1 0.7 copy-start.4
  6.7 20.7 %copy-start.1 = (bf16[2,128,640]{2,1,0:T(8,128)(2,1)S(1)}, bf16[2,128,640]{2,1,0:T(8,128)(2,1)}, u32[]{:S(2)}) copy-start(bf16[2,128,640]{2,1,0:T(8,128)(2,1)} %weights_ref.5) | copy-start | bytes 983044
  59.4 12.1 %copy-start.2 = (bf16[2,128,128]{2,1,0:T(8,128)(2,1)S(1)}, bf16[2,128,128]{2,1,0:T(8,128)(2,1)}, u32[]{:S(2)}) copy-start(bf16[2,128,128]{2,1,0:T(8,128)(2,1)} %wo_ref.3) | copy-start | bytes 196612

commit v4 on v2

--- a/solution.py
+++ b/solution.py
@@ -1,4 +1,5 @@
 import functools
+import itertools
 
 import jax
 import jax.numpy as jnp
@@ -11,6 +12,10 @@
 F32 = jnp.float32
 BF16 = jnp.bfloat16
 VMEM_LIMIT = 32 * 1024 * 1024
+FIRST_VMEM_LIMIT = 56 * 1024 * 1024
+ROW_AXES = ("row_a", "row_b", "row_c", "row_d")
+SIDES_ORDER = ("col", "row_d", "row_c", "row_a", "row_b")
+TRIANGLE_ORDER = ("col", "row_c", "row_b", "row_d", "row_a")
 
 
 def layer_norm(values, along_axis):
@@ -28,18 +33,14 @@
     return jnp.dot(lhs, rhs, preferred_element_type=F32)
 
 
-def mask_of(limits, first, group, cols):
-    lane = lax.broadcasted_iota(jnp.int32, (1, cols), 1)
-    col_valid = lane < limits[1]
-    parts = [
-        jnp.where(jnp.logical_and(col_valid, first + g < limits[0]), 1.0, 0.0) for g in range(group)
-    ]
-    return jnp.concatenate(parts, axis=1).astype(F32)
-
-
-def limits_of(lengths_ref, rows, cols):
-    valid = rows * lax.axis_size("row") - lengths_ref[lengths_ref.shape[0] - 1]
-    return valid - lax.axis_index("row") * rows, valid - lax.axis_index("col") * cols
+def store_mask(ref, row_limit, col_limit):
+    row = lax.broadcasted_iota(jnp.int32, ref.shape, 0)
+    col = lax.broadcasted_iota(jnp.int32, ref.shape, 1)
+    ref[...] = jnp.where(jnp.logical_and(row < row_limit, col < col_limit), 1.0, 0.0).astype(F32)
+
+
+def load_mask(ref, first, group):
+    return jnp.concatenate([ref[first + g : first + g + 1, :] for g in range(group)], axis=1)
 
 
 def store_rows(ref, first, group, vals):
@@ -63,37 +64,41 @@
     store_rows(gate_ref, first, group, gate.astype(BF16))
 
 
-def send_channels(left_scr, right_scr, send_ref):
-    rows, width, cols = left_scr.shape
-    group, _, per = send_ref.shape[:3]
+def send_channels(blocks, left_scr, right_scr, send_ref):
+    per = send_ref.shape[2]
     for side, scr in enumerate((left_scr, right_scr)):
-        send_ref[:, side] = jnp.swapaxes(scr[...], 0, 1).reshape(group, per, rows, cols)
+        swapped = jnp.swapaxes(scr[...], 0, 1)
+        for place, block in enumerate(blocks):
+            send_ref[place, side] = swapped[block * per : (block + 1) * per]
 
 
 def first_kernel(
-    lengths_ref, pair_hbm, weights_hbm, send_ref, gate_ref, pair_t_ref,
-    left_scr, right_scr, wt_scr, pair_scr, weights_scr, sems,
+    blocks, lengths_hbm, pair_hbm, weights_hbm, send_ref, gate_ref, pair_t_ref, mask_ref,
+    left_scr, right_scr, wt_scr, lengths_scr, pair_scr, weights_scr, sems,
 ):
     rows, cols, width = pair_scr.shape
     group = 2
-    copies = [
+    fetches = [
         pltpu.make_async_copy(weights_hbm.at[0], weights_scr, sems.at[0]),
         pltpu.make_async_copy(pair_hbm, pair_scr, sems.at[1]),
+        pltpu.make_async_copy(lengths_hbm, lengths_scr, sems.at[2]),
     ]
-    for copy in copies:
-        copy.start()
-    limits = limits_of(lengths_ref, rows, cols)
-    copies[0].wait()
+    for fetch in fetches:
+        fetch.start()
+    for fetch in fetches:
+        fetch.wait()
+    valid = rows * lax.axis_size(ROW_AXES) - lengths_scr[lengths_scr.shape[0] - 1]
+    row_first = functools.reduce(lambda at, axis: at * lax.axis_size(axis) + lax.axis_index(axis), ROW_AXES, 0)
+    store_mask(mask_ref, valid - row_first * rows, valid - lax.axis_index("col") * cols)
     wt_scr[...] = weights_scr[...].T
-    copies[1].wait()
     for first in range(0, rows, group):
-        blocks = jnp.concatenate([pair_scr[first + g].T for g in range(group)], axis=1)
-        store_rows(pair_t_ref, first, group, blocks)
+        pair = jnp.concatenate([pair_scr[first + g].T for g in range(group)], axis=1)
+        store_rows(pair_t_ref, first, group, pair)
         project_rows(
-            first, group, blocks.astype(F32), mask_of(limits, first, group, cols),
+            first, group, pair.astype(F32), load_mask(mask_ref, first, group),
             wt_scr, left_scr, right_scr, gate_ref,
         )
-    send_channels(left_scr, right_scr, send_ref)
+    send_channels(blocks, left_scr, right_scr, send_ref)
 
 
 def finish_rows(first, group, tri_scr, wo_t, gate_ref, pair_t_ref):
@@ -104,12 +109,11 @@
 
 
 def middle_kernel(
-    lengths_ref, tri_ref, gate_in_ref, pair_t_in_ref, wo_ref, weights_ref,
+    blocks, tri_ref, gate_in_ref, pair_t_in_ref, mask_ref, wo_ref, weights_ref,
     send_ref, gate_ref, pair_t_ref, left_scr, right_scr, wt_scr, tri_scr,
 ):
     width, rows, cols = tri_ref.shape
     group = 2
-    limits = limits_of(lengths_ref, rows, cols)
     wt_scr[...] = weights_ref[1].T
     wo_t = wo_ref[0].T
     tri_scr[...] = jnp.swapaxes(tri_ref[...], 0, 1)
@@ -117,10 +121,10 @@
         passed = finish_rows(first, group, tri_scr, wo_t, gate_in_ref, pair_t_in_ref)
         store_rows(pair_t_ref, first, group, passed)
         project_rows(
-            first, group, passed.astype(F32), mask_of(limits, first, group, cols),
+            first, group, passed.astype(F32), load_mask(mask_ref, first, group),
             wt_scr, left_scr, right_scr, gate_ref,
         )
-    send_channels(left_scr, right_scr, send_ref)
+    send_channels(blocks, left_scr, right_scr, send_ref)
 
 
 def last_kernel(tri_ref, gate_ref, pair_t_ref, wo_ref, out_ref, tri_scr):
@@ -134,22 +138,23 @@
             out_ref[first + g] = passed[:, g * cols : (g + 1) * cols].T
 
 
-def triangle_kernel(incoming, recv_ref, out_ref):
-    n_row, n_col, _, per, rows, cols = recv_ref.shape
+def triangle_kernel(incoming, places, out_places, recv_ref, out_ref):
+    _, _, per, rows, cols = recv_ref.shape
     for c in range(per):
         left, right = (
             jnp.concatenate(
-                [recv_ref[:, x, side, c].reshape(n_row * rows, cols) for x in range(n_col)], axis=1
+                [jnp.concatenate([recv_ref[p, side, c] for p in column], axis=0) for column in places], axis=1
             )
             for side in (0, 1)
         )
         dims = (((0,), (0,)), ((), ())) if incoming else (((1,), (1,)), ((), ()))
         tri = lax.dot_general(left, right, dims, preferred_element_type=F32).astype(BF16)
-        for x in range(n_col):
-            out_ref[:, x, c] = tri[:, x * cols : (x + 1) * cols].reshape(n_row, rows, cols)
-
-
-def call(kernel, name, out_shape, scratch, in_specs, flops, *args):
+        for x, column in enumerate(out_places):
+            for r, p in enumerate(column):
+                out_ref[p, c] = tri[r * rows : (r + 1) * rows, x * cols : (x + 1) * cols]
+
+
+def call(kernel, name, out_shape, scratch, in_specs, flops, *args, vmem=VMEM_LIMIT):
     return pl.pallas_call(
         kernel,
         name=name,
@@ -157,53 +162,67 @@
         in_specs=in_specs,
         out_specs=jax.tree.map(lambda _: pl.BlockSpec(memory_space=pltpu.VMEM), out_shape),
         scratch_shapes=scratch,
-        compiler_params=pltpu.CompilerParams(vmem_limit_bytes=VMEM_LIMIT),
+        compiler_params=pltpu.CompilerParams(vmem_limit_bytes=vmem),
         cost_estimate=pl.CostEstimate(flops=flops, bytes_accessed=2 << 20, transcendentals=0),
     )(*args)
 
 
 VM = pl.BlockSpec(memory_space=pltpu.VMEM)
-SM = pl.BlockSpec(memory_space=pltpu.SMEM)
 HBM = pl.BlockSpec(memory_space=pltpu.HBM)
 
 
-def split_channels(n_row, n_col, pair_act, in_weights, out_weights, chain_lengths):
+def places_of(sizes, order):
+    places = {}
+    for place, index in enumerate(itertools.product(*(range(sizes[axis]) for axis in order))):
+        at = dict(zip(order, index))
+        row = 0
+        for axis in ROW_AXES:
+            row = row * sizes[axis] + at[axis]
+        places[at["col"], row] = place
+    n_col, n_row = sizes["col"], len(places) // sizes["col"]
+    return [[places[x, r] for r in range(n_row)] for x in range(n_col)]
+
+
+def split_channels(sizes, pair_act, in_weights, out_weights, chain_lengths):
     rows, cols, width = pair_act.shape
-    group = n_row * n_col
+    places, out_places = places_of(sizes, SIDES_ORDER), places_of(sizes, TRIANGLE_ORDER)
+    group = len(places) * len(places[0])
     per = width // group
-    axes = ("row", "col")
+    owner = {p: q for col, out_col in zip(places, out_places) for p, q in zip(col, out_col)}
+    blocks = [owner[p] for p in range(group)]
+
     send_shape = jax.ShapeDtypeStruct((group, 2, per, rows, cols), BF16)
     block_shape = jax.ShapeDtypeStruct((rows, width, cols), BF16)
-    tri_shape = jax.ShapeDtypeStruct((n_row, n_col, per, rows, cols), BF16)
+    tri_shape = jax.ShapeDtypeStruct((group, per, rows, cols), BF16)
     scr = pltpu.VMEM((rows, width, cols), BF16)
     wt_scr = pltpu.VMEM((5 * width, width), BF16)
     flops_in = 2 * rows * cols * width * 5 * width
     flops_out = 2 * rows * cols * width * width
-    flops_tri = 2 * per * (n_row * rows) ** 2 * n_col * cols
-
-    def exchange(array):
-        return lax.all_to_all(array, axes, split_axis=0, concat_axis=0, tiled=True)
+    flops_tri = 2 * group * rows * cols * width * rows * len(places[0])
+
+    def exchange(array, order):
+        return lax.all_to_all(array, order, split_axis=0, concat_axis=0, tiled=True)
 
     def triangle(send, incoming):
-        recv = exchange(send).reshape((n_row, n_col) + send.shape[1:])
-        tri = call(
-            functools.partial(triangle_kernel, incoming), "triangle", tri_shape, [], [VM], flops_tri, recv
-        )
-        return exchange(tri.reshape((group,) + tri.shape[2:])).reshape(width, rows, cols)
-
-    send, gate, pair_t = call(
-        first_kernel, "project", (send_shape, block_shape, block_shape),
+        kernel = functools.partial(triangle_kernel, incoming, places, out_places)
+        recv = exchange(send, SIDES_ORDER)
+        tri = call(kernel, "triangle", tri_shape, [], [VM], flops_tri, recv)
+        return exchange(tri, TRIANGLE_ORDER).reshape(width, rows, cols)
+
+    send, gate, pair_t, mask = call(
+        functools.partial(first_kernel, blocks), "project",
+        (send_shape, block_shape, block_shape, jax.ShapeDtypeStruct((rows, cols), F32)),
         [
-            scr, scr, wt_scr, pltpu.VMEM(pair_act.shape, BF16),
-            pltpu.VMEM(in_weights.shape[1:], BF16), pltpu.SemaphoreType.DMA((2,)),
+            scr, scr, wt_scr, pltpu.SMEM(chain_lengths.shape, jnp.int32), pltpu.VMEM(pair_act.shape, BF16),
+            pltpu.VMEM(in_weights.shape[1:], BF16), pltpu.SemaphoreType.DMA((3,)),
         ],
-        [SM, HBM, HBM], flops_in, chain_lengths, pair_act, in_weights,
+        [HBM, HBM, HBM], flops_in, chain_lengths, pair_act, in_weights, vmem=FIRST_VMEM_LIMIT,
     )
     tri = triangle(send, False)
     send, gate, pair_t = call(
-        middle_kernel, "finish_project", (send_shape, block_shape, block_shape), [scr, scr, wt_scr, scr],
-        [SM, VM, VM, VM, VM, VM], flops_in + flops_out,
-        chain_lengths, tri, gate, pair_t, out_weights, in_weights,
+        functools.partial(middle_kernel, blocks), "finish_project", (send_shape, block_shape, block_shape),
+        [scr, scr, wt_scr, scr], [VM] * 6, flops_in + flops_out,
+        tri, gate, pair_t, mask, out_weights, in_weights,
     )
     tri = triangle(send, True)
     return call(
@@ -280,15 +299,27 @@
 
 
 def solution(mesh):
-    n_row, n_col = mesh.shape["row"], mesh.shape["col"]
-
-    def per_device(pair_act, in_weights, out_weights, chain_lengths):
-        if pair_act.shape[2] % (n_row * n_col) == 0:
-            return split_channels(n_row, n_col, pair_act, in_weights, out_weights, chain_lengths)
-        return split_rows(pair_act, in_weights, out_weights, chain_lengths)
-
-    in_specs = (P(("parts", "row"), "col", None), P(), P(), P("parts"))
-    out_specs = P(("parts", "row"), "col", None)
-    return jax.shard_map(
-        per_device, mesh=mesh, in_specs=in_specs, out_specs=out_specs, check_vma=False
-    )
+    n_parts, n_row, n_col = (mesh.shape[axis] for axis in ("parts", "row", "col"))
+
+    def by_rows(*args):
+        in_specs = (P(("parts", "row"), "col", None), P(), P(), P("parts"))
+        return jax.shard_map(
+            split_rows, mesh=mesh, in_specs=in_specs, out_specs=in_specs[0], check_vma=False
+        )(*args)
+
+    def by_channels(*args):
+        shape = (n_parts, n_row // 8, 2, 2, 2, n_col)
+        axes = ("parts",) + ROW_AXES + ("col",)
+        fine = jax.sharding.Mesh(mesh.devices.reshape(shape), axes)
+        in_specs = (P(axes[:-1], "col", None), P(), P(), P("parts"))
+        return jax.shard_map(
+            functools.partial(split_channels, dict(zip(axes, shape))),
+            mesh=fine, in_specs=in_specs, out_specs=in_specs[0], check_vma=False,
+        )(*args)
+
+    def program(pair_act, in_weights, out_weights, chain_lengths):
+        fits = n_row % 8 == 0 and pair_act.shape[2] % (n_row * n_col) == 0
+        form = by_channels if fits else by_rows
+        return form(pair_act, in_weights, out_weights, chain_lengths)
+
+    return program

time: 112 us -> 108 us (0.964)
  local copies, waits for them, and re-layouts: 3.33 us -> 0.02 us
  blocking collectives: 99.9 us -> 97.9 us
    unnamed x12 -> x10, local copies, waits for them, and re-layouts: 3.33 us -> 0.02 us
    all_to_all x4, blocking collectives: 99.9 us -> 97.9 us  [exchange(): return lax.all_to_all(array, order, split_axis=0, concat_axis=0, tiled=True)]
where the time goes in v4:
time: 108 us; the launch traced here: 107 us
  blocking collectives  97.9 us (91%)
  Pallas kernels  9.34 us (9%)
    all_to_all x4, blocking collectives, exchange(): return lax.all_to_all(array, order, split_axis=0, concat_axis=0, tiled=True)  97.9 us
    pallas_call x5, Pallas kernels, call(): pl.pallas_call(kernel, name=name, out_shape=out_shape, in_specs=in_specs,...  9.34 us

profile of v4, /device:TPU:0, one launch (start us, length us, event | category | flops | bytes accessed | tf_op | source)
XLA Modules:
  0.0 107.3 jit_solution(1507119270941563043)
XLA Ops:
  0.0 4.1 %project.1 = (bf16[32,2,4,16,128]{4,3,2,1,0:T(8,128)(2,1)}, bf16[16,128,128]{2,1,0:T(8,128)(2,1)}, bf16[16,128,128]{2,1,0:T(8,128)(2,1)}, f32[16,128]{1,0:T(8,128)}) custom-call(s32[8]{0:T(128)} %lengths_hbm.1, bf16[16,128,128]{2,1,0:T(8,128)(2,1)} %pair_hbm.1, bf16[2,128,640]{2,1,0:T(8,128)(2,1)} %weights_ref.1), custom_call_target="tpu_custom_call" | custom-call | flops 335544320 | bytes 2097152 | tf_op jit(solution)/shard_map/project/pallas_call | solution.py:158
  4.1 34.1 %all_to_all.20.recv_ref = bf16[32,2,4,16,128]{4,3,2,1,0:T(8,128)(2,1)S(1)} all-to-all(bf16[32,2,4,16,128]{4,3,2,1,0:T(8,128)(2,1)} %get-tuple-element.12), channel_id=1, replica_groups=mesh['parts'=1,'row_a'=2,'row_b'=2,'row_c'=2,'row_d'=2,'col'=2] {'col','..., dimensions={0} | all-to-all | bytes 2097152 | tf_op jit(solution)/shard_map/all_to_all | solution.py:204
  38.2 0.0 copy-start.2
  38.2 0.0 copy-start.3
  38.2 0.0 copy-start.4
  38.2 0.3 triangle.2
  38.5 0.0 copy-start
  38.5 0.0 copy-start.1
  38.6 17.1 %all_to_all.21 = bf16[32,4,16,128]{3,2,1,0:T(8,128)(2,1)S(1)} all-to-all(bf16[32,4,16,128]{3,2,1,0:T(8,128)(2,1)S(1)} %triangle.2), channel_id=1, replica_groups=mesh['parts'=1,'row_a'=2,'row_b'=2,'row_c'=2,'row_d'=2,'col'=2] {'col','..., dimensions={0} | all-to-all | bytes 1048576 | tf_op jit(solution)/shard_map/all_to_all | solution.py:204
  55.7 0.0 copy-done.2
  55.7 0.0 copy-done.3
  55.7 0.0 copy-done.4
  55.7 0.0 copy-done
  55.7 0.0 copy-done.1
  55.7 3.1 %finish_project.1 = (bf16[32,2,4,16,128]{4,3,2,1,0:T(8,128)(2,1)S(1)}, bf16[16,128,128]{2,1,0:T(8,128)(2,1)S(1)}, bf16[16,128,128]{2,1,0:T(8,128)(2,1)S(1)}) custom-call(bf16[128,16,128]{2,1,0:T(8,128)(2,1)S(1)} %bitcast.2, bf16[16,128,128]{2,1,0:T(8,128)(2,1)S(1)} %copy-done, bf16[16,128,128]{2,1,0:T(8,128)(2,1)S(1)} %copy-done.1, f32[16,128]{1,0:T(8,128)S(1)} %copy-done.4, ...), custom_call_target="tpu_custom_call" | custom-call | flops 402653184 | bytes 2097152 | tf_op jit(solution)/shard_map/finish_project/pallas_call | solution.py:158
  58.8 29.5 %all_to_all.22.recv_ref = bf16[32,2,4,16,128]{4,3,2,1,0:T(8,128)(2,1)S(1)} all-to-all(bf16[32,2,4,16,128]{4,3,2,1,0:T(8,128)(2,1)S(1)} %get-tuple-element.16), channel_id=1, replica_groups=mesh['parts'=1,'row_a'=2,'row_b'=2,'row_c'=2,'row_d'=2,'col'=2] {'col','..., dimensions={0} | all-to-all | bytes 2097152 | tf_op jit(solution)/shard_map/all_to_all | solution.py:204
  88.3 0.3 triangle.3
  88.7 17.1 %all_to_all.23 = bf16[32,4,16,128]{3,2,1,0:T(8,128)(2,1)S(1)} all-to-all(bf16[32,4,16,128]{3,2,1,0:T(8,128)(2,1)S(1)} %triangle.3), channel_id=1, replica_groups=mesh['parts'=1,'row_a'=2,'row_b'=2,'row_c'=2,'row_d'=2,'col'=2] {'col','..., dimensions={0} | all-to-all | bytes 1048576 | tf_op jit(solution)/shard_map/all_to_all | solution.py:204
  105.8 1.5 %finish.1 = bf16[16,128,128]{2,1,0:T(8,128)(2,1)} custom-call(bf16[128,16,128]{2,1,0:T(8,128)(2,1)S(1)} %bitcast.3, bf16[16,128,128]{2,1,0:T(8,128)(2,1)S(1)} %get-tuple-element.17.gate_ref, bf16[16,128,128]{2,1,0:T(8,128)(2,1)S(1)} %get-tuple-element.18.pair_t_ref, bf16[2,128,128]{2,1,0:T(8,128)(2,1)S(1)} %copy-done.3), custom_call_target="tpu_custom_call" | custom-call | flops 67108864 | bytes 2097152 | tf_op jit(solution)/shard_map/finish/pallas_call | solution.py:158
Async XLA Ops:
  38.2 17.5 %copy-start.2 = (bf16[2,128,640]{2,1,0:T(8,128)(2,1)S(1)}, bf16[2,128,640]{2,1,0:T(8,128)(2,1)}, u32[]{:S(2)}) copy-start(bf16[2,128,640]{2,1,0:T(8,128)(2,1)} %weights_ref.1) | copy-start | bytes 983044
  38.2 17.5 %copy-start.3 = (bf16[2,128,128]{2,1,0:T(8,128)(2,1)S(1)}, bf16[2,128,128]{2,1,0:T(8,128)(2,1)}, u32[]{:S(2)}) copy-start(bf16[2,128,128]{2,1,0:T(8,128)(2,1)} %wo_ref.3) | copy-start | bytes 196612
  38.2 17.5 %copy-start.4 = (f32[16,128]{1,0:T(8,128)S(1)}, f32[16,128]{1,0:T(8,128)}, u32[]{:S(2)}) copy-start(f32[16,128]{1,0:T(8,128)} %get-tuple-element.15.mask_ref) | copy-start | bytes 24580
  38.5 17.2 %copy-start = (bf16[16,128,128]{2,1,0:T(8,128)(2,1)S(1)}, bf16[16,128,128]{2,1,0:T(8,128)(2,1)}, u32[]{:S(2)}) copy-start(bf16[16,128,128]{2,1,0:T(8,128)(2,1)} %get-tuple-element.13.gate_in_ref) | copy-start | bytes 1572868
  38.5 17.2 %copy-start.1 = (bf16[16,128,128]{2,1,0:T(8,128)(2,1)S(1)}, bf16[16,128,128]{2,1,0:T(8,128)(2,1)}, u32[]{:S(2)}) copy-start(bf16[16,128,128]{2,1,0:T(8,128)(2,1)} %get-tuple-element.14.pair_t_in_ref) | copy-start | bytes 1572868

commit v5 on v4

--- a/solution.py
+++ b/solution.py
@@ -14,8 +14,11 @@
 VMEM_LIMIT = 32 * 1024 * 1024
 FIRST_VMEM_LIMIT = 56 * 1024 * 1024
 ROW_AXES = ("row_a", "row_b", "row_c", "row_d")
+RIGHT_ORDER = ("col", "row_d", "row_a", "row_c", "row_b")
 SIDES_ORDER = ("col", "row_d", "row_c", "row_a", "row_b")
 TRIANGLE_ORDER = ("col", "row_c", "row_b", "row_d", "row_a")
+HALF_ORDER = ("row_c", "col", "row_d", "row_b")
+FLIPS = ((0, 0), (0, 1), (1, 0), (1, 1))
 
 
 def layer_norm(values, along_axis):
@@ -72,9 +75,20 @@
             send_ref[place, side] = swapped[block * per : (block + 1) * per]
 
 
+def half_place(col, row_c, row_b, row_d):
+    at = {"col": col, "row_c": row_c, "row_b": row_b, "row_d": row_d}
+    return functools.reduce(lambda place, axis: 2 * place + at[axis], HALF_ORDER, 0)
+
+
+def flip(axis, by):
+    at = lax.axis_index(axis)
+    return 1 - at if by else at
+
+
 def first_kernel(
-    blocks, lengths_hbm, pair_hbm, weights_hbm, send_ref, gate_ref, pair_t_ref, mask_ref,
-    left_scr, right_scr, wt_scr, lengths_scr, pair_scr, weights_scr, sems,
+    blocks, lengths_hbm, pair_hbm, weights_hbm, right_ref, own_ref, core_ref, z_ref, z_core_ref,
+    gate_ref, pair_t_ref, mask_ref,
+    left_scr, right_scr, wt_scr, lengths_scr, pair_scr, weights_scr, owner_scr, sems,
 ):
     rows, cols, width = pair_scr.shape
     group = 2
@@ -98,7 +112,21 @@
             first, group, pair.astype(F32), load_mask(mask_ref, first, group),
             wt_scr, left_scr, right_scr, gate_ref,
         )
-    send_channels(blocks, left_scr, right_scr, send_ref)
+    per = right_ref.shape[1]
+    swapped = jnp.swapaxes(right_scr[...], 0, 1)
+    for place, block in enumerate(blocks):
+        right_ref[place] = swapped[block * per : (block + 1) * per]
+    owner_scr[...] = jnp.swapaxes(left_scr[...], 0, 1).reshape(owner_scr.shape)
+    for part_ref, (by_z, by_core) in zip((own_ref, core_ref, z_ref, z_core_ref), FLIPS):
+        for x_y in range(4):
+            part_ref[x_y] = owner_scr[half_place(x_y // 2, x_y % 2, flip("row_b", by_z), flip("row_d", by_core))]
+
+
+def regroup_kernel(*refs):
+    for part_ref, (by_y, by_x) in zip(refs[4:], FLIPS):
+        at = flip("col", by_x) * 2 + flip("row_c", by_y)
+        for sender in range(4):
+            part_ref[sender] = refs[sender][at]
 
 
 def finish_rows(first, group, tri_scr, wo_t, gate_ref, pair_t_ref):
@@ -138,7 +166,33 @@
             out_ref[first + g] = passed[:, g * cols : (g + 1) * cols].T
 
 
-def triangle_kernel(incoming, places, out_places, recv_ref, out_ref):
+def outgoing_kernel(places, *refs):
+    left_refs, (right_ref, out_ref) = refs[:4], refs[4:]
+    _, per, rows, cols = right_ref.shape
+    first_col = lax.axis_index("col") == 0
+    deltas = [(z_core, by_y) for z_core in range(4) for by_y in range(2)]
+    for c in range(per):
+        same, across = (
+            jnp.concatenate([left_refs[2 * by_y + by_x][z_core, c] for z_core, by_y in deltas], axis=0)
+            for by_x in (0, 1)
+        )
+        left = jnp.concatenate(
+            [jnp.where(first_col, same, across), jnp.where(first_col, across, same)], axis=1
+        )
+        right = jnp.concatenate(
+            [jnp.concatenate([right_ref[p, c] for p in column], axis=0) for column in places], axis=1
+        )
+        tri = lax.dot_general(
+            left, right, (((1,), (1,)), ((), ())), preferred_element_type=F32
+        ).astype(BF16)
+        for block, (z_core, by_y) in enumerate(deltas):
+            by_z, by_core = FLIPS[z_core]
+            at = flip("row_c", by_y), flip("row_b", by_z), flip("row_d", by_core)
+            for x in range(len(places)):
+                out_ref[half_place(x, *at), c] = tri[block * rows : (block + 1) * rows, x * cols : (x + 1) * cols]
+
+
+def incoming_kernel(places, out_places, recv_ref, out_ref):
     _, _, per, rows, cols = recv_ref.shape
     for c in range(per):
         left, right = (
@@ -147,8 +201,9 @@
             )
             for side in (0, 1)
         )
-        dims = (((0,), (0,)), ((), ())) if incoming else (((1,), (1,)), ((), ()))
-        tri = lax.dot_general(left, right, dims, preferred_element_type=F32).astype(BF16)
+        tri = lax.dot_general(
+            left, right, (((0,), (0,)), ((), ())), preferred_element_type=F32
+        ).astype(BF16)
         for x, column in enumerate(out_places):
             for r, p in enumerate(column):
                 out_ref[p, c] = tri[r * rows : (r + 1) * rows, x * cols : (x + 1) * cols]
@@ -183,50 +238,73 @@
     return [[places[x, r] for r in range(n_row)] for x in range(n_col)]
 
 
+def to_partners(parts, axes):
+    pairs = [[(0, 1), (1, 0)], [(0, 1), (1, 0)], [(0, 3), (1, 2), (2, 1), (3, 0)]]
+    names = (axes[1], axes[0], axes)
+    return [parts[0]] + [lax.ppermute(p, name, pair) for p, name, pair in zip(parts[1:], names, pairs)]
+
+
 def split_channels(sizes, pair_act, in_weights, out_weights, chain_lengths):
     rows, cols, width = pair_act.shape
     places, out_places = places_of(sizes, SIDES_ORDER), places_of(sizes, TRIANGLE_ORDER)
-    group = len(places) * len(places[0])
-    per = width // group
+    n_col, n_row = len(places), len(places[0])
+    group, half_group = n_col * n_row, n_col * n_row // 2
+    per, half_per = width // group, width // half_group
     owner = {p: q for col, out_col in zip(places, out_places) for p, q in zip(col, out_col)}
     blocks = [owner[p] for p in range(group)]
-
-    send_shape = jax.ShapeDtypeStruct((group, 2, per, rows, cols), BF16)
-    block_shape = jax.ShapeDtypeStruct((rows, width, cols), BF16)
-    tri_shape = jax.ShapeDtypeStruct((group, per, rows, cols), BF16)
+    right_places = places_of(sizes, RIGHT_ORDER)
+    half_places = places_of({**sizes, "row_a": 1}, HALF_ORDER + ("row_a",))
+    half_owner = {p: q for col, half_col in zip(right_places, half_places) for p, q in zip(col, half_col * 2)}
+    half_blocks = [half_owner[p] for p in range(group)]
+
+    def shape_of(*dims, dtype=BF16):
+        return jax.ShapeDtypeStruct(dims, dtype)
+
+    block_shape = shape_of(rows, width, cols)
+    part_shape = shape_of(4, half_per, rows, cols)
     scr = pltpu.VMEM((rows, width, cols), BF16)
     wt_scr = pltpu.VMEM((5 * width, width), BF16)
     flops_in = 2 * rows * cols * width * 5 * width
     flops_out = 2 * rows * cols * width * width
-    flops_tri = 2 * group * rows * cols * width * rows * len(places[0])
+    flops_tri = 2 * group * rows * cols * width * rows * n_row
 
     def exchange(array, order):
         return lax.all_to_all(array, order, split_axis=0, concat_axis=0, tiled=True)
 
-    def triangle(send, incoming):
-        kernel = functools.partial(triangle_kernel, incoming, places, out_places)
-        recv = exchange(send, SIDES_ORDER)
-        tri = call(kernel, "triangle", tri_shape, [], [VM], flops_tri, recv)
-        return exchange(tri, TRIANGLE_ORDER).reshape(width, rows, cols)
-
-    send, gate, pair_t, mask = call(
-        functools.partial(first_kernel, blocks), "project",
-        (send_shape, block_shape, block_shape, jax.ShapeDtypeStruct((rows, cols), F32)),
+    right, *left, gate, pair_t, mask = call(
+        functools.partial(first_kernel, half_blocks), "project",
+        (shape_of(group, half_per, rows, cols),) + (part_shape,) * 4
+        + (block_shape, block_shape, shape_of(rows, cols, dtype=F32)),
         [
             scr, scr, wt_scr, pltpu.SMEM(chain_lengths.shape, jnp.int32), pltpu.VMEM(pair_act.shape, BF16),
-            pltpu.VMEM(in_weights.shape[1:], BF16), pltpu.SemaphoreType.DMA((3,)),
+            pltpu.VMEM(in_weights.shape[1:], BF16), pltpu.VMEM((half_group, half_per, rows, cols), BF16),
+            pltpu.SemaphoreType.DMA((3,)),
         ],
         [HBM, HBM, HBM], flops_in, chain_lengths, pair_act, in_weights, vmem=FIRST_VMEM_LIMIT,
     )
-    tri = triangle(send, False)
+    right = exchange(right, RIGHT_ORDER)
+    left = to_partners(left, ("row_b", "row_d"))
+    left = call(regroup_kernel, "regroup", (part_shape,) * 4, [], [VM] * 4, 3000 * flops_out, *left, vmem=4 * 1024 * 1024)
+    left = to_partners(left, ("row_c", "col"))
+    tri = call(
+        functools.partial(outgoing_kernel, right_places), "outgoing", shape_of(half_group, half_per, rows, cols),
+        [], [VM] * 5, flops_tri, *left, right,
+    )
+    tri = exchange(tri, HALF_ORDER).reshape(width, rows, cols)
     send, gate, pair_t = call(
-        functools.partial(middle_kernel, blocks), "finish_project", (send_shape, block_shape, block_shape),
+        functools.partial(middle_kernel, blocks), "finish_project",
+        (shape_of(group, 2, per, rows, cols), block_shape, block_shape),
         [scr, scr, wt_scr, scr], [VM] * 6, flops_in + flops_out,
         tri, gate, pair_t, mask, out_weights, in_weights,
     )
-    tri = triangle(send, True)
+    recv = exchange(send, SIDES_ORDER)
+    tri = call(
+        functools.partial(incoming_kernel, places, out_places), "incoming", shape_of(group, per, rows, cols),
+        [], [VM], flops_tri, recv,
+    )
+    tri = exchange(tri, TRIANGLE_ORDER).reshape(width, rows, cols)
     return call(
-        last_kernel, "finish", jax.ShapeDtypeStruct(pair_act.shape, BF16), [scr],
+        last_kernel, "finish", shape_of(*pair_act.shape), [scr],
         [VM, VM, VM, VM], flops_out, tri, gate, pair_t, out_weights,
     )
 
@@ -318,7 +396,7 @@
         )(*args)
 
     def program(pair_act, in_weights, out_weights, chain_lengths):
-        fits = n_row % 8 == 0 and pair_act.shape[2] % (n_row * n_col) == 0
+        fits = n_row == 16 and n_col == 2 and pair_act.shape[2] % 32 == 0
         form = by_channels if fits else by_rows
         return form(pair_act, in_weights, out_weights, chain_lengths)
 

time: 108 us -> 106 us (0.981)
  blocking collectives: 97.9 us -> 59.1 us
  waiting for transfers between devices: 0 us -> 22.6 us
  starting transfers between devices: 0 us -> 12.9 us
  Pallas kernels: 9.34 us -> 11 us
    all_to_all x4 -> x3, blocking collectives: 97.9 us -> 59.1 us  [exchange(): return lax.all_to_all(array, order, split_axis=0, concat_axis=0, tiled=True)]
    ppermute x0 -> x6, waiting for transfers between devices: none -> 14.3 us  [to_partners(): lax.ppermute(p, name, pair)]
    all_to_all x0 -> x1, waiting for transfers between devices: none -> 8.33 us  [exchange(): return lax.all_to_all(array, order, split_axis=0, concat_axis=0, tiled=True)]
    ppermute x0 -> x6, starting transfers between devices: none -> 6.79 us  [to_partners(): lax.ppermute(p, name, pair)]
    all_to_all x0 -> x1, starting transfers between devices: none -> 6.12 us  [exchange(): return lax.all_to_all(array, order, split_axis=0, concat_axis=0, tiled=True)]
    pallas_call x5 -> x6, Pallas kernels: 9.34 us -> 11 us  [call(): pl.pallas_call(kernel, name=name, out_shape=out_shape, in_specs=in_specs,...]
  transfers between devices with their start and end apart: 0 -> 7, of which waited for: 0 -> 4; matrix products, arithmetic and copies ran while one was open for 0% -> 0% of each run, Pallas kernels for 0% -> 0%
where the time goes in v5:
time: 106 us
  blocking collectives  59.1 us (56%)
  waiting for transfers between devices  22.6 us (21%)
  starting transfers between devices  12.9 us (12%)
  Pallas kernels  11 us (10%)
    all_to_all x3, blocking collectives, exchange(): return lax.all_to_all(array, order, split_axis=0, concat_axis=0, tiled=True)  59.1 us
    ppermute x6, waiting for transfers between devices, to_partners(): lax.ppermute(p, name, pair)  14.3 us
    pallas_call x6, Pallas kernels, call(): pl.pallas_call(kernel, name=name, out_shape=out_shape, in_specs=in_specs,...  11 us
    all_to_all x1, waiting for transfers between devices, exchange(): return lax.all_to_all(array, order, split_axis=0, concat_axis=0, tiled=True)  8.33 us
    ppermute x6, starting transfers between devices, to_partners(): lax.ppermute(p, name, pair)  6.79 us
    all_to_all x1, starting transfers between devices, exchange(): return lax.all_to_all(array, order, split_axis=0, concat_axis=0, tiled=True)  6.12 us
  transfers between devices with their start and end apart: 7, of which 4 were waited for; matrix products, arithmetic and copies ran while one was open for 0% of the time, Pallas kernels for 0%

profile of v5, /device:TPU:0, one launch (start us, length us, event | category | flops | bytes accessed | tf_op | source)
XLA Modules:
  0.0 105.7 jit_solution(15904778412693411166)
XLA Ops:
  0.0 4.2 %project.1 = (bf16[32,8,16,128]{3,2,1,0:T(8,128)(2,1)}, bf16[4,8,16,128]{3,2,1,0:T(8,128)(2,1)}, bf16[4,8,16,128]{3,2,1,0:T(8,128)(2,1)}, bf16[4,8,16,128]{3,2,1...) custom-call(s32[8]{0:T(128)} %lengths_hbm.1, ...), custom_call_target="tpu_custom_call" | custom-call | flops 335544320 | bytes 2097152 | tf_op jit(solution)/shard_map/project/pallas_call | solution.py:213
  4.2 0.5 collective-permute-start
  4.8 2.7 %collective-permute-start.1 = (bf16[4,8,16,128]{3,2,1,0:T(8,128)(2,1)}, bf16[4,8,16,128]{3,2,1,0:T(8,128)(2,1)S(1)}, u32[]{:S(2)}, u32[]{:S(2)}) collective-permute-start(bf16[4,8,16,128]{3,2,1,0:T(8,128)(2,1)} %get-tuple-element.22), channel_id=1, source_target_pairs={{0,8},{8,0},{1,9},{9,1},{2,10},{10,2},{3,11},{11,3},{4,12},{12,4},... | collective-permute-start | bytes 393224 | tf_op jit(solution)/shard_map/ppermute | solution.py:244
  7.4 0.1 collective-permute-start.2
  7.5 6.1 %all-to-all-start = ((bf16[32,8,16,128]{3,2,1,0:T(8,128)(2,1)}), bf16[32,8,16,128]{3,2,1,0:T(8,128)(2,1)}, u32[]{:S(2)}, u32[]{:S(2)}) async-start(bf16[32,8,16,128]{3,2,1,0:T(8,128)(2,1)} %get-tuple-element.28), calls=%async_computation | async-start | bytes 2097152 | tf_op jit(solution)/shard_map/all_to_all | solution.py:272
  13.6 0.0 collective-permute-done.refs_1_
  13.6 0.0 collective-permute-done.1.refs_2_
  13.6 0.6 collective-permute-done.2.refs_3_
  14.3 1.5 %collective-permute-start.3 = (bf16[4,8,16,128]{3,2,1,0:T(8,128)(2,1)S(1)}, bf16[4,8,16,128]{3,2,1,0:T(8,128)(2,1)S(1)}, u32[]{:S(2)}, u32[]{:S(2)}) collective-permute-start(bf16[4,8,16,128]{3,2,1,0:T(8,128)(2,1)S(1)} %get-tuple-element.25), channel_id=1, source_target_pairs={{0,1},{1,0},{2,3},{3,2},{4,5},{5,4},{6,7},{7,6},{8,9},{9,8},{10,11... | collective-permute-start | bytes 393224 | tf_op jit(solution)/shard_map/ppermute | solution.py:244
  15.9 1.5 %collective-permute-start.4 = (bf16[4,8,16,128]{3,2,1,0:T(8,128)(2,1)S(1)}, bf16[4,8,16,128]{3,2,1,0:T(8,128)(2,1)S(1)}, u32[]{:S(2)}, u32[]{:S(2)}) collective-permute-start(bf16[4,8,16,128]{3,2,1,0:T(8,128)(2,1)S(1)} %get-tuple-element.26), channel_id=1, source_target_pairs={{0,4},{4,0},{1,5},{5,1},{2,6},{6,2},{3,7},{7,3},{8,12},{12,8},{9,1... | collective-permute-start | bytes 393224 | tf_op jit(solution)/shard_map/ppermute | solution.py:244
  17.4 0.5 collective-permute-start.5
  17.9 10.3 %collective-permute-done.3.refs_1_ = bf16[4,8,16,128]{3,2,1,0:T(8,128)(2,1)S(1)} collective-permute-done((bf16[4,8,16,128]{3,2,1,0:T(8,128)(2,1)S(1)}, bf16[4,8,16,128]{3,2,1,0:T(8,128)(2,1)S(1)}, u32[]{:S(2)}, u32[]{:S(2)}) %collective-permute-start.3) | collective-permute-done | bytes 131104 | tf_op jit(solution)/shard_map/ppermute | solution.py:244
  28.2 0.0 collective-permute-done.4.refs_2_
  28.2 3.3 %collective-permute-done.5.refs_3_ = bf16[4,8,16,128]{3,2,1,0:T(8,128)(2,1)S(1)} collective-permute-done((bf16[4,8,16,128]{3,2,1,0:T(8,128)(2,1)S(1)}, bf16[4,8,16,128]{3,2,1,0:T(8,128)(2,1)S(1)}, u32[]{:S(2)}, u32[]{:S(2)}) %collective-permute-start.5) | collective-permute-done | bytes 131104 | tf_op jit(solution)/shard_map/ppermute | solution.py:244
  31.5 8.3 %all-to-all-done.refs_4_ = bf16[32,8,16,128]{3,2,1,0:T(8,128)(2,1)} async-done(((bf16[32,8,16,128]{3,2,1,0:T(8,128)(2,1)}), bf16[32,8,16,128]{3,2,1,0:T(8,128)(2,1)}, u32[]{:S(2)}, u32[]{:S(2)}) %all-to-all-start) | async-done | bytes 1048608 | tf_op jit(solution)/shard_map/all_to_all | solution.py:272
  39.8 1.8 %outgoing.1 = bf16[16,8,16,128]{3,2,1,0:T(8,128)(2,1)S(1)} custom-call(bf16[4,8,16,128]{3,2,1,0:T(8,128)(2,1)S(1)} %get-tuple-element.24.refs_0_, bf16[4,8,16,128]{3,2,1,0:T(8,128)(2,1)S(1)} %collective-permute-done.3.refs_1_, bf16[4,8,16,128]{3,2,1,0:T(8,128)(2,1)S(1)} %collective-permute-done.4.refs_2_, ...), custom_call_target="tpu_custom_call" | custom-call | flops 4294967296 | bytes 2097152 | tf_op jit(solution)/shard_map/outgoing/pallas_call | solution.py:213
  41.6 0.0 copy-start
  41.6 0.0 copy-start.1
  41.6 12.0 %all_to_all.20 = bf16[16,8,16,128]{3,2,1,0:T(8,128)(2,1)S(1)} all-to-all(bf16[16,8,16,128]{3,2,1,0:T(8,128)(2,1)S(1)} %outgoing.1), channel_id=1, replica_groups=mesh['parts'=1,'row_a'=2,'row_b'=2,'row_c'=2,'row_d'=2,'col'=2] {'row_c'..., dimensions={0} | all-to-all | bytes 1048576 | tf_op jit(solution)/shard_map/all_to_all | solution.py:272
  53.6 3.1 %finish_project.1 = (bf16[32,2,4,16,128]{4,3,2,1,0:T(8,128)(2,1)S(1)}, bf16[16,128,128]{2,1,0:T(8,128)(2,1)S(1)}, bf16[16,128,128]{2,1,0:T(8,128)(2,1)S(1)}) custom-call(bf16[128,16,128]{2,1,0:T(8,128)(2,1)S(1)} %bitcast.2, bf16[16,128,128]{2,1,0:T(8,128)(2,1)S(1)} %copy-done, bf16[16,128,128]{2,1,0:T(8,128)(2,1)S(1)} %copy-done.1, f32[16,128]{1,0:T(8,128)S(1)} %copy-done.4, ...), custom_call_target="tpu_custom_call" | custom-call | flops 402653184 | bytes 2097152 | tf_op jit(solution)/shard_map/finish_project/pallas_call | solution.py:213
  56.8 29.9 %all_to_all.21.recv_ref = bf16[32,2,4,16,128]{4,3,2,1,0:T(8,128)(2,1)S(1)} all-to-all(bf16[32,2,4,16,128]{4,3,2,1,0:T(8,128)(2,1)S(1)} %get-tuple-element.32), channel_id=1, replica_groups=mesh['parts'=1,'row_a'=2,'row_b'=2,'row_c'=2,'row_d'=2,'col'=2] {'col','..., dimensions={0} | all-to-all | bytes 2097152 | tf_op jit(solution)/shard_map/all_to_all | solution.py:272
  86.7 0.3 incoming.1
  87.1 17.1 %all_to_all.22 = bf16[32,4,16,128]{3,2,1,0:T(8,128)(2,1)S(1)} all-to-all(bf16[32,4,16,128]{3,2,1,0:T(8,128)(2,1)S(1)} %incoming.1), channel_id=1, replica_groups=mesh['parts'=1,'row_a'=2,'row_b'=2,'row_c'=2,'row_d'=2,'col'=2] {'col','..., dimensions={0} | all-to-all | bytes 1048576 | tf_op jit(solution)/shard_map/all_to_all | solution.py:272
  104.2 1.5 %finish.1 = bf16[16,128,128]{2,1,0:T(8,128)(2,1)} custom-call(bf16[128,16,128]{2,1,0:T(8,128)(2,1)S(1)} %bitcast.3, bf16[16,128,128]{2,1,0:T(8,128)(2,1)S(1)} %get-tuple-element.33.gate_ref, bf16[16,128,128]{2,1,0:T(8,128)(2,1)S(1)} %get-tuple-element.34.pair_t_ref, bf16[2,128,128]{2,1,0:T(8,128)(2,1)S(1)} %copy-done.3), custom_call_target="tpu_custom_call" | custom-call | flops 67108864 | bytes 2097152 | tf_op jit(solution)/shard_map/finish/pallas_call | solution.py:213
  (11 shorter events, 0.1 us)
Async XLA Ops:
  4.2 9.4 %collective-permute-start = (bf16[4,8,16,128]{3,2,1,0:T(8,128)(2,1)}, bf16[4,8,16,128]{3,2,1,0:T(8,128)(2,1)S(1)}, u32[]{:S(2)}, u32[]{:S(2)}) collective-permute-start(bf16[4,8,16,128]{3,2,1,0:T(8,128)(2,1)} %get-tuple-element.21), channel_id=1, source_target_pairs={{0,2},{2,0},{1,3},{3,1},{4,6},{6,4},{5,7},{7,5},{8,10},{10,8},{9,1... | collective-permute-start | bytes 393224 | tf_op jit(solution)/shard_map/ppermute | solution.py:244
  4.8 8.9 %collective-permute-start.1 = (bf16[4,8,16,128]{3,2,1,0:T(8,128)(2,1)}, bf16[4,8,16,128]{3,2,1,0:T(8,128)(2,1)S(1)}, u32[]{:S(2)}, u32[]{:S(2)}) collective-permute-start(bf16[4,8,16,128]{3,2,1,0:T(8,128)(2,1)} %get-tuple-element.22), channel_id=1, source_target_pairs={{0,8},{8,0},{1,9},{9,1},{2,10},{10,2},{3,11},{11,3},{4,12},{12,4},... | collective-permute-start | bytes 393224 | tf_op jit(solution)/shard_map/ppermute | solution.py:244
  7.4 6.8 %collective-permute-start.2 = (bf16[4,8,16,128]{3,2,1,0:T(8,128)(2,1)}, bf16[4,8,16,128]{3,2,1,0:T(8,128)(2,1)S(1)}, u32[]{:S(2)}, u32[]{:S(2)}) collective-permute-start(bf16[4,8,16,128]{3,2,1,0:T(8,128)(2,1)} %get-tuple-element.23), channel_id=1, source_target_pairs={{0,10},{2,8},{8,2},{10,0},{1,11},{3,9},{9,3},{11,1},{4,14},{6,12},... | collective-permute-start | bytes 393224 | tf_op jit(solution)/shard_map/ppermute | solution.py:244
  7.5 6.8 %copy-start.5 = (bf16[4,8,16,128]{3,2,1,0:T(8,128)(2,1)S(1)}, bf16[4,8,16,128]{3,2,1,0:T(8,128)(2,1)}, u32[]{:S(2)}) copy-start(bf16[4,8,16,128]{3,2,1,0:T(8,128)(2,1)} %get-tuple-element.20.refs_0_) | copy-start | bytes 393220
  7.5 32.3 %all-to-all-start = ((bf16[32,8,16,128]{3,2,1,0:T(8,128)(2,1)}), bf16[32,8,16,128]{3,2,1,0:T(8,128)(2,1)}, u32[]{:S(2)}, u32[]{:S(2)}) async-start(bf16[32,8,16,128]{3,2,1,0:T(8,128)(2,1)} %get-tuple-element.28), calls=%async_computation | async-start | bytes 2097152 | tf_op jit(solution)/shard_map/all_to_all | solution.py:272
  14.3 13.9 %collective-permute-start.3 = (bf16[4,8,16,128]{3,2,1,0:T(8,128)(2,1)S(1)}, bf16[4,8,16,128]{3,2,1,0:T(8,128)(2,1)S(1)}, u32[]{:S(2)}, u32[]{:S(2)}) collective-permute-start(bf16[4,8,16,128]{3,2,1,0:T(8,128)(2,1)S(1)} %get-tuple-element.25), channel_id=1, source_target_pairs={{0,1},{1,0},{2,3},{3,2},{4,5},{5,4},{6,7},{7,6},{8,9},{9,8},{10,11... | collective-permute-start | bytes 393224 | tf_op jit(solution)/shard_map/ppermute | solution.py:244
  15.9 12.3 %collective-permute-start.4 = (bf16[4,8,16,128]{3,2,1,0:T(8,128)(2,1)S(1)}, bf16[4,8,16,128]{3,2,1,0:T(8,128)(2,1)S(1)}, u32[]{:S(2)}, u32[]{:S(2)}) collective-permute-start(bf16[4,8,16,128]{3,2,1,0:T(8,128)(2,1)S(1)} %get-tuple-element.26), channel_id=1, source_target_pairs={{0,4},{4,0},{1,5},{5,1},{2,6},{6,2},{3,7},{7,3},{8,12},{12,8},{9,1... | collective-permute-start | bytes 393224 | tf_op jit(solution)/shard_map/ppermute | solution.py:244
  17.4 14.1 %collective-permute-start.5 = (bf16[4,8,16,128]{3,2,1,0:T(8,128)(2,1)S(1)}, bf16[4,8,16,128]{3,2,1,0:T(8,128)(2,1)S(1)}, u32[]{:S(2)}, u32[]{:S(2)}) collective-permute-start(bf16[4,8,16,128]{3,2,1,0:T(8,128)(2,1)S(1)} %get-tuple-element.27), channel_id=1, source_target_pairs={{0,5},{1,4},{4,1},{5,0},{2,7},{3,6},{6,3},{7,2},{8,13},{9,12},{12,... | collective-permute-start | bytes 393224 | tf_op jit(solution)/shard_map/ppermute | solution.py:244
  39.8 13.8 %copy-start.2 = (bf16[2,128,640]{2,1,0:T(8,128)(2,1)S(1)}, bf16[2,128,640]{2,1,0:T(8,128)(2,1)}, u32[]{:S(2)}) copy-start(bf16[2,128,640]{2,1,0:T(8,128)(2,1)} %weights_ref.1) | copy-start | bytes 983044
  39.8 13.8 %copy-start.3 = (bf16[2,128,128]{2,1,0:T(8,128)(2,1)S(1)}, bf16[2,128,128]{2,1,0:T(8,128)(2,1)}, u32[]{:S(2)}) copy-start(bf16[2,128,128]{2,1,0:T(8,128)(2,1)} %wo_ref.3) | copy-start | bytes 196612
  39.8 13.8 %copy-start.4 = (f32[16,128]{1,0:T(8,128)S(1)}, f32[16,128]{1,0:T(8,128)}, u32[]{:S(2)}) copy-start(f32[16,128]{1,0:T(8,128)} %get-tuple-element.31.mask_ref) | copy-start | bytes 24580
  41.6 12.0 %copy-start = (bf16[16,128,128]{2,1,0:T(8,128)(2,1)S(1)}, bf16[16,128,128]{2,1,0:T(8,128)(2,1)}, u32[]{:S(2)}) copy-start(bf16[16,128,128]{2,1,0:T(8,128)(2,1)} %get-tuple-element.29.gate_in_ref) | copy-start | bytes 1572868
  41.6 12.0 %copy-start.1 = (bf16[16,128,128]{2,1,0:T(8,128)(2,1)S(1)}, bf16[16,128,128]{2,1,0:T(8,128)(2,1)}, u32[]{:S(2)}) copy-start(bf16[16,128,128]{2,1,0:T(8,128)(2,1)} %get-tuple-element.30.pair_t_in_ref) | copy-start | bytes 1572868

commit v6 on v5

--- a/solution.py
+++ b/solution.py
@@ -56,13 +56,17 @@
     return jnp.concatenate([ref[first + g] for g in range(group)], axis=1)
 
 
+def project_side(normed, mask, weights_t, side):
+    width = normed.shape[0]
+    both = dot(weights_t[2 * side * width : (2 * side + 2) * width, :], normed)
+    return (sigmoid(both[0:width]) * both[width : 2 * width] * mask).astype(BF16)
+
+
 def project_rows(first, group, pair_vals, mask, weights_t, left_scr, right_scr, gate_ref):
     width = pair_vals.shape[0]
     normed = layer_norm(pair_vals, 0).astype(BF16)
     for side, scr in enumerate((left_scr, right_scr)):
-        both = dot(weights_t[2 * side * width : (2 * side + 2) * width, :], normed)
-        vals = sigmoid(both[0:width]) * both[width : 2 * width] * mask
-        store_rows(scr, first, group, vals.astype(BF16))
+        store_rows(scr, first, group, project_side(normed, mask, weights_t, side))
     gate = sigmoid(dot(weights_t[4 * width : 5 * width, :], normed))
     store_rows(gate_ref, first, group, gate.astype(BF16))
 
@@ -86,8 +90,7 @@
 
 
 def first_kernel(
-    blocks, lengths_hbm, pair_hbm, weights_hbm, right_ref, own_ref, core_ref, z_ref, z_core_ref,
-    gate_ref, pair_t_ref, mask_ref,
+    blocks, lengths_hbm, pair_hbm, weights_hbm, right_ref, own_ref, core_ref, z_ref, z_core_ref, mask_ref,
     left_scr, right_scr, wt_scr, lengths_scr, pair_scr, weights_scr, owner_scr, sems,
 ):
     rows, cols, width = pair_scr.shape
@@ -107,11 +110,10 @@
     wt_scr[...] = weights_scr[...].T
     for first in range(0, rows, group):
         pair = jnp.concatenate([pair_scr[first + g].T for g in range(group)], axis=1)
-        store_rows(pair_t_ref, first, group, pair)
-        project_rows(
-            first, group, pair.astype(F32), load_mask(mask_ref, first, group),
-            wt_scr, left_scr, right_scr, gate_ref,
-        )
+        normed = layer_norm(pair.astype(F32), 0).astype(BF16)
+        mask = load_mask(mask_ref, first, group)
+        for side, scr in enumerate((left_scr, right_scr)):
+            store_rows(scr, first, group, project_side(normed, mask, wt_scr, side))
     per = right_ref.shape[1]
     swapped = jnp.swapaxes(right_scr[...], 0, 1)
     for place, block in enumerate(blocks):
@@ -120,6 +122,17 @@
     for part_ref, (by_z, by_core) in zip((own_ref, core_ref, z_ref, z_core_ref), FLIPS):
         for x_y in range(4):
             part_ref[x_y] = owner_scr[half_place(x_y // 2, x_y % 2, flip("row_b", by_z), flip("row_d", by_core))]
+
+
+def gate_kernel(pair_ref, weights_ref, gate_ref, pair_t_ref):
+    rows, cols, width = pair_ref.shape
+    group = 2
+    gate_t = weights_ref[0, :, 4 * width : 5 * width].T
+    for first in range(0, rows, group):
+        pair = jnp.concatenate([pair_ref[first + g].T for g in range(group)], axis=1)
+        store_rows(pair_t_ref, first, group, pair)
+        normed = layer_norm(pair.astype(F32), 0).astype(BF16)
+        store_rows(gate_ref, first, group, sigmoid(dot(gate_t, normed)).astype(BF16))
 
 
 def regroup_kernel(*refs):
@@ -167,7 +180,7 @@
 
 
 def outgoing_kernel(places, *refs):
-    left_refs, (right_ref, out_ref) = refs[:4], refs[4:]
+    left_refs, right_ref, out_ref = refs[:4], refs[4], refs[6]
     _, per, rows, cols = right_ref.shape
     first_col = lax.axis_index("col") == 0
     deltas = [(z_core, by_y) for z_core in range(4) for by_y in range(2)]
@@ -224,6 +237,7 @@
 
 VM = pl.BlockSpec(memory_space=pltpu.VMEM)
 HBM = pl.BlockSpec(memory_space=pltpu.HBM)
+ANY = pl.BlockSpec(memory_space=pl.ANY)
 
 
 def places_of(sizes, order):
@@ -271,10 +285,10 @@
     def exchange(array, order):
         return lax.all_to_all(array, order, split_axis=0, concat_axis=0, tiled=True)
 
-    right, *left, gate, pair_t, mask = call(
+    right, *left, mask = call(
         functools.partial(first_kernel, half_blocks), "project",
         (shape_of(group, half_per, rows, cols),) + (part_shape,) * 4
-        + (block_shape, block_shape, shape_of(rows, cols, dtype=F32)),
+        + (shape_of(rows, cols, dtype=F32),),
         [
             scr, scr, wt_scr, pltpu.SMEM(chain_lengths.shape, jnp.int32), pltpu.VMEM(pair_act.shape, BF16),
             pltpu.VMEM(in_weights.shape[1:], BF16), pltpu.VMEM((half_group, half_per, rows, cols), BF16),
@@ -286,9 +300,12 @@
     left = to_partners(left, ("row_b", "row_d"))
     left = call(regroup_kernel, "regroup", (part_shape,) * 4, [], [VM] * 4, 3000 * flops_out, *left, vmem=4 * 1024 * 1024)
     left = to_partners(left, ("row_c", "col"))
+    gate, pair_t = call(
+        gate_kernel, "gate", (block_shape, block_shape), [], [VM, VM], flops_out, pair_act, in_weights
+    )
     tri = call(
         functools.partial(outgoing_kernel, right_places), "outgoing", shape_of(half_group, half_per, rows, cols),
-        [], [VM] * 5, flops_tri, *left, right,
+        [], [VM] * 5 + [ANY], flops_tri, *left, right, gate,
     )
     tri = exchange(tri, HALF_ORDER).reshape(width, rows, cols)
     send, gate, pair_t = call(

time: 106 us -> 105 us (level)
    pallas_call x6 -> x7, Pallas kernels: 11 us -> 11.1 us  [call(): pl.pallas_call(kernel, name=name, out_shape=out_shape, in_specs=in_specs,...]
  transfers between devices with their start and end apart: 7 -> 7, of which waited for: 4 -> 4; matrix products, arithmetic and copies ran while one was open for 0% -> 0% of each run, Pallas kernels for 0% -> 1%
where the time goes in v6:
time: 105 us
  blocking collectives  59.1 us (56%)
  waiting for transfers between devices  21.9 us (21%)
  starting transfers between devices  12.9 us (12%)
  Pallas kernels  11.1 us (11%)
    all_to_all x3, blocking collectives, exchange(): return lax.all_to_all(array, order, split_axis=0, concat_axis=0, tiled=True)  59.1 us
    ppermute x6, waiting for transfers between devices, to_partners(): lax.ppermute(p, name, pair)  13.6 us
    pallas_call x7, Pallas kernels, call(): pl.pallas_call(kernel, name=name, out_shape=out_shape, in_specs=in_specs,...  11.1 us
    all_to_all x1, waiting for transfers between devices, exchange(): return lax.all_to_all(array, order, split_axis=0, concat_axis=0, tiled=True)  8.33 us
    ppermute x6, starting transfers between devices, to_partners(): lax.ppermute(p, name, pair)  6.78 us
    all_to_all x1, starting transfers between devices, exchange(): return lax.all_to_all(array, order, split_axis=0, concat_axis=0, tiled=True)  6.13 us
  transfers between devices with their start and end apart: 7, of which 4 were waited for; matrix products, arithmetic and copies ran while one was open for 0% of the time, Pallas kernels for 1%

profile of v6, /device:TPU:0, one launch (start us, length us, event | category | flops | bytes accessed | tf_op | source)
XLA Modules:
  0.0 105.1 jit_solution(4229996728617307551)
XLA Ops:
  0.0 3.8 %project.1 = (bf16[32,8,16,128]{3,2,1,0:T(8,128)(2,1)}, bf16[4,8,16,128]{3,2,1,0:T(8,128)(2,1)}, bf16[4,8,16,128]{3,2,1,0:T(8,128)(2,1)}, bf16[4,8,16,128]{3,2,1...) custom-call(s32[8]{0:T(128)} %lengths_hbm.1, bf16[16,128,128]{2,1,0:T(8,128)(2,1)} %pair_ref.1, ...), custom_call_target="tpu_custom_call" | custom-call | flops 335544320 | bytes 2097152 | tf_op jit(solution)/shard_map/project/pallas_call | solution.py:226
  3.8 0.5 collective-permute-start
  4.3 2.6 %collective-permute-start.1 = (bf16[4,8,16,128]{3,2,1,0:T(8,128)(2,1)}, bf16[4,8,16,128]{3,2,1,0:T(8,128)(2,1)S(1)}, u32[]{:S(2)}, u32[]{:S(2)}) collective-permute-start(bf16[4,8,16,128]{3,2,1,0:T(8,128)(2,1)} %get-tuple-element.22), channel_id=1, source_target_pairs={{0,8},{8,0},{1,9},{9,1},{2,10},{10,2},{3,11},{11,3},{4,12},{12,4},... | collective-permute-start | bytes 393224 | tf_op jit(solution)/shard_map/ppermute | solution.py:258
  7.0 0.1 collective-permute-start.2
  7.1 6.1 %all-to-all-start = ((bf16[32,8,16,128]{3,2,1,0:T(8,128)(2,1)}), bf16[32,8,16,128]{3,2,1,0:T(8,128)(2,1)}, u32[]{:S(2)}, u32[]{:S(2)}) async-start(bf16[32,8,16,128]{3,2,1,0:T(8,128)(2,1)} %get-tuple-element.28), calls=%async_computation | async-start | bytes 2097152 | tf_op jit(solution)/shard_map/all_to_all | solution.py:286
  13.2 0.0 collective-permute-done.refs_1_
  13.2 0.0 collective-permute-done.1.refs_2_
  13.2 0.6 collective-permute-done.2.refs_3_
  13.9 1.6 %collective-permute-start.3 = (bf16[4,8,16,128]{3,2,1,0:T(8,128)(2,1)S(1)}, bf16[4,8,16,128]{3,2,1,0:T(8,128)(2,1)S(1)}, u32[]{:S(2)}, u32[]{:S(2)}) collective-permute-start(bf16[4,8,16,128]{3,2,1,0:T(8,128)(2,1)S(1)} %get-tuple-element.25), channel_id=1, source_target_pairs={{0,1},{1,0},{2,3},{3,2},{4,5},{5,4},{6,7},{7,6},{8,9},{9,8},{10,11... | collective-permute-start | bytes 393224 | tf_op jit(solution)/shard_map/ppermute | solution.py:258
  15.4 1.5 %collective-permute-start.4 = (bf16[4,8,16,128]{3,2,1,0:T(8,128)(2,1)S(1)}, bf16[4,8,16,128]{3,2,1,0:T(8,128)(2,1)S(1)}, u32[]{:S(2)}, u32[]{:S(2)}) collective-permute-start(bf16[4,8,16,128]{3,2,1,0:T(8,128)(2,1)S(1)} %get-tuple-element.26), channel_id=1, source_target_pairs={{0,4},{4,0},{1,5},{5,1},{2,6},{6,2},{3,7},{7,3},{8,12},{12,8},{9,1... | collective-permute-start | bytes 393224 | tf_op jit(solution)/shard_map/ppermute | solution.py:258
  17.0 0.5 collective-permute-start.5
  17.4 0.7 gate.1
  18.1 9.7 %collective-permute-done.3.refs_1_ = bf16[4,8,16,128]{3,2,1,0:T(8,128)(2,1)S(1)} collective-permute-done((bf16[4,8,16,128]{3,2,1,0:T(8,128)(2,1)S(1)}, bf16[4,8,16,128]{3,2,1,0:T(8,128)(2,1)S(1)}, u32[]{:S(2)}, u32[]{:S(2)}) %collective-permute-start.3) | collective-permute-done | bytes 131104 | tf_op jit(solution)/shard_map/ppermute | solution.py:258
  27.8 0.0 collective-permute-done.4.refs_2_
  27.8 3.3 %collective-permute-done.5.refs_3_ = bf16[4,8,16,128]{3,2,1,0:T(8,128)(2,1)S(1)} collective-permute-done((bf16[4,8,16,128]{3,2,1,0:T(8,128)(2,1)S(1)}, bf16[4,8,16,128]{3,2,1,0:T(8,128)(2,1)S(1)}, u32[]{:S(2)}, u32[]{:S(2)}) %collective-permute-start.5) | collective-permute-done | bytes 131104 | tf_op jit(solution)/shard_map/ppermute | solution.py:258
  31.1 8.3 %all-to-all-done.refs_4_ = bf16[32,8,16,128]{3,2,1,0:T(8,128)(2,1)} async-done(((bf16[32,8,16,128]{3,2,1,0:T(8,128)(2,1)}), bf16[32,8,16,128]{3,2,1,0:T(8,128)(2,1)}, u32[]{:S(2)}, u32[]{:S(2)}) %all-to-all-start) | async-done | bytes 1048608 | tf_op jit(solution)/shard_map/all_to_all | solution.py:286
  39.4 1.7 %outgoing.1 = bf16[16,8,16,128]{3,2,1,0:T(8,128)(2,1)S(1)} custom-call(bf16[4,8,16,128]{3,2,1,0:T(8,128)(2,1)S(1)} %get-tuple-element.24.refs_0_, bf16[4,8,16,128]{3,2,1,0:T(8,128)(2,1)S(1)} %collective-permute-done.3.refs_1_, bf16[4,8,16,128]{3,2,1,0:T(8,128)(2,1)S(1)} %collective-permute-done.4.refs_2_, ...), custom_call_target="tpu_custom_call" | custom-call | flops 4294967296 | bytes 2097152 | tf_op jit(solution)/shard_map/outgoing/pallas_call | solution.py:226
  41.1 0.0 copy-start.2
  41.1 12.0 %all_to_all.20 = bf16[16,8,16,128]{3,2,1,0:T(8,128)(2,1)S(1)} all-to-all(bf16[16,8,16,128]{3,2,1,0:T(8,128)(2,1)S(1)} %outgoing.1), channel_id=1, replica_groups=mesh['parts'=1,'row_a'=2,'row_b'=2,'row_c'=2,'row_d'=2,'col'=2] {'row_c'..., dimensions={0} | all-to-all | bytes 1048576 | tf_op jit(solution)/shard_map/all_to_all | solution.py:286
  53.1 3.1 %finish_project.1 = (bf16[32,2,4,16,128]{4,3,2,1,0:T(8,128)(2,1)S(1)}, bf16[16,128,128]{2,1,0:T(8,128)(2,1)S(1)}, bf16[16,128,128]{2,1,0:T(8,128)(2,1)S(1)}) custom-call(bf16[128,16,128]{2,1,0:T(8,128)(2,1)S(1)} %bitcast.2, bf16[16,128,128]{2,1,0:T(8,128)(2,1)S(1)} %get-tuple-element.29.refs_5_.gate_in_ref, ...), custom_call_target="tpu_custom_call" | custom-call | flops 402653184 | bytes 2097152 | tf_op jit(solution)/shard_map/finish_project/pallas_call | solution.py:226
  56.2 29.9 %all_to_all.21.recv_ref = bf16[32,2,4,16,128]{4,3,2,1,0:T(8,128)(2,1)S(1)} all-to-all(bf16[32,2,4,16,128]{4,3,2,1,0:T(8,128)(2,1)S(1)} %get-tuple-element.32), channel_id=1, replica_groups=mesh['parts'=1,'row_a'=2,'row_b'=2,'row_c'=2,'row_d'=2,'col'=2] {'col','..., dimensions={0} | all-to-all | bytes 2097152 | tf_op jit(solution)/shard_map/all_to_all | solution.py:286
  86.2 0.3 incoming.1
  86.5 17.1 %all_to_all.22 = bf16[32,4,16,128]{3,2,1,0:T(8,128)(2,1)S(1)} all-to-all(bf16[32,4,16,128]{3,2,1,0:T(8,128)(2,1)S(1)} %incoming.1), channel_id=1, replica_groups=mesh['parts'=1,'row_a'=2,'row_b'=2,'row_c'=2,'row_d'=2,'col'=2] {'col','..., dimensions={0} | all-to-all | bytes 1048576 | tf_op jit(solution)/shard_map/all_to_all | solution.py:286
  103.7 1.5 %finish.1 = bf16[16,128,128]{2,1,0:T(8,128)(2,1)} custom-call(bf16[128,16,128]{2,1,0:T(8,128)(2,1)S(1)} %bitcast.3, bf16[16,128,128]{2,1,0:T(8,128)(2,1)S(1)} %get-tuple-element.33.gate_ref, bf16[16,128,128]{2,1,0:T(8,128)(2,1)S(1)} %get-tuple-element.34.pair_t_ref, bf16[2,128,128]{2,1,0:T(8,128)(2,1)S(1)} %copy-done.2), custom_call_target="tpu_custom_call" | custom-call | flops 67108864 | bytes 2097152 | tf_op jit(solution)/shard_map/finish/pallas_call | solution.py:226
  (10 shorter events, 0.1 us)
Async XLA Ops:
  3.8 9.4 %collective-permute-start = (bf16[4,8,16,128]{3,2,1,0:T(8,128)(2,1)}, bf16[4,8,16,128]{3,2,1,0:T(8,128)(2,1)S(1)}, u32[]{:S(2)}, u32[]{:S(2)}) collective-permute-start(bf16[4,8,16,128]{3,2,1,0:T(8,128)(2,1)} %get-tuple-element.21), channel_id=1, source_target_pairs={{0,2},{2,0},{1,3},{3,1},{4,6},{6,4},{5,7},{7,5},{8,10},{10,8},{9,1... | collective-permute-start | bytes 393224 | tf_op jit(solution)/shard_map/ppermute | solution.py:258
  4.3 8.9 %collective-permute-start.1 = (bf16[4,8,16,128]{3,2,1,0:T(8,128)(2,1)}, bf16[4,8,16,128]{3,2,1,0:T(8,128)(2,1)S(1)}, u32[]{:S(2)}, u32[]{:S(2)}) collective-permute-start(bf16[4,8,16,128]{3,2,1,0:T(8,128)(2,1)} %get-tuple-element.22), channel_id=1, source_target_pairs={{0,8},{8,0},{1,9},{9,1},{2,10},{10,2},{3,11},{11,3},{4,12},{12,4},... | collective-permute-start | bytes 393224 | tf_op jit(solution)/shard_map/ppermute | solution.py:258
  7.0 6.8 %collective-permute-start.2 = (bf16[4,8,16,128]{3,2,1,0:T(8,128)(2,1)}, bf16[4,8,16,128]{3,2,1,0:T(8,128)(2,1)S(1)}, u32[]{:S(2)}, u32[]{:S(2)}) collective-permute-start(bf16[4,8,16,128]{3,2,1,0:T(8,128)(2,1)} %get-tuple-element.23), channel_id=1, source_target_pairs={{0,10},{2,8},{8,2},{10,0},{1,11},{3,9},{9,3},{11,1},{4,14},{6,12},... | collective-permute-start | bytes 393224 | tf_op jit(solution)/shard_map/ppermute | solution.py:258
  7.1 6.8 %copy-start.4 = (bf16[4,8,16,128]{3,2,1,0:T(8,128)(2,1)S(1)}, bf16[4,8,16,128]{3,2,1,0:T(8,128)(2,1)}, u32[]{:S(2)}) copy-start(bf16[4,8,16,128]{3,2,1,0:T(8,128)(2,1)} %get-tuple-element.20.refs_0_) | copy-start | bytes 393220
  7.1 32.3 %all-to-all-start = ((bf16[32,8,16,128]{3,2,1,0:T(8,128)(2,1)}), bf16[32,8,16,128]{3,2,1,0:T(8,128)(2,1)}, u32[]{:S(2)}, u32[]{:S(2)}) async-start(bf16[32,8,16,128]{3,2,1,0:T(8,128)(2,1)} %get-tuple-element.28), calls=%async_computation | async-start | bytes 2097152 | tf_op jit(solution)/shard_map/all_to_all | solution.py:286
  13.8 3.6 %copy-start = (bf16[2,128,640]{2,1,0:T(8,128)(2,1)S(1)}, bf16[2,128,640]{2,1,0:T(8,128)(2,1)}, u32[]{:S(2)}) copy-start(bf16[2,128,640]{2,1,0:T(8,128)(2,1)} %weights_ref.3) | copy-start | bytes 983044
  13.8 3.6 %copy-start.1 = (bf16[16,128,128]{2,1,0:T(8,128)(2,1)S(1)}, bf16[16,128,128]{2,1,0:T(8,128)(2,1)}, u32[]{:S(2)}) copy-start(bf16[16,128,128]{2,1,0:T(8,128)(2,1)} %pair_ref.1) | copy-start | bytes 1572868
  13.9 13.9 %collective-permute-start.3 = (bf16[4,8,16,128]{3,2,1,0:T(8,128)(2,1)S(1)}, bf16[4,8,16,128]{3,2,1,0:T(8,128)(2,1)S(1)}, u32[]{:S(2)}, u32[]{:S(2)}) collective-permute-start(bf16[4,8,16,128]{3,2,1,0:T(8,128)(2,1)S(1)} %get-tuple-element.25), channel_id=1, source_target_pairs={{0,1},{1,0},{2,3},{3,2},{4,5},{5,4},{6,7},{7,6},{8,9},{9,8},{10,11... | collective-permute-start | bytes 393224 | tf_op jit(solution)/shard_map/ppermute | solution.py:258
  15.4 12.3 %collective-permute-start.4 = (bf16[4,8,16,128]{3,2,1,0:T(8,128)(2,1)S(1)}, bf16[4,8,16,128]{3,2,1,0:T(8,128)(2,1)S(1)}, u32[]{:S(2)}, u32[]{:S(2)}) collective-permute-start(bf16[4,8,16,128]{3,2,1,0:T(8,128)(2,1)S(1)} %get-tuple-element.26), channel_id=1, source_target_pairs={{0,4},{4,0},{1,5},{5,1},{2,6},{6,2},{3,7},{7,3},{8,12},{12,8},{9,1... | collective-permute-start | bytes 393224 | tf_op jit(solution)/shard_map/ppermute | solution.py:258
  17.0 14.1 %collective-permute-start.5 = (bf16[4,8,16,128]{3,2,1,0:T(8,128)(2,1)S(1)}, bf16[4,8,16,128]{3,2,1,0:T(8,128)(2,1)S(1)}, u32[]{:S(2)}, u32[]{:S(2)}) collective-permute-start(bf16[4,8,16,128]{3,2,1,0:T(8,128)(2,1)S(1)} %get-tuple-element.27), channel_id=1, source_target_pairs={{0,5},{1,4},{4,1},{5,0},{2,7},{3,6},{6,3},{7,2},{8,13},{9,12},{12,... | collective-permute-start | bytes 393224 | tf_op jit(solution)/shard_map/ppermute | solution.py:258
  41.1 12.0 %copy-start.2 = (bf16[2,128,128]{2,1,0:T(8,128)(2,1)S(1)}, bf16[2,128,128]{2,1,0:T(8,128)(2,1)}, u32[]{:S(2)}) copy-start(bf16[2,128,128]{2,1,0:T(8,128)(2,1)} %wo_ref.3) | copy-start | bytes 196612
  41.1 12.0 %copy-start.3 = (f32[16,128]{1,0:T(8,128)S(1)}, f32[16,128]{1,0:T(8,128)}, u32[]{:S(2)}) copy-start(f32[16,128]{1,0:T(8,128)} %get-tuple-element.31.mask_ref) | copy-start | bytes 24580

commit v7 on v6

--- a/solution.py
+++ b/solution.py
@@ -94,7 +94,7 @@
     left_scr, right_scr, wt_scr, lengths_scr, pair_scr, weights_scr, owner_scr, sems,
 ):
     rows, cols, width = pair_scr.shape
-    group = 2
+    group = rows
     fetches = [
         pltpu.make_async_copy(weights_hbm.at[0], weights_scr, sems.at[0]),
         pltpu.make_async_copy(pair_hbm, pair_scr, sems.at[1]),
@@ -126,7 +126,7 @@
 
 def gate_kernel(pair_ref, weights_ref, gate_ref, pair_t_ref):
     rows, cols, width = pair_ref.shape
-    group = 2
+    group = rows
     gate_t = weights_ref[0, :, 4 * width : 5 * width].T
     for first in range(0, rows, group):
         pair = jnp.concatenate([pair_ref[first + g].T for g in range(group)], axis=1)
@@ -154,7 +154,7 @@
     send_ref, gate_ref, pair_t_ref, left_scr, right_scr, wt_scr, tri_scr,
 ):
     width, rows, cols = tri_ref.shape
-    group = 2
+    group = rows
     wt_scr[...] = weights_ref[1].T
     wo_t = wo_ref[0].T
     tri_scr[...] = jnp.swapaxes(tri_ref[...], 0, 1)
@@ -170,7 +170,7 @@
 
 def last_kernel(tri_ref, gate_ref, pair_t_ref, wo_ref, out_ref, tri_scr):
     width, rows, cols = tri_ref.shape
-    group = 2
+    group = rows
     wo_t = wo_ref[1].T
     tri_scr[...] = jnp.swapaxes(tri_ref[...], 0, 1)
     for first in range(0, rows, group):

time: 105 us -> 104 us (level)
    pallas_call x7, Pallas kernels: 11.1 us -> 10.1 us  [call(): pl.pallas_call(kernel, name=name, out_shape=out_shape, in_specs=in_specs,...]
where the time goes in v7:
time: 104 us
  blocking collectives  59.1 us (57%)
  waiting for transfers between devices  21.9 us (21%)
  starting transfers between devices  12.9 us (12%)
  Pallas kernels  10.1 us (10%)
    all_to_all x3, blocking collectives, exchange(): return lax.all_to_all(array, order, split_axis=0, concat_axis=0, tiled=True)  59.1 us
    ppermute x6, waiting for transfers between devices, to_partners(): lax.ppermute(p, name, pair)  13.6 us
    pallas_call x7, Pallas kernels, call(): pl.pallas_call(kernel, name=name, out_shape=out_shape, in_specs=in_specs,...  10.1 us
    all_to_all x1, waiting for transfers between devices, exchange(): return lax.all_to_all(array, order, split_axis=0, concat_axis=0, tiled=True)  8.33 us
    ppermute x6, starting transfers between devices, to_partners(): lax.ppermute(p, name, pair)  6.79 us
    all_to_all x1, starting transfers between devices, exchange(): return lax.all_to_all(array, order, split_axis=0, concat_axis=0, tiled=True)  6.13 us
  transfers between devices with their start and end apart: 7, of which 4 were waited for; matrix products, arithmetic and copies ran while one was open for 0% of the time, Pallas kernels for 1%

profile of v7, /device:TPU:0, one launch (start us, length us, event | category | flops | bytes accessed | tf_op | source)
XLA Modules:
  0.0 104.1 jit_solution(17548460059115343435)
XLA Ops:
  0.0 3.7 %project.1 = (bf16[32,8,16,128]{3,2,1,0:T(8,128)(2,1)}, bf16[4,8,16,128]{3,2,1,0:T(8,128)(2,1)}, bf16[4,8,16,128]{3,2,1,0:T(8,128)(2,1)}, bf16[4,8,16,128]{3,2,1...) custom-call(s32[8]{0:T(128)} %lengths_hbm.1, bf16[16,128,128]{2,1,0:T(8,128)(2,1)} %pair_ref.1, ...), custom_call_target="tpu_custom_call" | custom-call | flops 335544320 | bytes 2097152 | tf_op jit(solution)/shard_map/project/pallas_call | solution.py:226
  3.7 0.5 collective-permute-start
  4.2 2.7 %collective-permute-start.1 = (bf16[4,8,16,128]{3,2,1,0:T(8,128)(2,1)}, bf16[4,8,16,128]{3,2,1,0:T(8,128)(2,1)S(1)}, u32[]{:S(2)}, u32[]{:S(2)}) collective-permute-start(bf16[4,8,16,128]{3,2,1,0:T(8,128)(2,1)} %get-tuple-element.22), channel_id=1, source_target_pairs={{0,8},{8,0},{1,9},{9,1},{2,10},{10,2},{3,11},{11,3},{4,12},{12,4},... | collective-permute-start | bytes 393224 | tf_op jit(solution)/shard_map/ppermute | solution.py:258
  6.9 0.1 collective-permute-start.2
  7.0 6.1 %all-to-all-start = ((bf16[32,8,16,128]{3,2,1,0:T(8,128)(2,1)}), bf16[32,8,16,128]{3,2,1,0:T(8,128)(2,1)}, u32[]{:S(2)}, u32[]{:S(2)}) async-start(bf16[32,8,16,128]{3,2,1,0:T(8,128)(2,1)} %get-tuple-element.28), calls=%async_computation | async-start | bytes 2097152 | tf_op jit(solution)/shard_map/all_to_all | solution.py:286
  13.1 0.0 collective-permute-done.refs_1_
  13.1 0.0 collective-permute-done.1.refs_2_
  13.1 0.6 collective-permute-done.2.refs_3_
  13.8 1.5 %collective-permute-start.3 = (bf16[4,8,16,128]{3,2,1,0:T(8,128)(2,1)S(1)}, bf16[4,8,16,128]{3,2,1,0:T(8,128)(2,1)S(1)}, u32[]{:S(2)}, u32[]{:S(2)}) collective-permute-start(bf16[4,8,16,128]{3,2,1,0:T(8,128)(2,1)S(1)} %get-tuple-element.25), channel_id=1, source_target_pairs={{0,1},{1,0},{2,3},{3,2},{4,5},{5,4},{6,7},{7,6},{8,9},{9,8},{10,11... | collective-permute-start | bytes 393224 | tf_op jit(solution)/shard_map/ppermute | solution.py:258
  15.3 1.5 %collective-permute-start.4 = (bf16[4,8,16,128]{3,2,1,0:T(8,128)(2,1)S(1)}, bf16[4,8,16,128]{3,2,1,0:T(8,128)(2,1)S(1)}, u32[]{:S(2)}, u32[]{:S(2)}) collective-permute-start(bf16[4,8,16,128]{3,2,1,0:T(8,128)(2,1)S(1)} %get-tuple-element.26), channel_id=1, source_target_pairs={{0,4},{4,0},{1,5},{5,1},{2,6},{6,2},{3,7},{7,3},{8,12},{12,8},{9,1... | collective-permute-start | bytes 393224 | tf_op jit(solution)/shard_map/ppermute | solution.py:258
  16.8 0.5 collective-permute-start.5
  17.3 0.7 gate.1
  18.0 9.7 %collective-permute-done.3.refs_1_ = bf16[4,8,16,128]{3,2,1,0:T(8,128)(2,1)S(1)} collective-permute-done((bf16[4,8,16,128]{3,2,1,0:T(8,128)(2,1)S(1)}, bf16[4,8,16,128]{3,2,1,0:T(8,128)(2,1)S(1)}, u32[]{:S(2)}, u32[]{:S(2)}) %collective-permute-start.3) | collective-permute-done | bytes 131104 | tf_op jit(solution)/shard_map/ppermute | solution.py:258
  27.7 0.0 collective-permute-done.4.refs_2_
  27.7 3.3 %collective-permute-done.5.refs_3_ = bf16[4,8,16,128]{3,2,1,0:T(8,128)(2,1)S(1)} collective-permute-done((bf16[4,8,16,128]{3,2,1,0:T(8,128)(2,1)S(1)}, bf16[4,8,16,128]{3,2,1,0:T(8,128)(2,1)S(1)}, u32[]{:S(2)}, u32[]{:S(2)}) %collective-permute-start.5) | collective-permute-done | bytes 131104 | tf_op jit(solution)/shard_map/ppermute | solution.py:258
  31.0 8.3 %all-to-all-done.refs_4_ = bf16[32,8,16,128]{3,2,1,0:T(8,128)(2,1)} async-done(((bf16[32,8,16,128]{3,2,1,0:T(8,128)(2,1)}), bf16[32,8,16,128]{3,2,1,0:T(8,128)(2,1)}, u32[]{:S(2)}, u32[]{:S(2)}) %all-to-all-start) | async-done | bytes 1048608 | tf_op jit(solution)/shard_map/all_to_all | solution.py:286
  39.3 1.7 %outgoing.1 = bf16[16,8,16,128]{3,2,1,0:T(8,128)(2,1)S(1)} custom-call(bf16[4,8,16,128]{3,2,1,0:T(8,128)(2,1)S(1)} %get-tuple-element.24.refs_0_, bf16[4,8,16,128]{3,2,1,0:T(8,128)(2,1)S(1)} %collective-permute-done.3.refs_1_, bf16[4,8,16,128]{3,2,1,0:T(8,128)(2,1)S(1)} %collective-permute-done.4.refs_2_, ...), custom_call_target="tpu_custom_call" | custom-call | flops 4294967296 | bytes 2097152 | tf_op jit(solution)/shard_map/outgoing/pallas_call | solution.py:226
  41.0 0.0 copy-start.2
  41.0 12.0 %all_to_all.20 = bf16[16,8,16,128]{3,2,1,0:T(8,128)(2,1)S(1)} all-to-all(bf16[16,8,16,128]{3,2,1,0:T(8,128)(2,1)S(1)} %outgoing.1), channel_id=1, replica_groups=mesh['parts'=1,'row_a'=2,'row_b'=2,'row_c'=2,'row_d'=2,'col'=2] {'row_c'..., dimensions={0} | all-to-all | bytes 1048576 | tf_op jit(solution)/shard_map/all_to_all | solution.py:286
  53.0 2.1 %finish_project.1 = (bf16[32,2,4,16,128]{4,3,2,1,0:T(8,128)(2,1)S(1)}, bf16[16,128,128]{2,1,0:T(8,128)(2,1)S(1)}, bf16[16,128,128]{2,1,0:T(8,128)(2,1)S(1)}) custom-call(bf16[128,16,128]{2,1,0:T(8,128)(2,1)S(1)} %bitcast.2, bf16[16,128,128]{2,1,0:T(8,128)(2,1)S(1)} %get-tuple-element.29.refs_5_.gate_in_ref, ...), custom_call_target="tpu_custom_call" | custom-call | flops 402653184 | bytes 2097152 | tf_op jit(solution)/shard_map/finish_project/pallas_call | solution.py:226
  55.2 30.0 %all_to_all.21.recv_ref = bf16[32,2,4,16,128]{4,3,2,1,0:T(8,128)(2,1)S(1)} all-to-all(bf16[32,2,4,16,128]{4,3,2,1,0:T(8,128)(2,1)S(1)} %get-tuple-element.32), channel_id=1, replica_groups=mesh['parts'=1,'row_a'=2,'row_b'=2,'row_c'=2,'row_d'=2,'col'=2] {'col','..., dimensions={0} | all-to-all | bytes 2097152 | tf_op jit(solution)/shard_map/all_to_all | solution.py:286
  85.1 0.3 incoming.1
  85.5 17.1 %all_to_all.22 = bf16[32,4,16,128]{3,2,1,0:T(8,128)(2,1)S(1)} all-to-all(bf16[32,4,16,128]{3,2,1,0:T(8,128)(2,1)S(1)} %incoming.1), channel_id=1, replica_groups=mesh['parts'=1,'row_a'=2,'row_b'=2,'row_c'=2,'row_d'=2,'col'=2] {'col','..., dimensions={0} | all-to-all | bytes 1048576 | tf_op jit(solution)/shard_map/all_to_all | solution.py:286
  102.6 1.5 %finish.1 = bf16[16,128,128]{2,1,0:T(8,128)(2,1)} custom-call(bf16[128,16,128]{2,1,0:T(8,128)(2,1)S(1)} %bitcast.3, bf16[16,128,128]{2,1,0:T(8,128)(2,1)S(1)} %get-tuple-element.33.gate_ref, bf16[16,128,128]{2,1,0:T(8,128)(2,1)S(1)} %get-tuple-element.34.pair_t_ref, bf16[2,128,128]{2,1,0:T(8,128)(2,1)S(1)} %copy-done.2), custom_call_target="tpu_custom_call" | custom-call | flops 67108864 | bytes 2097152 | tf_op jit(solution)/shard_map/finish/pallas_call | solution.py:226
  (10 shorter events, 0.1 us)
Async XLA Ops:
  3.7 9.4 %collective-permute-start = (bf16[4,8,16,128]{3,2,1,0:T(8,128)(2,1)}, bf16[4,8,16,128]{3,2,1,0:T(8,128)(2,1)S(1)}, u32[]{:S(2)}, u32[]{:S(2)}) collective-permute-start(bf16[4,8,16,128]{3,2,1,0:T(8,128)(2,1)} %get-tuple-element.21), channel_id=1, source_target_pairs={{0,2},{2,0},{1,3},{3,1},{4,6},{6,4},{5,7},{7,5},{8,10},{10,8},{9,1... | collective-permute-start | bytes 393224 | tf_op jit(solution)/shard_map/ppermute | solution.py:258
  4.2 8.9 %collective-permute-start.1 = (bf16[4,8,16,128]{3,2,1,0:T(8,128)(2,1)}, bf16[4,8,16,128]{3,2,1,0:T(8,128)(2,1)S(1)}, u32[]{:S(2)}, u32[]{:S(2)}) collective-permute-start(bf16[4,8,16,128]{3,2,1,0:T(8,128)(2,1)} %get-tuple-element.22), channel_id=1, source_target_pairs={{0,8},{8,0},{1,9},{9,1},{2,10},{10,2},{3,11},{11,3},{4,12},{12,4},... | collective-permute-start | bytes 393224 | tf_op jit(solution)/shard_map/ppermute | solution.py:258
  6.9 6.8 %collective-permute-start.2 = (bf16[4,8,16,128]{3,2,1,0:T(8,128)(2,1)}, bf16[4,8,16,128]{3,2,1,0:T(8,128)(2,1)S(1)}, u32[]{:S(2)}, u32[]{:S(2)}) collective-permute-start(bf16[4,8,16,128]{3,2,1,0:T(8,128)(2,1)} %get-tuple-element.23), channel_id=1, source_target_pairs={{0,10},{2,8},{8,2},{10,0},{1,11},{3,9},{9,3},{11,1},{4,14},{6,12},... | collective-permute-start | bytes 393224 | tf_op jit(solution)/shard_map/ppermute | solution.py:258
  7.0 6.8 %copy-start.4 = (bf16[4,8,16,128]{3,2,1,0:T(8,128)(2,1)S(1)}, bf16[4,8,16,128]{3,2,1,0:T(8,128)(2,1)}, u32[]{:S(2)}) copy-start(bf16[4,8,16,128]{3,2,1,0:T(8,128)(2,1)} %get-tuple-element.20.refs_0_) | copy-start | bytes 393220
  7.0 32.3 %all-to-all-start = ((bf16[32,8,16,128]{3,2,1,0:T(8,128)(2,1)}), bf16[32,8,16,128]{3,2,1,0:T(8,128)(2,1)}, u32[]{:S(2)}, u32[]{:S(2)}) async-start(bf16[32,8,16,128]{3,2,1,0:T(8,128)(2,1)} %get-tuple-element.28), calls=%async_computation | async-start | bytes 2097152 | tf_op jit(solution)/shard_map/all_to_all | solution.py:286
  13.7 3.6 %copy-start = (bf16[2,128,640]{2,1,0:T(8,128)(2,1)S(1)}, bf16[2,128,640]{2,1,0:T(8,128)(2,1)}, u32[]{:S(2)}) copy-start(bf16[2,128,640]{2,1,0:T(8,128)(2,1)} %weights_ref.3) | copy-start | bytes 983044
  13.7 3.6 %copy-start.1 = (bf16[16,128,128]{2,1,0:T(8,128)(2,1)S(1)}, bf16[16,128,128]{2,1,0:T(8,128)(2,1)}, u32[]{:S(2)}) copy-start(bf16[16,128,128]{2,1,0:T(8,128)(2,1)} %pair_ref.1) | copy-start | bytes 1572868
  13.8 13.9 %collective-permute-start.3 = (bf16[4,8,16,128]{3,2,1,0:T(8,128)(2,1)S(1)}, bf16[4,8,16,128]{3,2,1,0:T(8,128)(2,1)S(1)}, u32[]{:S(2)}, u32[]{:S(2)}) collective-permute-start(bf16[4,8,16,128]{3,2,1,0:T(8,128)(2,1)S(1)} %get-tuple-element.25), channel_id=1, source_target_pairs={{0,1},{1,0},{2,3},{3,2},{4,5},{5,4},{6,7},{7,6},{8,9},{9,8},{10,11... | collective-permute-start | bytes 393224 | tf_op jit(solution)/shard_map/ppermute | solution.py:258
  15.3 12.3 %collective-permute-start.4 = (bf16[4,8,16,128]{3,2,1,0:T(8,128)(2,1)S(1)}, bf16[4,8,16,128]{3,2,1,0:T(8,128)(2,1)S(1)}, u32[]{:S(2)}, u32[]{:S(2)}) collective-permute-start(bf16[4,8,16,128]{3,2,1,0:T(8,128)(2,1)S(1)} %get-tuple-element.26), channel_id=1, source_target_pairs={{0,4},{4,0},{1,5},{5,1},{2,6},{6,2},{3,7},{7,3},{8,12},{12,8},{9,1... | collective-permute-start | bytes 393224 | tf_op jit(solution)/shard_map/ppermute | solution.py:258
  16.8 14.1 %collective-permute-start.5 = (bf16[4,8,16,128]{3,2,1,0:T(8,128)(2,1)S(1)}, bf16[4,8,16,128]{3,2,1,0:T(8,128)(2,1)S(1)}, u32[]{:S(2)}, u32[]{:S(2)}) collective-permute-start(bf16[4,8,16,128]{3,2,1,0:T(8,128)(2,1)S(1)} %get-tuple-element.27), channel_id=1, source_target_pairs={{0,5},{1,4},{4,1},{5,0},{2,7},{3,6},{6,3},{7,2},{8,13},{9,12},{12,... | collective-permute-start | bytes 393224 | tf_op jit(solution)/shard_map/ppermute | solution.py:258
  41.0 12.0 %copy-start.2 = (bf16[2,128,128]{2,1,0:T(8,128)(2,1)S(1)}, bf16[2,128,128]{2,1,0:T(8,128)(2,1)}, u32[]{:S(2)}) copy-start(bf16[2,128,128]{2,1,0:T(8,128)(2,1)} %wo_ref.3) | copy-start | bytes 196612
  41.0 12.0 %copy-start.3 = (f32[16,128]{1,0:T(8,128)S(1)}, f32[16,128]{1,0:T(8,128)}, u32[]{:S(2)}) copy-start(f32[16,128]{1,0:T(8,128)} %get-tuple-element.31.mask_ref) | copy-start | bytes 24580

commit v8 on v7

--- a/solution.py
+++ b/solution.py
@@ -12,7 +12,7 @@
 F32 = jnp.float32
 BF16 = jnp.bfloat16
 VMEM_LIMIT = 32 * 1024 * 1024
-FIRST_VMEM_LIMIT = 56 * 1024 * 1024
+FIRST_VMEM_LIMIT = 54 * 1024 * 1024
 ROW_AXES = ("row_a", "row_b", "row_c", "row_d")
 RIGHT_ORDER = ("col", "row_d", "row_a", "row_c", "row_b")
 SIDES_ORDER = ("col", "row_d", "row_c", "row_a", "row_b")
@@ -124,10 +124,13 @@
             part_ref[x_y] = owner_scr[half_place(x_y // 2, x_y % 2, flip("row_b", by_z), flip("row_d", by_core))]
 
 
-def gate_kernel(pair_ref, weights_ref, gate_ref, pair_t_ref):
+def gate_kernel(pair_ref, weights_ref, wo_ref, gate_ref, pair_t_ref, wt_ref, wo_t_ref, last_wo_t_ref):
     rows, cols, width = pair_ref.shape
     group = rows
     gate_t = weights_ref[0, :, 4 * width : 5 * width].T
+    wt_ref[...] = weights_ref[1].T
+    wo_t_ref[...] = wo_ref[0].T
+    last_wo_t_ref[...] = wo_ref[1].T
     for first in range(0, rows, group):
         pair = jnp.concatenate([pair_ref[first + g].T for g in range(group)], axis=1)
         store_rows(pair_t_ref, first, group, pair)
@@ -150,33 +153,36 @@
 
 
 def middle_kernel(
-    blocks, tri_ref, gate_in_ref, pair_t_in_ref, mask_ref, wo_ref, weights_ref,
-    send_ref, gate_ref, pair_t_ref, left_scr, right_scr, wt_scr, tri_scr,
+    blocks, tri_ref, gate_in_ref, pair_t_in_ref, mask_ref, wo_t_ref, wt_ref,
+    send_ref, gate_ref, pair_t_ref, left_scr, right_scr, tri_scr,
 ):
     width, rows, cols = tri_ref.shape
     group = rows
-    wt_scr[...] = weights_ref[1].T
-    wo_t = wo_ref[0].T
     tri_scr[...] = jnp.swapaxes(tri_ref[...], 0, 1)
     for first in range(0, rows, group):
-        passed = finish_rows(first, group, tri_scr, wo_t, gate_in_ref, pair_t_in_ref)
+        passed = finish_rows(first, group, tri_scr, wo_t_ref[...], gate_in_ref, pair_t_in_ref)
         store_rows(pair_t_ref, first, group, passed)
         project_rows(
             first, group, passed.astype(F32), load_mask(mask_ref, first, group),
-            wt_scr, left_scr, right_scr, gate_ref,
+            wt_ref, left_scr, right_scr, gate_ref,
         )
     send_channels(blocks, left_scr, right_scr, send_ref)
 
 
-def last_kernel(tri_ref, gate_ref, pair_t_ref, wo_ref, out_ref, tri_scr):
+def last_kernel(tri_ref, gate_ref, pair_t_ref, wo_t_ref, out_hbm, tri_scr, out_scr, sems):
     width, rows, cols = tri_ref.shape
-    group = rows
-    wo_t = wo_ref[1].T
+    group = rows // sems.shape[0]
     tri_scr[...] = jnp.swapaxes(tri_ref[...], 0, 1)
+    stores = []
     for first in range(0, rows, group):
-        passed = finish_rows(first, group, tri_scr, wo_t, gate_ref, pair_t_ref)
+        passed = finish_rows(first, group, tri_scr, wo_t_ref[...], gate_ref, pair_t_ref)
         for g in range(group):
-            out_ref[first + g] = passed[:, g * cols : (g + 1) * cols].T
+            out_scr[first + g] = passed[:, g * cols : (g + 1) * cols].T
+        at = pl.ds(first, group)
+        stores.append(pltpu.make_async_copy(out_scr.at[at], out_hbm.at[at], sems.at[first // group]))
+        stores[-1].start()
+    for store in stores:
+        store.wait()
 
 
 def outgoing_kernel(places, *refs):
@@ -222,13 +228,13 @@
                 out_ref[p, c] = tri[r * rows : (r + 1) * rows, x * cols : (x + 1) * cols]
 
 
-def call(kernel, name, out_shape, scratch, in_specs, flops, *args, vmem=VMEM_LIMIT):
+def call(kernel, name, out_shape, scratch, in_specs, flops, *args, vmem=VMEM_LIMIT, out_specs=None):
     return pl.pallas_call(
         kernel,
         name=name,
         out_shape=out_shape,
         in_specs=in_specs,
-        out_specs=jax.tree.map(lambda _: pl.BlockSpec(memory_space=pltpu.VMEM), out_shape),
+        out_specs=out_specs or jax.tree.map(lambda _: VM, out_shape),
         scratch_shapes=scratch,
         compiler_params=pltpu.CompilerParams(vmem_limit_bytes=vmem),
         cost_estimate=pl.CostEstimate(flops=flops, bytes_accessed=2 << 20, transcendentals=0),
@@ -287,8 +293,8 @@
 
     right, *left, mask = call(
         functools.partial(first_kernel, half_blocks), "project",
-        (shape_of(group, half_per, rows, cols),) + (part_shape,) * 4
-        + (shape_of(rows, cols, dtype=F32),),
+        (shape_of(group, half_per, rows, cols),) + (pltpu.VMEM(part_shape.shape, BF16),) * 4
+        + (pltpu.VMEM((rows, cols), F32),),
         [
             scr, scr, wt_scr, pltpu.SMEM(chain_lengths.shape, jnp.int32), pltpu.VMEM(pair_act.shape, BF16),
             pltpu.VMEM(in_weights.shape[1:], BF16), pltpu.VMEM((half_group, half_per, rows, cols), BF16),
@@ -300,8 +306,10 @@
     left = to_partners(left, ("row_b", "row_d"))
     left = call(regroup_kernel, "regroup", (part_shape,) * 4, [], [VM] * 4, 3000 * flops_out, *left, vmem=4 * 1024 * 1024)
     left = to_partners(left, ("row_c", "col"))
-    gate, pair_t = call(
-        gate_kernel, "gate", (block_shape, block_shape), [], [VM, VM], flops_out, pair_act, in_weights
+    wo_shape = shape_of(width, width)
+    gate, pair_t, wt, wo_t, last_wo_t = call(
+        gate_kernel, "gate", (block_shape, block_shape, shape_of(5 * width, width), wo_shape, wo_shape), [],
+        [VM] * 3, flops_out, pair_act, in_weights, out_weights,
     )
     tri = call(
         functools.partial(outgoing_kernel, right_places), "outgoing", shape_of(half_group, half_per, rows, cols),
@@ -311,8 +319,7 @@
     send, gate, pair_t = call(
         functools.partial(middle_kernel, blocks), "finish_project",
         (shape_of(group, 2, per, rows, cols), block_shape, block_shape),
-        [scr, scr, wt_scr, scr], [VM] * 6, flops_in + flops_out,
-        tri, gate, pair_t, mask, out_weights, in_weights,
+        [scr, scr, scr], [VM] * 6, flops_in + flops_out, tri, gate, pair_t, mask, wo_t, wt,
     )
     recv = exchange(send, SIDES_ORDER)
     tri = call(
@@ -321,8 +328,9 @@
     )
     tri = exchange(tri, TRIANGLE_ORDER).reshape(width, rows, cols)
     return call(
-        last_kernel, "finish", shape_of(*pair_act.shape), [scr],
-        [VM, VM, VM, VM], flops_out, tri, gate, pair_t, out_weights,
+        last_kernel, "finish", shape_of(*pair_act.shape),
+        [scr, pltpu.VMEM(pair_act.shape, BF16), pltpu.SemaphoreType.DMA((4,))],
+        [VM, VM, VM, VM], flops_out, tri, gate, pair_t, last_wo_t, out_specs=HBM,
     )
 
 

time: 104 us -> 104 us (level)
  no operation moved by 1% of the time
where the time goes in v8:
time: 104 us
  blocking collectives  58.9 us (57%)
  waiting for transfers between devices  21.9 us (21%)
  starting transfers between devices  12.9 us (12%)
  Pallas kernels  10 us (10%)
    all_to_all x3, blocking collectives, exchange(): return lax.all_to_all(array, order, split_axis=0, concat_axis=0, tiled=True)  58.9 us
    ppermute x6, waiting for transfers between devices, to_partners(): lax.ppermute(p, name, pair)  13.6 us
    pallas_call x7, Pallas kernels, call(): pl.pallas_call(kernel, name=name, out_shape=out_shape, in_specs=in_specs,...  10 us
    all_to_all x1, waiting for transfers between devices, exchange(): return lax.all_to_all(array, order, split_axis=0, concat_axis=0, tiled=True)  8.33 us
    ppermute x6, starting transfers between devices, to_partners(): lax.ppermute(p, name, pair)  6.78 us
    all_to_all x1, starting transfers between devices, exchange(): return lax.all_to_all(array, order, split_axis=0, concat_axis=0, tiled=True)  6.13 us
  transfers between devices with their start and end apart: 7, of which 4 were waited for; matrix products, arithmetic and copies ran while one was open for 0% of the time, Pallas kernels for 1%

profile of v8, /device:TPU:0, one launch (start us, length us, event | category | flops | bytes accessed | tf_op | source)
XLA Modules:
  0.0 103.9 jit_solution(17741252834925676260)
XLA Ops:
  0.0 3.7 %project.1 = (bf16[32,8,16,128]{3,2,1,0:T(8,128)(2,1)}, bf16[4,8,16,128]{3,2,1,0:T(8,128)(2,1)S(1)}, bf16[4,8,16,128]{3,2,1,0:T(8,128)(2,1)S(1)}, bf16[4,8,16,12...) custom-call(s32[8]{0:T(128)} %lengths_hbm.1, bf16[16,128,128]{2,1,0:T(8,128)(2,1)} %pair_ref.1, ...), custom_call_target="tpu_custom_call" | custom-call | flops 335544320 | bytes 2097152 | tf_op jit(solution)/shard_map/project/pallas_call | solution.py:232
  3.8 0.5 collective-permute-start
  4.3 2.6 %collective-permute-start.1 = (bf16[4,8,16,128]{3,2,1,0:T(8,128)(2,1)S(1)}, bf16[4,8,16,128]{3,2,1,0:T(8,128)(2,1)S(1)}, u32[]{:S(2)}, u32[]{:S(2)}) collective-permute-start(bf16[4,8,16,128]{3,2,1,0:T(8,128)(2,1)S(1)} %get-tuple-element.25), channel_id=1, source_target_pairs={{0,8},{8,0},{1,9},{9,1},{2,10},{10,2},{3,11},{11,3},{4,12},{12,4},... | collective-permute-start | bytes 393224 | tf_op jit(solution)/shard_map/ppermute | solution.py:264
  6.9 0.1 collective-permute-start.2
  7.0 6.1 %all-to-all-start = ((bf16[32,8,16,128]{3,2,1,0:T(8,128)(2,1)}), bf16[32,8,16,128]{3,2,1,0:T(8,128)(2,1)}, u32[]{:S(2)}, u32[]{:S(2)}) async-start(bf16[32,8,16,128]{3,2,1,0:T(8,128)(2,1)} %get-tuple-element.31), calls=%async_computation | async-start | bytes 2097152 | tf_op jit(solution)/shard_map/all_to_all | solution.py:292
  13.1 0.0 collective-permute-done.refs_1_
  13.1 0.0 collective-permute-done.1.refs_2_
  13.1 0.4 collective-permute-done.2.refs_3_
  13.6 1.6 %collective-permute-start.3 = (bf16[4,8,16,128]{3,2,1,0:T(8,128)(2,1)S(1)}, bf16[4,8,16,128]{3,2,1,0:T(8,128)(2,1)S(1)}, u32[]{:S(2)}, u32[]{:S(2)}) collective-permute-start(bf16[4,8,16,128]{3,2,1,0:T(8,128)(2,1)S(1)} %get-tuple-element.28), channel_id=1, source_target_pairs={{0,1},{1,0},{2,3},{3,2},{4,5},{5,4},{6,7},{7,6},{8,9},{9,8},{10,11... | collective-permute-start | bytes 393224 | tf_op jit(solution)/shard_map/ppermute | solution.py:264
  15.1 1.5 %collective-permute-start.4 = (bf16[4,8,16,128]{3,2,1,0:T(8,128)(2,1)S(1)}, bf16[4,8,16,128]{3,2,1,0:T(8,128)(2,1)S(1)}, u32[]{:S(2)}, u32[]{:S(2)}) collective-permute-start(bf16[4,8,16,128]{3,2,1,0:T(8,128)(2,1)S(1)} %get-tuple-element.29), channel_id=1, source_target_pairs={{0,4},{4,0},{1,5},{5,1},{2,6},{6,2},{3,7},{7,3},{8,12},{12,8},{9,1... | collective-permute-start | bytes 393224 | tf_op jit(solution)/shard_map/ppermute | solution.py:264
  16.7 0.5 collective-permute-start.5
  17.2 0.0 copy-done
  17.2 0.7 gate.1
  17.8 9.9 %collective-permute-done.3.refs_1_ = bf16[4,8,16,128]{3,2,1,0:T(8,128)(2,1)S(1)} collective-permute-done((bf16[4,8,16,128]{3,2,1,0:T(8,128)(2,1)S(1)}, bf16[4,8,16,128]{3,2,1,0:T(8,128)(2,1)S(1)}, u32[]{:S(2)}, u32[]{:S(2)}) %collective-permute-start.3) | collective-permute-done | bytes 131104 | tf_op jit(solution)/shard_map/ppermute | solution.py:264
  27.7 0.0 collective-permute-done.4.refs_2_
  27.7 3.3 %collective-permute-done.5.refs_3_ = bf16[4,8,16,128]{3,2,1,0:T(8,128)(2,1)S(1)} collective-permute-done((bf16[4,8,16,128]{3,2,1,0:T(8,128)(2,1)S(1)}, bf16[4,8,16,128]{3,2,1,0:T(8,128)(2,1)S(1)}, u32[]{:S(2)}, u32[]{:S(2)}) %collective-permute-start.5) | collective-permute-done | bytes 131104 | tf_op jit(solution)/shard_map/ppermute | solution.py:264
  31.0 8.3 %all-to-all-done.refs_4_ = bf16[32,8,16,128]{3,2,1,0:T(8,128)(2,1)} async-done(((bf16[32,8,16,128]{3,2,1,0:T(8,128)(2,1)}), bf16[32,8,16,128]{3,2,1,0:T(8,128)(2,1)}, u32[]{:S(2)}, u32[]{:S(2)}) %all-to-all-start) | async-done | bytes 1048608 | tf_op jit(solution)/shard_map/all_to_all | solution.py:292
  39.3 1.7 %outgoing.1 = bf16[16,8,16,128]{3,2,1,0:T(8,128)(2,1)S(1)} custom-call(bf16[4,8,16,128]{3,2,1,0:T(8,128)(2,1)S(1)} %get-tuple-element.27.refs_0_, bf16[4,8,16,128]{3,2,1,0:T(8,128)(2,1)S(1)} %collective-permute-done.3.refs_1_, bf16[4,8,16,128]{3,2,1,0:T(8,128)(2,1)S(1)} %collective-permute-done.4.refs_2_, ...), custom_call_target="tpu_custom_call" | custom-call | flops 4294967296 | bytes 2097152 | tf_op jit(solution)/shard_map/outgoing/pallas_call | solution.py:232
  41.0 11.9 %all_to_all.20 = bf16[16,8,16,128]{3,2,1,0:T(8,128)(2,1)S(1)} all-to-all(bf16[16,8,16,128]{3,2,1,0:T(8,128)(2,1)S(1)} %outgoing.1), channel_id=1, replica_groups=mesh['parts'=1,'row_a'=2,'row_b'=2,'row_c'=2,'row_d'=2,'col'=2] {'row_c'..., dimensions={0} | all-to-all | bytes 1048576 | tf_op jit(solution)/shard_map/all_to_all | solution.py:292
  52.9 2.2 %finish_project.1 = (bf16[32,2,4,16,128]{4,3,2,1,0:T(8,128)(2,1)S(1)}, bf16[16,128,128]{2,1,0:T(8,128)(2,1)S(1)}, bf16[16,128,128]{2,1,0:T(8,128)(2,1)S(1)}) custom-call(bf16[128,16,128]{2,1,0:T(8,128)(2,1)S(1)} %bitcast.2, bf16[16,128,128]{2,1,0:T(8,128)(2,1)S(1)} %get-tuple-element.32.refs_5_.gate_in_ref, ...), custom_call_target="tpu_custom_call" | custom-call | flops 402653184 | bytes 2097152 | tf_op jit(solution)/shard_map/finish_project/pallas_call | solution.py:232
  55.1 29.9 %all_to_all.21.recv_ref = bf16[32,2,4,16,128]{4,3,2,1,0:T(8,128)(2,1)S(1)} all-to-all(bf16[32,2,4,16,128]{4,3,2,1,0:T(8,128)(2,1)S(1)} %get-tuple-element.37), channel_id=1, replica_groups=mesh['parts'=1,'row_a'=2,'row_b'=2,'row_c'=2,'row_d'=2,'col'=2] {'col','..., dimensions={0} | all-to-all | bytes 2097152 | tf_op jit(solution)/shard_map/all_to_all | solution.py:292
  85.0 0.3 incoming.1
  85.4 17.1 %all_to_all.22 = bf16[32,4,16,128]{3,2,1,0:T(8,128)(2,1)S(1)} all-to-all(bf16[32,4,16,128]{3,2,1,0:T(8,128)(2,1)S(1)} %incoming.1), channel_id=1, replica_groups=mesh['parts'=1,'row_a'=2,'row_b'=2,'row_c'=2,'row_d'=2,'col'=2] {'col','..., dimensions={0} | all-to-all | bytes 1048576 | tf_op jit(solution)/shard_map/all_to_all | solution.py:292
  102.5 1.4 %finish.1 = bf16[16,128,128]{2,1,0:T(8,128)(2,1)} custom-call(bf16[128,16,128]{2,1,0:T(8,128)(2,1)S(1)} %bitcast.3, bf16[16,128,128]{2,1,0:T(8,128)(2,1)S(1)} %get-tuple-element.38.gate_ref, bf16[16,128,128]{2,1,0:T(8,128)(2,1)S(1)} %get-tuple-element.39.pair_t_ref, bf16[128,128]{1,0:T(8,128)(2,1)S(1)} %get-tuple-element.40.wo_t_ref), custom_call_target="tpu_custom_call" | custom-call | flops 67108864 | bytes 2097152 | tf_op jit(solution)/shard_map/finish/pallas_call | solution.py:232
  (6 shorter events, 0.0 us)
Async XLA Ops:
  3.8 9.4 %collective-permute-start = (bf16[4,8,16,128]{3,2,1,0:T(8,128)(2,1)S(1)}, bf16[4,8,16,128]{3,2,1,0:T(8,128)(2,1)S(1)}, u32[]{:S(2)}, u32[]{:S(2)}) collective-permute-start(bf16[4,8,16,128]{3,2,1,0:T(8,128)(2,1)S(1)} %get-tuple-element.24), channel_id=1, source_target_pairs={{0,2},{2,0},{1,3},{3,1},{4,6},{6,4},{5,7},{7,5},{8,10},{10,8},{9,1... | collective-permute-start | bytes 393224 | tf_op jit(solution)/shard_map/ppermute | solution.py:264
  4.3 8.9 %collective-permute-start.1 = (bf16[4,8,16,128]{3,2,1,0:T(8,128)(2,1)S(1)}, bf16[4,8,16,128]{3,2,1,0:T(8,128)(2,1)S(1)}, u32[]{:S(2)}, u32[]{:S(2)}) collective-permute-start(bf16[4,8,16,128]{3,2,1,0:T(8,128)(2,1)S(1)} %get-tuple-element.25), channel_id=1, source_target_pairs={{0,8},{8,0},{1,9},{9,1},{2,10},{10,2},{3,11},{11,3},{4,12},{12,4},... | collective-permute-start | bytes 393224 | tf_op jit(solution)/shard_map/ppermute | solution.py:264
  6.9 6.6 %collective-permute-start.2 = (bf16[4,8,16,128]{3,2,1,0:T(8,128)(2,1)S(1)}, bf16[4,8,16,128]{3,2,1,0:T(8,128)(2,1)S(1)}, u32[]{:S(2)}, u32[]{:S(2)}) collective-permute-start(bf16[4,8,16,128]{3,2,1,0:T(8,128)(2,1)S(1)} %get-tuple-element.26), channel_id=1, source_target_pairs={{0,10},{2,8},{8,2},{10,0},{1,11},{3,9},{9,3},{11,1},{4,14},{6,12},... | collective-permute-start | bytes 393224 | tf_op jit(solution)/shard_map/ppermute | solution.py:264
  7.0 32.3 %all-to-all-start = ((bf16[32,8,16,128]{3,2,1,0:T(8,128)(2,1)}), bf16[32,8,16,128]{3,2,1,0:T(8,128)(2,1)}, u32[]{:S(2)}, u32[]{:S(2)}) async-start(bf16[32,8,16,128]{3,2,1,0:T(8,128)(2,1)} %get-tuple-element.31), calls=%async_computation | async-start | bytes 2097152 | tf_op jit(solution)/shard_map/all_to_all | solution.py:292
  13.6 3.6 %copy-start = (bf16[16,128,128]{2,1,0:T(8,128)(2,1)S(1)}, bf16[16,128,128]{2,1,0:T(8,128)(2,1)}, u32[]{:S(2)}) copy-start(bf16[16,128,128]{2,1,0:T(8,128)(2,1)} %pair_ref.1) | copy-start | bytes 1572868
  13.6 3.6 %copy-start.1 = (bf16[2,128,640]{2,1,0:T(8,128)(2,1)S(1)}, bf16[2,128,640]{2,1,0:T(8,128)(2,1)}, u32[]{:S(2)}) copy-start(bf16[2,128,640]{2,1,0:T(8,128)(2,1)} %weights_ref.1) | copy-start | bytes 983044
  13.6 3.6 %copy-start.2 = (bf16[2,128,128]{2,1,0:T(8,128)(2,1)S(1)}, bf16[2,128,128]{2,1,0:T(8,128)(2,1)}, u32[]{:S(2)}) copy-start(bf16[2,128,128]{2,1,0:T(8,128)(2,1)} %wo_ref.1) | copy-start | bytes 196612
  13.6 14.1 %collective-permute-start.3 = (bf16[4,8,16,128]{3,2,1,0:T(8,128)(2,1)S(1)}, bf16[4,8,16,128]{3,2,1,0:T(8,128)(2,1)S(1)}, u32[]{:S(2)}, u32[]{:S(2)}) collective-permute-start(bf16[4,8,16,128]{3,2,1,0:T(8,128)(2,1)S(1)} %get-tuple-element.28), channel_id=1, source_target_pairs={{0,1},{1,0},{2,3},{3,2},{4,5},{5,4},{6,7},{7,6},{8,9},{9,8},{10,11... | collective-permute-start | bytes 393224 | tf_op jit(solution)/shard_map/ppermute | solution.py:264
  15.1 12.6 %collective-permute-start.4 = (bf16[4,8,16,128]{3,2,1,0:T(8,128)(2,1)S(1)}, bf16[4,8,16,128]{3,2,1,0:T(8,128)(2,1)S(1)}, u32[]{:S(2)}, u32[]{:S(2)}) collective-permute-start(bf16[4,8,16,128]{3,2,1,0:T(8,128)(2,1)S(1)} %get-tuple-element.29), channel_id=1, source_target_pairs={{0,4},{4,0},{1,5},{5,1},{2,6},{6,2},{3,7},{7,3},{8,12},{12,8},{9,1... | collective-permute-start | bytes 393224 | tf_op jit(solution)/shard_map/ppermute | solution.py:264
  16.7 14.3 %collective-permute-start.5 = (bf16[4,8,16,128]{3,2,1,0:T(8,128)(2,1)S(1)}, bf16[4,8,16,128]{3,2,1,0:T(8,128)(2,1)S(1)}, u32[]{:S(2)}, u32[]{:S(2)}) collective-permute-start(bf16[4,8,16,128]{3,2,1,0:T(8,128)(2,1)S(1)} %get-tuple-element.30), channel_id=1, source_target_pairs={{0,5},{1,4},{4,1},{5,0},{2,7},{3,6},{6,3},{7,2},{8,13},{9,12},{12,... | collective-permute-start | bytes 393224 | tf_op jit(solution)/shard_map/ppermute | solution.py:264
